TPU v7x, 128 devices: a whole 4x4x4 slice. The times are simulated.
128 devices in a mesh: fsdp: 16 (over y, x), row: 8 (over z, core).
Axes of the slice: x: 4, y: 4, z: 4, core: 2. Of those that a mesh axis runs over, the one named last changes fastest.
Arguments:
- grad_gate: bfloat16 [25600, 5120], P('row', 'fsdp'), may hold values from -400 to 400
- grad_up: bfloat16 [25600, 5120], P('row', 'fsdp'), may hold values from -400 to 400
- grad_down: bfloat16 [5120, 25600], P('row', 'fsdp'), may hold values from -400 to 400
- proj_gate: bfloat16 [256, 5120], P(None, 'fsdp'), may hold values from -0.375 to 0.375
- proj_up: bfloat16 [256, 5120], P(None, 'fsdp'), may hold values from -0.375 to 0.375
- proj_down: bfloat16 [256, 5120], P(None, 'row'), may hold values from -0.375 to 0.375
- first_gate: float32 [256, 25600], P('fsdp', 'row'), may hold values from -800 to 800
- second_gate: float32 [256, 25600], P('fsdp', 'row'), may hold values from 400 to 40000
- first_up: float32 [256, 25600], P('fsdp', 'row'), may hold values from -800 to 800
- second_up: float32 [256, 25600], P('fsdp', 'row'), may hold values from 400 to 40000
- first_down: float32 [256, 25600], P('row', 'fsdp'), may hold values from -800 to 800
- second_down: float32 [256, 25600], P('row', 'fsdp'), may hold values from 400 to 40000
Outputs:
- update_gate: bfloat16 [25600, 5120], P('row', 'fsdp')
- update_up: bfloat16 [25600, 5120], P('row', 'fsdp')
- update_down: bfloat16 [5120, 25600], P('row', 'fsdp')
- first_gate_new: float32 [256, 25600], P('fsdp', 'row')
- second_gate_new: float32 [256, 25600], P('fsdp', 'row')
- first_up_new: float32 [256, 25600], P('fsdp', 'row')
- second_up_new: float32 [256, 25600], P('fsdp', 'row')
- first_down_new: float32 [256, 25600], P('row', 'fsdp')
- second_down_new: float32 [256, 25600], P('row', 'fsdp')
All inputs are finite; a program needn't handle non-finite values.
Results may differ from a plain program's by a relative error of at most 0.015.
Values may be sent and summed in bfloat16 or wider, within the bound.
No kernel may reach another device: no remote copies, remote signals or barrier semaphores. Data moves between devices by JAX's collectives and lax.ppermute only.
A program may use at most 64 MiB of HBM per device.

v0:
```python
import jax
import jax.numpy as jnp
from jax import lax
from jax.sharding import PartitionSpec as P

STEP = 100


beta_first = 0.9
beta_second = 0.999
adam_epsilon = 1e-08
norm_epsilon = 1e-06
update_scale = 4.0


def adam_step(own_rows, first_moment, second_moment):
    first_new = beta_first * first_moment + (1.0 - beta_first) * own_rows
    second_new = beta_second * second_moment + (1.0 - beta_second) * own_rows * own_rows
    corrected = (
        first_new
        / (1.0 - beta_first**STEP)
        / (jnp.sqrt(second_new / (1.0 - beta_second**STEP)) + adam_epsilon)
    )
    return (first_new, second_new, corrected)


def against_features(projection, gradient):
    return lax.dot_general(
        projection, gradient, (((1,), (1,)), ((), ())), preferred_element_type=jnp.float32
    )


def per_device(
    grad_gate,
    grad_up,
    grad_down,
    proj_gate,
    proj_up,
    proj_down,
    first_gate,
    second_gate,
    first_up,
    second_up,
    first_down,
    second_down,
):
    fsdp_count = lax.axis_size("fsdp")
    row_devices = lax.axis_size("row")
    local_ff = grad_gate.shape[0]
    rank_rows = proj_gate.shape[0]
    first_pair = jnp.concatenate((first_gate, first_up), 1)
    second_pair = jnp.concatenate((second_gate, second_up), 1)
    gate_share = rank_rows // fsdp_count
    partial_pair = jnp.concatenate(
        (against_features(proj_gate, grad_gate), against_features(proj_up, grad_up)), 1
    )
    summed_pair = lax.psum(partial_pair.astype(jnp.bfloat16), "fsdp").astype(jnp.float32)
    own_rows = lax.dynamic_slice_in_dim(
        summed_pair, lax.axis_index("fsdp") * gate_share, gate_share, 0
    )
    pair_first, pair_second, corrected = adam_step(own_rows, first_pair, second_pair)
    projected_sq = jnp.sum(summed_pair * summed_pair, 0)
    corrected_sq = lax.psum(jnp.sum(corrected * corrected, 0), "fsdp")
    pair_scale = jnp.sqrt(corrected_sq) / (jnp.sqrt(projected_sq) + norm_epsilon)
    update_gate = (
        update_scale * grad_gate.astype(jnp.float32) * pair_scale[:local_ff, None]
    ).astype(jnp.bfloat16)
    update_up = (update_scale * grad_up.astype(jnp.float32) * pair_scale[local_ff:, None]).astype(
        jnp.bfloat16
    )
    down_share = rank_rows // row_devices
    partial_down = jnp.dot(proj_down, grad_down, preferred_element_type=jnp.float32)
    summed_down = lax.psum(partial_down.astype(jnp.bfloat16), "row").astype(jnp.float32)
    own_down = lax.dynamic_slice_in_dim(
        summed_down, lax.axis_index("row") * down_share, down_share, 0
    )
    first_down_new, second_down_new, corrected_down = adam_step(own_down, first_down, second_down)
    down_projected_sq = jnp.sum(summed_down * summed_down, 0)
    down_corrected_sq = lax.psum(jnp.sum(corrected_down * corrected_down, 0), "row")
    down_scale = jnp.sqrt(down_corrected_sq) / (jnp.sqrt(down_projected_sq) + norm_epsilon)
    update_down = (update_scale * grad_down.astype(jnp.float32) * down_scale[None, :]).astype(
        jnp.bfloat16
    )
    first_gate_new = pair_first[:, :local_ff]
    first_up_new = pair_first[:, local_ff:]
    second_gate_new = pair_second[:, :local_ff]
    second_up_new = pair_second[:, local_ff:]
    return (
        update_gate,
        update_up,
        update_down,
        first_gate_new,
        second_gate_new,
        first_up_new,
        second_up_new,
        first_down_new,
        second_down_new,
    )


def solution(mesh):
    return jax.shard_map(
        per_device,
        mesh=mesh,
        in_specs=(
            P("row", "fsdp"),
            P("row", "fsdp"),
            P("row", "fsdp"),
            P(None, "fsdp"),
            P(None, "fsdp"),
            P(None, "row"),
            P("fsdp", "row"),
            P("fsdp", "row"),
            P("fsdp", "row"),
            P("fsdp", "row"),
            P("row", "fsdp"),
            P("row", "fsdp"),
        ),
        out_specs=(
            P("row", "fsdp"),
            P("row", "fsdp"),
            P("row", "fsdp"),
            P("fsdp", "row"),
            P("fsdp", "row"),
            P("fsdp", "row"),
            P("fsdp", "row"),
            P("row", "fsdp"),
            P("row", "fsdp"),
        ),
        check_vma=False,
    )
```

profile of v0, /device:TPU:0, one launch (start us, length us, event | category | flops | bytes accessed | tf_op | source)
XLA Modules:
  0.0 263.7 jit_solution(2406805858180698573)
XLA Ops:
  7.2 0.0 copy-start
  7.2 0.0 copy-start.1
  7.2 0.0 copy-start.10
  7.2 0.0 all-reduce.5.cloned.1.call-start
  7.3 0.9 copy-done
  8.2 3.3 %convolution_convert_fusion.2 = bf16[256,1600]{1,0:T(8,128)(2,1)} fusion(bf16[256,640]{1,0:T(8,128)(2,1)S(1)} %copy-done, bf16[640,1600]{0,1:T(8,128)(2,1)} %param.14), kind=kOutput, calls=%fused_computation.7 | convolution fusion | flops 524697600 | bytes 3194880 | tf_op jit(solution)/shard_map/dot_general | solution.py:72
  11.5 0.0 all-reduce.5.cloned.1.call-update
  11.5 0.0 copy-start.11
  11.5 0.0 all-reduce.3.cloned.1.call-start
  11.6 0.0 copy-done.1
  11.6 0.0 copy-done.10
  11.6 0.0 copy-start.2
  11.6 1.1 convolution_convert_fusion
  12.7 0.0 copy-done.11
  12.7 0.5 copy-done.2
  13.2 1.1 convolution_convert_fusion.1
  14.3 1.9 pad_maximum_fusion
  16.2 0.0 all-reduce.3.cloned.1.call-update
  16.2 0.0 copy-start.5
  16.2 60.0 %all-reduce.5.cloned.1.call-done = bf16[256,1600]{1,0:T(8,128)(2,1)} async-done(((bf16[256,1600]{1,0:T(8,128)(2,1)}), bf16[256,1600]{1,0:T(8,128)(2,1)}) %all-reduce.5.cloned.1.call-update) | async-done | bytes 819216 | tf_op jit(solution)/shard_map/psum | solution.py:73
  76.2 0.0 copy-start.4
  76.2 1.3 convert_element_type.35
  77.6 0.0 copy-done.5
  77.6 1.8 multiply_reduce_fusion.3
  79.4 13.6 %psum.31 = f32[1600]{0:T(1024)S(1)} all-reduce(f32[1600]{0:T(1024)S(1)} %get-tuple-element.18), channel_id=1, replica_groups=mesh['fsdp'=16,'row'=8] {'row'}, use_global_device_ids=true, to_apply=%region_6.0 | all-reduce | flops 1600 | bytes 12800 | tf_op jit(solution)/shard_map/psum | solution.py:79
  93.0 0.0 copy-done.4
  93.0 0.2 multiply_reduce_fusion.1
  93.2 3.3 %multiply_convert_fusion = bf16[640,1600]{0,1:T(8,128)(2,1)} fusion(bf16[640,1600]{0,1:T(8,128)(2,1)} %param.14, f32[1600]{0:T(1024)S(1)} %divide_multiply_fusion), kind=kLoop, calls=%fused_computation.3 | loop fusion | flops 3072000 | bytes 4102400 | tf_op jit(solution)/shard_map/convert_element_type | solution.py:81
  96.6 0.0 copy-start.6
  96.6 78.8 %all-reduce.3.cloned.1.call-done = bf16[256,6400]{1,0:T(8,128)(2,1)} async-done(((bf16[256,6400]{1,0:T(8,128)(2,1)}), bf16[256,6400]{1,0:T(8,128)(2,1)}) %all-reduce.3.cloned.1.call-update) | async-done | bytes 3276816 | tf_op jit(solution)/shard_map/psum | solution.py:57
  175.4 0.0 copy-start.7
  175.4 0.0 copy-start.8
  175.4 0.0 copy-start.9
  175.4 2.4 convert_element_type.29
  177.8 0.0 copy-done.6
  177.9 0.0 copy-done.7
  177.9 0.0 copy-done.8
  177.9 0.0 copy-done.9
  177.9 0.4 multiply_reduce_fusion.2
  178.2 72.2 %psum.29 = f32[6400]{0:T(1024)S(1)} all-reduce(f32[6400]{0:T(1024)S(1)} %get-tuple-element.21), channel_id=1, replica_groups=mesh['fsdp'=16,'row'=8] {'fsdp'}, use_global_device_ids=true, to_apply=%region_2.0 | all-reduce | flops 6400 | bytes 51200 | tf_op jit(solution)/shard_map/psum | solution.py:63
  250.4 0.0 copy-start.3
  250.4 2.8 %multiply_reduce_fusion = f32[6400]{0:T(1024)S(1)} fusion(bf16[256,6400]{1,0:T(8,128)(2,1)} %all-reduce.3.cloned.1.call-done), kind=kLoop, calls=%fused_computation | loop fusion | flops 4908800 | bytes 3302400 | tf_op jit(solution)/shard_map/reduce_sum | solution.py:62
  253.2 0.0 copy-done.3
  253.2 2.7 %multiply_convert_fusion.1 = (bf16[3200,320]{0,1:T(8,128)(2,1)}, bf16[3200,320]{0,1:T(8,128)(2,1)}) fusion(bf16[3200,320]{0,1:T(8,128)(2,1)S(1)} %copy-done.1, f32[3200]{0:T(1024)S(1)} %get-tuple-element.28, f32[3200]{0:T(1024)S(1)} %get-tuple-element.29, bf16[3200,320]{0,1:T(8,128)(2,1)S(1)} %copy-done.3), kind=kLoop, calls=%fused_computation.4 | loop fusion | flops 6144000 | bytes 8217600 | tf_op jit(solution)/shard_map/convert_element_type | solution.py:68
  255.9 0.9 fusion.6
  (3 shorter events, 0.0 us)
Async XLA Ops:
  7.2 1.0 copy-start
  7.2 4.4 %copy-start.1 = (bf16[3200,320]{0,1:T(8,128)(2,1)S(1)}, bf16[3200,320]{0,1:T(8,128)(2,1)}, u32[]{:S(2)}) copy-start(bf16[3200,320]{0,1:T(8,128)(2,1)} %param.13) | copy-start | bytes 6144004
  7.2 4.4 %copy-start.10 = (bf16[256,320]{0,1:T(8,128)(2,1)S(1)}, bf16[256,320]{0,1:T(8,128)(2,1)}, u32[]{:S(2)}) copy-start(bf16[256,320]{0,1:T(8,128)(2,1)} %param.16) | copy-start | bytes 491524
  7.2 69.0 %all-reduce.5.cloned.1.call-start = ((), (), s32[]{:S(2)}) async-start(), calls=%async_computation.1 | async-start | bytes 1703936 | tf_op jit(solution)/shard_map/psum | solution.py:73
  11.5 1.2 copy-start.11
  11.5 163.9 %all-reduce.3.cloned.1.call-start = ((), (), s32[]{:S(2)}) async-start(), calls=%async_computation | async-start | bytes 6553600 | tf_op jit(solution)/shard_map/psum | solution.py:57
  11.6 1.6 copy-start.2
  16.2 61.4 %copy-start.5 = (f32[32,1600]{1,0:T(8,128)S(1)}, f32[32,1600]{1,0:T(8,128)}, u32[]{:S(2)}) copy-start(f32[32,1600]{1,0:T(8,128)} %param.22) | copy-start | bytes 614404
  76.2 16.8 %copy-start.4 = (bf16[256,1600]{1,0:T(8,128)(2,1)S(1)}, bf16[256,1600]{1,0:T(8,128)(2,1)}, u32[]{:S(2)}) copy-start(bf16[256,1600]{1,0:T(8,128)(2,1)} %all-reduce.5.cloned.1.call-done) | copy-start | bytes 2457604
  96.6 81.3 %copy-start.6 = (f32[16,3200]{1,0:T(8,128)S(1)}, f32[16,3200]{1,0:T(8,128)}, u32[]{:S(2)}) copy-start(f32[16,3200]{1,0:T(8,128)} %param.20) | copy-start | bytes 614404
  175.4 2.4 copy-start.7
  175.4 2.4 copy-start.8
  175.4 2.4 copy-start.9
  250.4 2.8 %copy-start.3 = (bf16[3200,320]{0,1:T(8,128)(2,1)S(1)}, bf16[3200,320]{0,1:T(8,128)(2,1)}, u32[]{:S(2)}) copy-start(bf16[3200,320]{0,1:T(8,128)(2,1)} %param.12) | copy-start | bytes 6144004
Sparse Core Ops, SparseCore 0:
  11.6 64.5 all-reduce.4
  80.0 95.3 all-reduce.2
where the time goes:
time: 264 us
  waiting for transfers between devices  139 us (53%)
  blocking collectives  85.7 us (32%)
  other arithmetic  16.9 us (6%)
  between operations  14.3 us (5%)
  matrix products  5.46 us (2%)
    psum x1, waiting for transfers between devices, per_device(): lax.psum(partial_pair.astype(jnp.bfloat16), 'fsdp').astype(jnp.float32)  78.8 us
    psum x1, blocking collectives, per_device(): corrected_sq = lax.psum(jnp.sum(corrected * corrected, 0), 'fsdp')  72.2 us
    psum x1, waiting for transfers between devices, per_device(): lax.psum(partial_down.astype(jnp.bfloat16), 'row').astype(jnp.float32)  60 us
    psum x1, blocking collectives, per_device(): lax.psum(jnp.sum(corrected_down * corrected_down, 0), 'row')  13.6 us
  transfers between devices with their start and end apart: 2, of which 2 were waited for; matrix products, arithmetic and copies ran while one was open for 4% of the time, Pallas kernels for 0%

commit v1 on v0

v1 whole, which is shorter than its diff:
```python
import jax
import jax.numpy as jnp
from jax import lax
from jax.sharding import Mesh
from jax.sharding import PartitionSpec as P

STEP = 100

beta_first = 0.9
beta_second = 0.999
adam_epsilon = 1e-08
norm_epsilon = 1e-06
update_scale = 4.0

AXES = ("y", "x", "z", "core")
SIZES = (4, 4, 4, 2)
ALONG = ("y", "x")
ACROSS = ("z", "core")


def adam_step(own_rows, first_moment, second_moment):
    first_new = beta_first * first_moment + (1.0 - beta_first) * own_rows
    second_new = beta_second * second_moment + (1.0 - beta_second) * own_rows * own_rows
    corrected = (
        first_new
        / (1.0 - beta_first**STEP)
        / (jnp.sqrt(second_new / (1.0 - beta_second**STEP)) + adam_epsilon)
    )
    return (first_new, second_new, corrected)


def against_features(projection, gradient):
    return lax.dot_general(
        projection, gradient, (((1,), (1,)), ((), ())), preferred_element_type=jnp.float32
    )


def device_number(y, x, z, core):
    return ((y * 4 + x) * 4 + z) * 2 + core


def ring_pairs(shift, stage):
    pairs = []
    for y in range(4):
        for x in range(4):
            for z in range(4):
                for core in range(2):
                    source = device_number(y, x, z, core)
                    if (core == 0) == (stage == 0):
                        target = device_number(y, (x + shift) % 4, z, core)
                    else:
                        target = device_number((y + shift) % 4, x, z, core)
                    pairs.append((source, target))
    return pairs


def ring_send(value, shift, stage):
    return lax.ppermute(value, AXES, ring_pairs(shift, stage))


def z_send(value, shift):
    return lax.ppermute(value, "z", [(i, (i + shift) % 4) for i in range(4)])


def core_send(value):
    return lax.ppermute(value, "core", [(0, 1), (1, 0)])


def add(*terms):
    total = terms[0].astype(jnp.float32)
    for term in terms[1:]:
        total = total + term.astype(jnp.float32)
    return total


def pick_rows(projection, rows):
    chosen = (rows[:, None] == jnp.arange(projection.shape[0])[None, :]).astype(projection.dtype)
    return jnp.dot(chosen, projection, preferred_element_type=jnp.float32).astype(projection.dtype)


def ring_reduce(forth, back, near, far, keep):
    half = keep.shape[0] // 2
    from_below = ring_send(forth, 1, 0)
    from_above = ring_send(back, 3, 0)
    onward = add(near, from_below[half:]).astype(jnp.bfloat16)
    backward = add(far, from_above[:half]).astype(jnp.bfloat16)
    last_below = ring_send(onward, 1, 0)
    last_above = ring_send(backward, 3, 0)
    last_below, last_above = lax.optimization_barrier((last_below, last_above))
    low = add(keep[:half], from_above[half:], last_below)
    high = add(keep[half:], from_below[:half], last_above)
    return low, high


def per_device(
    grad_gate,
    grad_up,
    grad_down,
    proj_gate,
    proj_up,
    proj_down,
    first_gate,
    second_gate,
    first_up,
    second_up,
    first_down,
    second_down,
):
    y, x, z, core = (lax.axis_index(name) for name in AXES)
    local_ff = grad_gate.shape[0]
    step = jnp.arange(256)
    outer, inner = step // 64, step // 16 % 4
    on_x, on_y = jnp.where(core == 0, outer, inner), jnp.where(core == 0, inner, outer)
    rows = ((y + on_y) % 4 * 4 + (x + on_x) % 4) * 16 + step % 16
    down_rows = ((z + step // 32 % 4) % 4 * 2 + (core + step // 128) % 2) * 32 + step % 32

    reduced = []
    for gradient, projection in ((grad_gate, proj_gate), (grad_up, proj_up)):
        ordered = pick_rows(projection, rows)
        sent = against_features(ordered[96:224], gradient).astype(jnp.bfloat16)
        rest = against_features(
            jnp.concatenate((ordered[:96], ordered[224:])), gradient
        ).astype(jnp.bfloat16)
        reduced.append(ring_reduce(sent[:64], sent[64:], rest[64:96], rest[96:], rest[:64]))
    low = jnp.concatenate((reduced[0][0], reduced[1][0]), 1)
    high = jnp.concatenate((reduced[0][1], reduced[1][1]), 1)
    opposite = ring_send(high[:16].astype(jnp.bfloat16), 2, 1)
    above = ring_send(high[16:].astype(jnp.bfloat16), 3, 1)
    below = ring_send(low[16:].astype(jnp.bfloat16), 1, 1)
    own_rows = add(low[:16], opposite, above, below)
    first_pair = jnp.concatenate((first_gate, first_up), 1)
    second_pair = jnp.concatenate((second_gate, second_up), 1)
    pair_first, pair_second, corrected = adam_step(own_rows, first_pair, second_pair)
    sums = jnp.stack((jnp.sum(corrected * corrected, 0), jnp.sum(own_rows * own_rows, 0)))
    for stage in (1, 0):
        sums = sums + (ring_send(sums, 2, stage) + ring_send(sums, 1, stage) + ring_send(sums, 3, stage))
    pair_scale = update_scale * jnp.sqrt(sums[0]) / (jnp.sqrt(sums[1]) + norm_epsilon)
    update_gate = (grad_gate.astype(jnp.float32) * pair_scale[:local_ff, None]).astype(jnp.bfloat16)
    update_up = (grad_up.astype(jnp.float32) * pair_scale[local_ff:, None]).astype(jnp.bfloat16)

    partial_down = jnp.dot(
        pick_rows(proj_down, down_rows), grad_down, preferred_element_type=jnp.float32
    ).astype(jnp.bfloat16)
    down_sum = add(partial_down[:128], core_send(partial_down[128:])).astype(jnp.bfloat16)
    own_down = add(
        down_sum[:32],
        z_send(down_sum[64:96], 2),
        z_send(down_sum[32:64], 1),
        z_send(down_sum[96:], 3),
    )
    first_down_new, second_down_new, corrected_down = adam_step(own_down, first_down, second_down)
    down_sums = jnp.stack((jnp.sum(corrected_down * corrected_down, 0), jnp.sum(own_down * own_down, 0)))
    down_sums = down_sums + core_send(down_sums)
    down_sums = down_sums + (z_send(down_sums, 2) + z_send(down_sums, 1) + z_send(down_sums, 3))
    down_scale = update_scale * jnp.sqrt(down_sums[0]) / (jnp.sqrt(down_sums[1]) + norm_epsilon)
    update_down = (grad_down.astype(jnp.float32) * down_scale[None, :]).astype(jnp.bfloat16)
    return (
        update_gate,
        update_up,
        update_down,
        pair_first[:, :local_ff],
        pair_second[:, :local_ff],
        pair_first[:, local_ff:],
        pair_second[:, local_ff:],
        first_down_new,
        second_down_new,
    )


def solution(mesh):
    fine = Mesh(mesh.devices.reshape(SIZES), AXES)
    gradient, state = P(ACROSS, ALONG), P(ALONG, ACROSS)
    return jax.shard_map(
        per_device,
        mesh=fine,
        in_specs=(
            gradient,
            gradient,
            gradient,
            P(None, ALONG),
            P(None, ALONG),
            P(None, ACROSS),
            state,
            state,
            state,
            state,
            gradient,
            gradient,
        ),
        out_specs=(
            gradient,
            gradient,
            gradient,
            state,
            state,
            state,
            state,
            gradient,
            gradient,
        ),
        check_vma=False,
    )
```

time: 264 us -> 78.4 us (0.30)
  waiting for transfers between devices: 139 us -> 10.7 us
  blocking collectives: 85.7 us -> 0 us
  starting transfers between devices: 0.08 us -> 39.5 us
  between operations: 14.3 us -> 1.07 us
  matrix products: 5.46 us -> 8.89 us
  other arithmetic: 16.9 us -> 13.5 us
    psum x2 -> x0, waiting for transfers between devices: 139 us -> none  [the longest x1 78.8 us: per_device(): lax.psum(partial_pair.astype(jnp.bfloat16), 'fsdp').astype(jnp.float32)]
    psum x2 -> x0, blocking collectives: 85.7 us -> none  [the longest x1 72.2 us: per_device(): corrected_sq = lax.psum(jnp.sum(corrected * corrected, 0), 'fsdp')]
    ppermute x0 -> x25, starting transfers between devices: none -> 39.5 us  [the longest x17 27.5 us: ring_send(): return lax.ppermute(value, AXES, ring_pairs(shift, stage))]
    ppermute x0 -> x25, waiting for transfers between devices: none -> 10.7 us  [the longest x17 10.6 us: ring_send(): return lax.ppermute(value, AXES, ring_pairs(shift, stage))]
    add x0 -> x10, other arithmetic: none -> 4.92 us  [the longest x4 4.15 us: add(): total = total + term.astype(jnp.float32)]
    convert_element_type x4 -> x5, other arithmetic: 9.81 us -> 6.8 us  [the longest x1 2.74 us: per_device(): (grad_up.astype(jnp.float32) * pair_scale[local_ff:, None]).astype(jnp.bf...]
    reduce_sum x3 -> x2, other arithmetic: 3.3 us -> 0.5 us  [the longest x1 0.43 us: per_device(): jnp.sum(corrected * corrected, 0)]
  transfers between devices with their start and end apart: 2 -> 25, of which waited for: 2 -> 5; matrix products, arithmetic and copies ran while one was open for 4% -> 22% of each run, Pallas kernels for 0% -> 0%
where the time goes in v1:
time: 78.4 us; the launch traced here: 77.4 us
  starting transfers between devices  39.5 us (50%)
  other arithmetic  13.5 us (17%)
  waiting for transfers between devices  10.7 us (14%)
  matrix products  8.89 us (11%)
  local copies, waits for them, and re-layouts  3.79 us (5%)
  between operations  1.07 us (1%)
    ppermute x17, starting transfers between devices, ring_send(): return lax.ppermute(value, AXES, ring_pairs(shift, stage))  27.5 us
    ppermute x6, starting transfers between devices, z_send(): return lax.ppermute(value, 'z', [(i, (i + shift) % 4) for i in range(4)])  11.8 us
    ppermute x17, waiting for transfers between devices, ring_send(): return lax.ppermute(value, AXES, ring_pairs(shift, stage))  10.6 us
    dot_general x4, matrix products, against_features(): lax.dot_general(projection, gradient, (((1,), (1,)), ((), ())), preferred...  4.54 us
    add x4, other arithmetic, add(): total = total + term.astype(jnp.float32)  4.15 us
    dot_general x1, matrix products, per_device(): jnp.dot(pick_rows(proj_down, down_rows), grad_down, preferred_element_typ...  2.79 us
    convert_element_type x1, other arithmetic, per_device(): (grad_up.astype(jnp.float32) * pair_scale[local_ff:, None]).astype(jnp.bf...  2.74 us
    convert_element_type x2, other arithmetic, ring_reduce(): backward = add(far, from_above[:half]).astype(jnp.bfloat16)  2.25 us
  transfers between devices with their start and end apart: 25, of which 5 were waited for; matrix products, arithmetic and copies ran while one was open for 22% of the time, Pallas kernels for 0%

profile of v1, /device:TPU:0, one launch (start us, length us, event | category | flops | bytes accessed | tf_op | source)
XLA Modules:
  0.0 77.4 jit_solution(293793652682446097)
XLA Ops:
  0.7 1.3 %convolution_convert_fusion.6 = bf16[256,320]{0,1:T(8,128)(2,1)S(1)} fusion(bf16[256,320]{0,1:T(8,128)(2,1)} %param.16, s32[256]{0:T(256)S(1)} %fusion.31), kind=kOutput, calls=%fused_computation.9 | convolution fusion | flops 42090496 | bytes 328704 | tf_op jit(solution)/shard_map/dot_general | solution.py:78
  2.0 2.4 %convolution_convert_fusion = bf16[128,3200]{1,0:T(8,128)(2,1)S(1)} fusion(bf16[3200,320]{0,1:T(8,128)(2,1)} %param.13, bf16[256,320]{0,1:T(8,128)(2,1)S(1)} %convolution_convert_fusion.6), kind=kOutput, calls=%fused_computation | convolution fusion | flops 262553600 | bytes 2949120 | tf_op jit(solution)/shard_map/dot_general | solution.py:33
  4.4 0.9 %fusion.54 = (bf16[64,3200]{1,0:T(8,128)(2,1)}, bf16[64,3200]{1,0:T(8,128)(2,1)}) fusion(bf16[128,3200]{1,0:T(8,128)(2,1)S(1)} %convolution_convert_fusion), kind=kLoop, calls=%fused_computation.129 | loop fusion | bytes 1638400 | tf_op jit(solution)/shard_map/slice | solution.py:124
  5.4 2.8 %collective-permute-start.4 = (bf16[64,3200]{1,0:T(8,128)(2,1)}, bf16[64,3200]{1,0:T(8,128)(2,1)}, u32[]{:S(2)}, u32[]{:S(2)}) collective-permute-start(bf16[64,3200]{1,0:T(8,128)(2,1)} %get-tuple-element.41), channel_id=1, source_target_pairs={{0,24},{1,97},{2,26},{3,99},{4,28},{5,101},{6,30},{7,103},{8,0},{9... | collective-permute-start | bytes 1228808 | tf_op jit(solution)/shard_map/ppermute | solution.py:58
  8.2 0.3 convolution_convert_fusion.7
  8.5 0.7 convolution_convert_fusion.2
  9.2 1.0 %fusion.53 = (bf16[64,3200]{1,0:T(8,128)(2,1)}, bf16[64,3200]{1,0:T(8,128)(2,1)}) fusion(bf16[128,3200]{1,0:T(8,128)(2,1)S(1)} %convolution_convert_fusion.2), kind=kLoop, calls=%fused_computation.128 | loop fusion | bytes 1638400 | tf_op jit(solution)/shard_map/slice | solution.py:124
  10.2 3.2 %collective-permute-start = (bf16[64,3200]{1,0:T(8,128)(2,1)}, bf16[64,3200]{1,0:T(8,128)(2,1)}, u32[]{:S(2)}, u32[]{:S(2)}) collective-permute-start(bf16[64,3200]{1,0:T(8,128)(2,1)} %get-tuple-element.37), channel_id=1, source_target_pairs={{0,24},{1,97},{2,26},{3,99},{4,28},{5,101},{6,30},{7,103},{8,0},{9... | collective-permute-start | bytes 1228808 | tf_op jit(solution)/shard_map/ppermute | solution.py:58
  13.4 0.6 fusion.30
  14.0 2.8 %convolution_convert_fusion.4 = bf16[256,1600]{1,0:T(8,128)(2,1)S(1)} fusion(bf16[640,1600]{0,1:T(8,128)(2,1)} %param.14, bf16[256,640]{1,0:T(8,128)(2,1)S(1)} %copy-done, s32[256]{0:T(256)} %fusion.30), kind=kOutput, calls=%fused_computation.7 | convolution fusion | flops 608813056 | bytes 3195904 | tf_op jit(solution)/shard_map/dot_general | solution.py:141
  17.0 0.1 slice.213
  17.1 0.7 convolution_convert_fusion.1
  17.8 0.1 slice.202
  17.9 0.5 copy-done.3
  18.4 0.7 convolution_convert_fusion.3
  19.2 0.1 add_convert_fusion
  19.3 3.9 %collective-permute-start.18 = (bf16[32,1600]{1,0:T(8,128)(2,1)S(1)}, bf16[32,1600]{1,0:T(8,128)(2,1)S(1)}, u32[]{:S(2)}, u32[]{:S(2)}) collective-permute-start(bf16[32,1600]{1,0:T(8,128)(2,1)S(1)} %get-tuple-element.44), channel_id=1, source_target_pairs={{0,4},{2,6},{4,0},{6,2},{1,5},{3,7},{5,1},{7,3},{8,12},{10,14},{12... | collective-permute-start | bytes 307208 | tf_op jit(solution)/shard_map/ppermute | solution.py:62
  23.3 0.7 collective-permute-start.20
  24.0 1.3 %collective-permute-start.19 = (bf16[32,1600]{1,0:T(8,128)(2,1)S(1)}, bf16[32,1600]{1,0:T(8,128)(2,1)S(1)}, u32[]{:S(2)}, u32[]{:S(2)}) collective-permute-start(bf16[32,1600]{1,0:T(8,128)(2,1)S(1)} %get-tuple-element.46), channel_id=1, source_target_pairs={{0,2},{2,4},{4,6},{6,0},{1,3},{3,5},{5,7},{7,1},{8,10},{10,12},{12... | collective-permute-start | bytes 307208 | tf_op jit(solution)/shard_map/ppermute | solution.py:62
  25.3 1.1 %add_convert_fusion.1 = (bf16[32,3200]{1,0:T(8,128)(2,1)S(1)}, bf16[32,3200]{1,0:T(8,128)(2,1)S(1)}) fusion(bf16[64,3200]{1,0:T(8,128)(2,1)} %collective-permute-done.4, bf16[128,3200]{1,0:T(8,128)(2,1)S(1)} %convolution_convert_fusion.1, bf16[64,3200]{1,0:T(8,128)(2,1)} %collective-permute-done.5), kind=kLoop, calls=%fused_computation.31 | loop fusion | flops 819200 | bytes 1228800 | tf_op jit(solution)/shard_map/convert_element_type | solution.py:86
  26.4 3.3 %collective-permute-start.7 = (bf16[32,3200]{1,0:T(8,128)(2,1)S(1)}, bf16[32,3200]{1,0:T(8,128)(2,1)S(1)}, u32[]{:S(2)}, u32[]{:S(2)}) collective-permute-start(bf16[32,3200]{1,0:T(8,128)(2,1)S(1)} %get-tuple-element.39), channel_id=1, source_target_pairs={{0,24},{1,97},{2,26},{3,99},{4,28},{5,101},{6,30},{7,103},{8,0},{9... | collective-permute-start | bytes 614408 | tf_op jit(solution)/shard_map/ppermute | solution.py:58
  29.7 0.5 collective-permute-start.6
  30.2 1.0 %multiply_reduce_fusion.3 = (f32[1600]{0:T(1024)S(1)}, f32[32,1600]{1,0:T(8,128)}, f32[32,1600]{1,0:T(8,128)}, f32[1600]{0:T(1024)S(1)}) fusion(bf16[32,1600]{1,0:T(8,128)(2,1)S(1)} %collective-permute-done.20, bf16[32,1600]{1,0:T(8,128)(2,1)S(1)} %collective-permute-done.19, bf16[32,1600]{1,0:T(8,128)(2,1)S(1)} %collective-permute-done.18, ...), kind=kLoop, calls=%fused_computation.41 | loop fusion | flops 1123200 | bytes 1241600 | tf_op jit(solution)/shard_map/reduce_sum | solution.py:152
  31.3 1.1 %add_convert_fusion.3 = (bf16[32,3200]{1,0:T(8,128)(2,1)S(1)}, bf16[32,3200]{1,0:T(8,128)(2,1)S(1)}) fusion(bf16[64,3200]{1,0:T(8,128)(2,1)} %collective-permute-done, bf16[128,3200]{1,0:T(8,128)(2,1)S(1)} %convolution_convert_fusion.3, bf16[64,3200]{1,0:T(8,128)(2,1)} %collective-permute-done.1), kind=kLoop, calls=%fused_computation.34 | loop fusion | flops 819200 | bytes 1228800 | tf_op jit(solution)/shard_map/convert_element_type | solution.py:86
  32.5 3.0 %collective-permute-start.3 = (bf16[32,3200]{1,0:T(8,128)(2,1)S(1)}, bf16[32,3200]{1,0:T(8,128)(2,1)S(1)}, u32[]{:S(2)}, u32[]{:S(2)}) collective-permute-start(bf16[32,3200]{1,0:T(8,128)(2,1)S(1)} %get-tuple-element.35), channel_id=1, source_target_pairs={{0,24},{1,97},{2,26},{3,99},{4,28},{5,101},{6,30},{7,103},{8,0},{9... | collective-permute-start | bytes 614408 | tf_op jit(solution)/shard_map/ppermute | solution.py:58
  35.5 4.2 %collective-permute-start.24 = (f32[2,1600]{1,0:T(2,128)S(1)}, f32[2,1600]{1,0:T(2,128)S(1)}, u32[]{:S(2)}, u32[]{:S(2)}) collective-permute-start(f32[2,1600]{1,0:T(2,128)S(1)} %fusion.48), channel_id=1, source_target_pairs={{0,6},{2,0},{4,2},{6,4},{1,7},{3,1},{5,3},{7,5},{8,14},{10,8},{12,... | collective-permute-start | bytes 38408 | tf_op jit(solution)/shard_map/ppermute | solution.py:62
  39.7 1.7 %collective-permute-start.22 = (f32[2,1600]{1,0:T(2,128)S(1)}, f32[2,1600]{1,0:T(2,128)S(1)}, u32[]{:S(2)}, u32[]{:S(2)}) collective-permute-start(f32[2,1600]{1,0:T(2,128)S(1)} %fusion.48), channel_id=1, source_target_pairs={{0,4},{2,6},{4,0},{6,2},{1,5},{3,7},{5,1},{7,3},{8,12},{10,14},{12... | collective-permute-start | bytes 38408 | tf_op jit(solution)/shard_map/ppermute | solution.py:62
  41.4 1.1 %collective-permute-done.2 = bf16[32,3200]{1,0:T(8,128)(2,1)S(1)} collective-permute-done((bf16[32,3200]{1,0:T(8,128)(2,1)S(1)}, bf16[32,3200]{1,0:T(8,128)(2,1)S(1)}, u32[]{:S(2)}, u32[]{:S(2)}) %collective-permute-start.2) | collective-permute-done | bytes 204832 | tf_op jit(solution)/shard_map/ppermute | solution.py:58
  42.4 1.0 %convert_add_fusion = bf16[32,3200]{1,0:T(8,128)(2,1)S(1)} fusion(bf16[32,3200]{1,0:T(8,128)(2,1)S(1)} %collective-permute-done.7, bf16[64,3200]{1,0:T(8,128)(2,1)} %collective-permute-done.5, bf16[128,3200]{1,0:T(8,128)(2,1)S(1)} %convolution_convert_fusion.1), kind=kLoop, calls=%fused_computation.28 | loop fusion | flops 614400 | bytes 819200 | tf_op jit(solution)/shard_map/add | solution.py:72
  43.4 1.0 %convert_add_fusion.1 = bf16[32,3200]{1,0:T(8,128)(2,1)S(1)} fusion(bf16[32,3200]{1,0:T(8,128)(2,1)S(1)} %collective-permute-done.3, bf16[64,3200]{1,0:T(8,128)(2,1)} %collective-permute-done.1, bf16[128,3200]{1,0:T(8,128)(2,1)S(1)} %convolution_convert_fusion.3), kind=kLoop, calls=%fused_computation.29 | loop fusion | flops 614400 | bytes 819200 | tf_op jit(solution)/shard_map/add | solution.py:72
  44.6 1.1 %convert_add_fusion.2 = f32[32,3200]{1,0:T(8,128)S(1)} fusion(bf16[32,3200]{1,0:T(8,128)(2,1)S(1)} %collective-permute-done.6, bf16[64,3200]{1,0:T(8,128)(2,1)} %collective-permute-done.4, bf16[128,3200]{1,0:T(8,128)(2,1)S(1)} %convolution_convert_fusion.1), kind=kLoop, calls=%fused_computation.30 | loop fusion | flops 512000 | bytes 1024000 | tf_op jit(solution)/shard_map/add | solution.py:72
  45.7 1.0 %convert_add_fusion.3 = f32[32,3200]{1,0:T(8,128)S(1)} fusion(bf16[32,3200]{1,0:T(8,128)(2,1)S(1)} %collective-permute-done.2, bf16[64,3200]{1,0:T(8,128)(2,1)} %collective-permute-done, bf16[128,3200]{1,0:T(8,128)(2,1)S(1)} %convolution_convert_fusion.3), kind=kLoop, calls=%fused_computation.33 | loop fusion | flops 512000 | bytes 1024000 | tf_op jit(solution)/shard_map/add | solution.py:72
  46.7 1.6 %collective-permute-start.10 = (bf16[16,6400]{1,0:T(8,128)(2,1)S(1)}, bf16[16,6400]{1,0:T(8,128)(2,1)S(1)}, u32[]{:S(2)}, u32[]{:S(2)}) collective-permute-start(bf16[16,6400]{1,0:T(8,128)(2,1)S(1)} %fusion.5), channel_id=1, source_target_pairs={{0,32},{1,9},{2,34},{3,11},{4,36},{5,13},{6,38},{7,15},{8,40},{9,1... | collective-permute-start | bytes 614408 | tf_op jit(solution)/shard_map/ppermute | solution.py:58
  48.4 2.9 %collective-permute-start.8 = (bf16[16,6400]{1,0:T(8,128)(2,1)S(1)}, bf16[16,6400]{1,0:T(8,128)(2,1)S(1)}, u32[]{:S(2)}, u32[]{:S(2)}) collective-permute-start(bf16[16,6400]{1,0:T(8,128)(2,1)S(1)} %get-tuple-element.51), channel_id=1, source_target_pairs={{0,64},{1,17},{2,66},{3,19},{4,68},{5,21},{6,70},{7,23},{8,72},{9,... | collective-permute-start | bytes 614408 | tf_op jit(solution)/shard_map/ppermute | solution.py:58
  51.3 1.3 %collective-permute-start.9 = (bf16[16,6400]{1,0:T(8,128)(2,1)S(1)}, bf16[16,6400]{1,0:T(8,128)(2,1)S(1)}, u32[]{:S(2)}, u32[]{:S(2)}) collective-permute-start(bf16[16,6400]{1,0:T(8,128)(2,1)S(1)} %get-tuple-element.52), channel_id=1, source_target_pairs={{0,96},{1,25},{2,98},{3,27},{4,100},{5,29},{6,102},{7,31},{8,104},... | collective-permute-start | bytes 614408 | tf_op jit(solution)/shard_map/ppermute | solution.py:58
  52.8 1.0 %collective-permute-done.10 = bf16[16,6400]{1,0:T(8,128)(2,1)S(1)} collective-permute-done((bf16[16,6400]{1,0:T(8,128)(2,1)S(1)}, bf16[16,6400]{1,0:T(8,128)(2,1)S(1)}, u32[]{:S(2)}, u32[]{:S(2)}) %collective-permute-start.10) | collective-permute-done | bytes 204832 | tf_op jit(solution)/shard_map/ppermute | solution.py:58
  53.8 3.4 %collective-permute-done.8 = bf16[16,6400]{1,0:T(8,128)(2,1)S(1)} collective-permute-done((bf16[16,6400]{1,0:T(8,128)(2,1)S(1)}, bf16[16,6400]{1,0:T(8,128)(2,1)S(1)}, u32[]{:S(2)}, u32[]{:S(2)}) %collective-permute-start.8) | collective-permute-done | bytes 204832 | tf_op jit(solution)/shard_map/ppermute | solution.py:58
  57.3 0.4 multiply_reduce_fusion.1
  57.9 2.5 %collective-permute-start.13 = (f32[2,6400]{1,0:T(2,128)S(1)}, f32[2,6400]{1,0:T(2,128)S(1)}, u32[]{:S(2)}, u32[]{:S(2)}) collective-permute-start(f32[2,6400]{1,0:T(2,128)S(1)} %pad_maximum_fusion.1), channel_id=1, source_target_pairs={{0,96},{1,25},{2,98},{3,27},{4,100},{5,29},{6,102},{7,31},{8,104},... | collective-permute-start | bytes 153608 | tf_op jit(solution)/shard_map/ppermute | solution.py:58
  60.3 2.5 %collective-permute-start.11 = (f32[2,6400]{1,0:T(2,128)S(1)}, f32[2,6400]{1,0:T(2,128)S(1)}, u32[]{:S(2)}, u32[]{:S(2)}) collective-permute-start(f32[2,6400]{1,0:T(2,128)S(1)} %pad_maximum_fusion.1), channel_id=1, source_target_pairs={{0,64},{1,17},{2,66},{3,19},{4,68},{5,21},{6,70},{7,23},{8,72},{9,... | collective-permute-start | bytes 153608 | tf_op jit(solution)/shard_map/ppermute | solution.py:58
  62.8 1.7 %multiply_convert_fusion = bf16[640,1600]{0,1:T(8,128)(2,1)} fusion(bf16[640,1600]{0,1:T(8,128)(2,1)S(1)} %copy-done.4, f32[1600]{0:T(1024)S(1)} %fusion.26), kind=kLoop, calls=%fused_computation.4 | loop fusion | flops 3072000 | bytes 4102400 | tf_op jit(solution)/shard_map/convert_element_type | solution.py:156
  64.5 1.7 %collective-permute-done.12 = f32[2,6400]{1,0:T(2,128)S(1)} collective-permute-done((f32[2,6400]{1,0:T(2,128)S(1)}, f32[2,6400]{1,0:T(2,128)S(1)}, u32[]{:S(2)}, u32[]{:S(2)}) %collective-permute-start.12) | collective-permute-done | bytes 51232 | tf_op jit(solution)/shard_map/ppermute | solution.py:58
  66.3 2.2 %collective-permute-start.16 = (f32[2,6400]{1,0:T(2,128)S(1)}, f32[2,6400]{1,0:T(2,128)S(1)}, u32[]{:S(2)}, u32[]{:S(2)}) collective-permute-start(f32[2,6400]{1,0:T(2,128)S(1)} %add_add_fusion.1), channel_id=1, source_target_pairs={{0,24},{1,97},{2,26},{3,99},{4,28},{5,101},{6,30},{7,103},{8,0},{9... | collective-permute-start | bytes 153608 | tf_op jit(solution)/shard_map/ppermute | solution.py:58
  68.5 1.5 %collective-permute-start.14 = (f32[2,6400]{1,0:T(2,128)S(1)}, f32[2,6400]{1,0:T(2,128)S(1)}, u32[]{:S(2)}, u32[]{:S(2)}) collective-permute-start(f32[2,6400]{1,0:T(2,128)S(1)} %add_add_fusion.1), channel_id=1, source_target_pairs={{0,16},{1,65},{2,18},{3,67},{4,20},{5,69},{6,22},{7,71},{8,24},{9,... | collective-permute-start | bytes 153608 | tf_op jit(solution)/shard_map/ppermute | solution.py:58
  70.1 0.9 %fusion.56 = (f32[16,3200]{1,0:T(8,128)}, f32[16,3200]{1,0:T(8,128)}, f32[16,3200]{1,0:T(8,128)}, f32[16,3200]{1,0:T(8,128)}) fusion(f32[16,6400]{1,0:T(8,128)S(1)} %get-tuple-element.33, f32[16,6400]{1,0:T(8,128)S(1)} %get-tuple-element.32), kind=kLoop, calls=%fused_computation.131 | loop fusion | bytes 1638400 | tf_op jit(solution)/shard_map/slice | solution.py:164
  71.0 3.4 %collective-permute-done.15 = f32[2,6400]{1,0:T(2,128)S(1)} collective-permute-done((f32[2,6400]{1,0:T(2,128)S(1)}, f32[2,6400]{1,0:T(2,128)S(1)}, u32[]{:S(2)}, u32[]{:S(2)}) %collective-permute-start.15) | collective-permute-done | bytes 51232 | tf_op jit(solution)/shard_map/ppermute | solution.py:58
  74.5 0.1 fusion.21
  74.7 2.7 %multiply_convert_fusion.1 = (bf16[3200,320]{0,1:T(8,128)(2,1)}, bf16[3200,320]{0,1:T(8,128)(2,1)}) fusion(bf16[3200,320]{0,1:T(8,128)(2,1)S(1)} %copy-done.1, f32[3200]{0:T(1024)S(1)} %get-tuple-element.26, f32[3200]{0:T(1024)S(1)} %get-tuple-element.27, bf16[3200,320]{0,1:T(8,128)(2,1)S(1)} %copy-done.3), kind=kLoop, calls=%fused_computation.5 | loop fusion | flops 6144000 | bytes 8217600 | tf_op jit(solution)/shard_map/convert_element_type | solution.py:139
  (72 shorter events, 1.0 us)
Async XLA Ops:
  0.6 13.4 %copy-start = (bf16[256,640]{1,0:T(8,128)(2,1)S(1)}, bf16[256,640]{1,0:T(8,128)(2,1)}, u32[]{:S(2)}) copy-start(bf16[256,640]{1,0:T(8,128)(2,1)} %param.17) | copy-start | bytes 983044
  1.9 6.3 %copy-start.11 = (bf16[256,320]{0,1:T(8,128)(2,1)S(1)}, bf16[256,320]{0,1:T(8,128)(2,1)}, u32[]{:S(2)}) copy-start(bf16[256,320]{0,1:T(8,128)(2,1)} %param.15) | copy-start | bytes 491524
  2.0 6.6 %copy-start.2 = (bf16[3200,320]{0,1:T(8,128)(2,1)S(1)}, bf16[3200,320]{0,1:T(8,128)(2,1)}, u32[]{:S(2)}) copy-start(bf16[3200,320]{0,1:T(8,128)(2,1)} %param.12) | copy-start | bytes 6144004
  5.4 17.9 %collective-permute-start.4 = (bf16[64,3200]{1,0:T(8,128)(2,1)}, bf16[64,3200]{1,0:T(8,128)(2,1)}, u32[]{:S(2)}, u32[]{:S(2)}) collective-permute-start(bf16[64,3200]{1,0:T(8,128)(2,1)} %get-tuple-element.41), channel_id=1, source_target_pairs={{0,24},{1,97},{2,26},{3,99},{4,28},{5,101},{6,30},{7,103},{8,0},{9... | collective-permute-start | bytes 1228808 | tf_op jit(solution)/shard_map/ppermute | solution.py:58
  8.2 15.8 %collective-permute-start.5 = (bf16[64,3200]{1,0:T(8,128)(2,1)}, bf16[64,3200]{1,0:T(8,128)(2,1)}, u32[]{:S(2)}, u32[]{:S(2)}) collective-permute-start(bf16[64,3200]{1,0:T(8,128)(2,1)} %get-tuple-element.42), channel_id=1, source_target_pairs={{0,8},{1,33},{2,10},{3,35},{4,12},{5,37},{6,14},{7,39},{8,16},{9,4... | collective-permute-start | bytes 1228808 | tf_op jit(solution)/shard_map/ppermute | solution.py:58
  10.2 21.1 %collective-permute-start = (bf16[64,3200]{1,0:T(8,128)(2,1)}, bf16[64,3200]{1,0:T(8,128)(2,1)}, u32[]{:S(2)}, u32[]{:S(2)}) collective-permute-start(bf16[64,3200]{1,0:T(8,128)(2,1)} %get-tuple-element.37), channel_id=1, source_target_pairs={{0,24},{1,97},{2,26},{3,99},{4,28},{5,101},{6,30},{7,103},{8,0},{9... | collective-permute-start | bytes 1228808 | tf_op jit(solution)/shard_map/ppermute | solution.py:58
  13.4 17.9 %collective-permute-start.1 = (bf16[64,3200]{1,0:T(8,128)(2,1)}, bf16[64,3200]{1,0:T(8,128)(2,1)}, u32[]{:S(2)}, u32[]{:S(2)}) collective-permute-start(bf16[64,3200]{1,0:T(8,128)(2,1)} %get-tuple-element.38), channel_id=1, source_target_pairs={{0,8},{1,33},{2,10},{3,35},{4,12},{5,37},{6,14},{7,39},{8,16},{9,4... | collective-permute-start | bytes 1228808 | tf_op jit(solution)/shard_map/ppermute | solution.py:58
  14.0 3.1 %copy-start.1 = (bf16[3200,320]{0,1:T(8,128)(2,1)S(1)}, bf16[3200,320]{0,1:T(8,128)(2,1)}, u32[]{:S(2)}) copy-start(bf16[3200,320]{0,1:T(8,128)(2,1)} %param.13) | copy-start | bytes 6144004
  16.9 1.6 %copy-start.3 = (bf16[3200,320]{0,1:T(8,128)(2,1)S(1)}, bf16[3200,320]{0,1:T(8,128)(2,1)}, u32[]{:S(2)}) copy-start(bf16[3200,320]{0,1:T(8,128)(2,1)} %param.12) | copy-start | bytes 6144004
  16.9 2.3 %collective-permute-start.17 = (bf16[128,1600]{1,0:T(8,128)(2,1)S(1)}, bf16[128,1600]{1,0:T(8,128)(2,1)S(1)}, u32[]{:S(2)}, u32[]{:S(2)}) collective-permute-start(bf16[128,1600]{1,0:T(8,128)(2,1)S(1)} %slice.236), channel_id=1, source_target_pairs={{0,1},{1,0},{2,3},{3,2},{4,5},{5,4},{6,7},{7,6},{8,9},{9,8},{10,11... | collective-permute-start | bytes 1228808 | tf_op jit(solution)/shard_map/ppermute | solution.py:66
  19.1 11.1 %copy-start.5 = (f32[32,1600]{1,0:T(8,128)S(1)}, f32[32,1600]{1,0:T(8,128)}, u32[]{:S(2)}) copy-start(f32[32,1600]{1,0:T(8,128)} %param.22) | copy-start | bytes 614404
  19.2 11.1 %copy-start.6 = (f32[32,1600]{1,0:T(8,128)S(1)}, f32[32,1600]{1,0:T(8,128)}, u32[]{:S(2)}) copy-start(f32[32,1600]{1,0:T(8,128)} %param.23) | copy-start | bytes 614404
  19.3 7.1 %collective-permute-start.18 = (bf16[32,1600]{1,0:T(8,128)(2,1)S(1)}, bf16[32,1600]{1,0:T(8,128)(2,1)S(1)}, u32[]{:S(2)}, u32[]{:S(2)}) collective-permute-start(bf16[32,1600]{1,0:T(8,128)(2,1)S(1)} %get-tuple-element.44), channel_id=1, source_target_pairs={{0,4},{2,6},{4,0},{6,2},{1,5},{3,7},{5,1},{7,3},{8,12},{10,14},{12... | collective-permute-start | bytes 307208 | tf_op jit(solution)/shard_map/ppermute | solution.py:62
  23.3 6.5 %collective-permute-start.20 = (bf16[32,1600]{1,0:T(8,128)(2,1)S(1)}, bf16[32,1600]{1,0:T(8,128)(2,1)S(1)}, u32[]{:S(2)}, u32[]{:S(2)}) collective-permute-start(bf16[32,1600]{1,0:T(8,128)(2,1)S(1)} %get-tuple-element.45), channel_id=1, source_target_pairs={{0,6},{2,0},{4,2},{6,4},{1,7},{3,1},{5,3},{7,5},{8,14},{10,8},{12,... | collective-permute-start | bytes 307208 | tf_op jit(solution)/shard_map/ppermute | solution.py:62
  24.0 6.2 %collective-permute-start.19 = (bf16[32,1600]{1,0:T(8,128)(2,1)S(1)}, bf16[32,1600]{1,0:T(8,128)(2,1)S(1)}, u32[]{:S(2)}, u32[]{:S(2)}) collective-permute-start(bf16[32,1600]{1,0:T(8,128)(2,1)S(1)} %get-tuple-element.46), channel_id=1, source_target_pairs={{0,2},{2,4},{4,6},{6,0},{1,3},{3,5},{5,7},{7,1},{8,10},{10,12},{12... | collective-permute-start | bytes 307208 | tf_op jit(solution)/shard_map/ppermute | solution.py:62
  26.4 13.2 %collective-permute-start.7 = (bf16[32,3200]{1,0:T(8,128)(2,1)S(1)}, bf16[32,3200]{1,0:T(8,128)(2,1)S(1)}, u32[]{:S(2)}, u32[]{:S(2)}) collective-permute-start(bf16[32,3200]{1,0:T(8,128)(2,1)S(1)} %get-tuple-element.39), channel_id=1, source_target_pairs={{0,24},{1,97},{2,26},{3,99},{4,28},{5,101},{6,30},{7,103},{8,0},{9... | collective-permute-start | bytes 614408 | tf_op jit(solution)/shard_map/ppermute | solution.py:58
  29.7 10.0 %collective-permute-start.6 = (bf16[32,3200]{1,0:T(8,128)(2,1)S(1)}, bf16[32,3200]{1,0:T(8,128)(2,1)S(1)}, u32[]{:S(2)}, u32[]{:S(2)}) collective-permute-start(bf16[32,3200]{1,0:T(8,128)(2,1)S(1)} %get-tuple-element.40), channel_id=1, source_target_pairs={{0,8},{1,33},{2,10},{3,35},{4,12},{5,37},{6,14},{7,39},{8,16},{9,4... | collective-permute-start | bytes 614408 | tf_op jit(solution)/shard_map/ppermute | solution.py:58
  31.2 4.2 %collective-permute-start.21 = (f32[2,1600]{1,0:T(2,128)S(1)}, f32[2,1600]{1,0:T(2,128)S(1)}, u32[]{:S(2)}, u32[]{:S(2)}) collective-permute-start(f32[2,1600]{1,0:T(2,128)S(1)} %pad_maximum_fusion.2), channel_id=1, source_target_pairs={{0,1},{1,0},{2,3},{3,2},{4,5},{5,4},{6,7},{7,6},{8,9},{9,8},{10,11... | collective-permute-start | bytes 38408 | tf_op jit(solution)/shard_map/ppermute | solution.py:66
  32.5 8.9 %collective-permute-start.3 = (bf16[32,3200]{1,0:T(8,128)(2,1)S(1)}, bf16[32,3200]{1,0:T(8,128)(2,1)S(1)}, u32[]{:S(2)}, u32[]{:S(2)}) collective-permute-start(bf16[32,3200]{1,0:T(8,128)(2,1)S(1)} %get-tuple-element.35), channel_id=1, source_target_pairs={{0,24},{1,97},{2,26},{3,99},{4,28},{5,101},{6,30},{7,103},{8,0},{9... | collective-permute-start | bytes 614408 | tf_op jit(solution)/shard_map/ppermute | solution.py:58
  35.5 7.0 %collective-permute-start.2 = (bf16[32,3200]{1,0:T(8,128)(2,1)S(1)}, bf16[32,3200]{1,0:T(8,128)(2,1)S(1)}, u32[]{:S(2)}, u32[]{:S(2)}) collective-permute-start(bf16[32,3200]{1,0:T(8,128)(2,1)S(1)} %get-tuple-element.36), channel_id=1, source_target_pairs={{0,8},{1,33},{2,10},{3,35},{4,12},{5,37},{6,14},{7,39},{8,16},{9,4... | collective-permute-start | bytes 614408 | tf_op jit(solution)/shard_map/ppermute | solution.py:58
  35.5 15.8 %collective-permute-start.24 = (f32[2,1600]{1,0:T(2,128)S(1)}, f32[2,1600]{1,0:T(2,128)S(1)}, u32[]{:S(2)}, u32[]{:S(2)}) collective-permute-start(f32[2,1600]{1,0:T(2,128)S(1)} %fusion.48), channel_id=1, source_target_pairs={{0,6},{2,0},{4,2},{6,4},{1,7},{3,1},{5,3},{7,5},{8,14},{10,8},{12,... | collective-permute-start | bytes 38408 | tf_op jit(solution)/shard_map/ppermute | solution.py:62
  39.7 13.0 %collective-permute-start.23 = (f32[2,1600]{1,0:T(2,128)S(1)}, f32[2,1600]{1,0:T(2,128)S(1)}, u32[]{:S(2)}, u32[]{:S(2)}) collective-permute-start(f32[2,1600]{1,0:T(2,128)S(1)} %fusion.48), channel_id=1, source_target_pairs={{0,2},{2,4},{4,6},{6,0},{1,3},{3,5},{5,7},{7,1},{8,10},{10,12},{12... | collective-permute-start | bytes 38408 | tf_op jit(solution)/shard_map/ppermute | solution.py:62
  39.7 13.0 %collective-permute-start.22 = (f32[2,1600]{1,0:T(2,128)S(1)}, f32[2,1600]{1,0:T(2,128)S(1)}, u32[]{:S(2)}, u32[]{:S(2)}) collective-permute-start(f32[2,1600]{1,0:T(2,128)S(1)} %fusion.48), channel_id=1, source_target_pairs={{0,4},{2,6},{4,0},{6,2},{1,5},{3,7},{5,1},{7,3},{8,12},{10,14},{12... | collective-permute-start | bytes 38408 | tf_op jit(solution)/shard_map/ppermute | solution.py:62
  44.5 12.7 %copy-start.7 = (f32[16,3200]{1,0:T(8,128)S(1)}, f32[16,3200]{1,0:T(8,128)}, u32[]{:S(2)}) copy-start(f32[16,3200]{1,0:T(8,128)} %param.20) | copy-start | bytes 614404
  44.5 12.7 %copy-start.8 = (f32[16,3200]{1,0:T(8,128)S(1)}, f32[16,3200]{1,0:T(8,128)}, u32[]{:S(2)}) copy-start(f32[16,3200]{1,0:T(8,128)} %param.18) | copy-start | bytes 614404
  44.5 12.7 %copy-start.9 = (f32[16,3200]{1,0:T(8,128)S(1)}, f32[16,3200]{1,0:T(8,128)}, u32[]{:S(2)}) copy-start(f32[16,3200]{1,0:T(8,128)} %param.21) | copy-start | bytes 614404
  44.5 12.7 %copy-start.10 = (f32[16,3200]{1,0:T(8,128)S(1)}, f32[16,3200]{1,0:T(8,128)}, u32[]{:S(2)}) copy-start(f32[16,3200]{1,0:T(8,128)} %param.19) | copy-start | bytes 614404
  46.7 7.0 %collective-permute-start.10 = (bf16[16,6400]{1,0:T(8,128)(2,1)S(1)}, bf16[16,6400]{1,0:T(8,128)(2,1)S(1)}, u32[]{:S(2)}, u32[]{:S(2)}) collective-permute-start(bf16[16,6400]{1,0:T(8,128)(2,1)S(1)} %fusion.5), channel_id=1, source_target_pairs={{0,32},{1,9},{2,34},{3,11},{4,36},{5,13},{6,38},{7,15},{8,40},{9,1... | collective-permute-start | bytes 614408 | tf_op jit(solution)/shard_map/ppermute | solution.py:58
  48.4 8.8 %collective-permute-start.8 = (bf16[16,6400]{1,0:T(8,128)(2,1)S(1)}, bf16[16,6400]{1,0:T(8,128)(2,1)S(1)}, u32[]{:S(2)}, u32[]{:S(2)}) collective-permute-start(bf16[16,6400]{1,0:T(8,128)(2,1)S(1)} %get-tuple-element.51), channel_id=1, source_target_pairs={{0,64},{1,17},{2,66},{3,19},{4,68},{5,21},{6,70},{7,23},{8,72},{9,... | collective-permute-start | bytes 614408 | tf_op jit(solution)/shard_map/ppermute | solution.py:58
  51.3 5.9 %collective-permute-start.9 = (bf16[16,6400]{1,0:T(8,128)(2,1)S(1)}, bf16[16,6400]{1,0:T(8,128)(2,1)S(1)}, u32[]{:S(2)}, u32[]{:S(2)}) collective-permute-start(bf16[16,6400]{1,0:T(8,128)(2,1)S(1)} %get-tuple-element.52), channel_id=1, source_target_pairs={{0,96},{1,25},{2,98},{3,27},{4,100},{5,29},{6,102},{7,31},{8,104},... | collective-permute-start | bytes 614408 | tf_op jit(solution)/shard_map/ppermute | solution.py:58
  52.8 10.1 %copy-start.4 = (bf16[640,1600]{0,1:T(8,128)(2,1)S(1)}, bf16[640,1600]{0,1:T(8,128)(2,1)}, u32[]{:S(2)}) copy-start(bf16[640,1600]{0,1:T(8,128)(2,1)} %param.14) | copy-start | bytes 6144004
  57.9 6.7 %collective-permute-start.13 = (f32[2,6400]{1,0:T(2,128)S(1)}, f32[2,6400]{1,0:T(2,128)S(1)}, u32[]{:S(2)}, u32[]{:S(2)}) collective-permute-start(f32[2,6400]{1,0:T(2,128)S(1)} %pad_maximum_fusion.1), channel_id=1, source_target_pairs={{0,96},{1,25},{2,98},{3,27},{4,100},{5,29},{6,102},{7,31},{8,104},... | collective-permute-start | bytes 153608 | tf_op jit(solution)/shard_map/ppermute | solution.py:58
  60.3 5.9 %collective-permute-start.12 = (f32[2,6400]{1,0:T(2,128)S(1)}, f32[2,6400]{1,0:T(2,128)S(1)}, u32[]{:S(2)}, u32[]{:S(2)}) collective-permute-start(f32[2,6400]{1,0:T(2,128)S(1)} %pad_maximum_fusion.1), channel_id=1, source_target_pairs={{0,32},{1,9},{2,34},{3,11},{4,36},{5,13},{6,38},{7,15},{8,40},{9,1... | collective-permute-start | bytes 153608 | tf_op jit(solution)/shard_map/ppermute | solution.py:58
  60.3 5.9 %collective-permute-start.11 = (f32[2,6400]{1,0:T(2,128)S(1)}, f32[2,6400]{1,0:T(2,128)S(1)}, u32[]{:S(2)}, u32[]{:S(2)}) collective-permute-start(f32[2,6400]{1,0:T(2,128)S(1)} %pad_maximum_fusion.1), channel_id=1, source_target_pairs={{0,64},{1,17},{2,66},{3,19},{4,68},{5,21},{6,70},{7,23},{8,72},{9,... | collective-permute-start | bytes 153608 | tf_op jit(solution)/shard_map/ppermute | solution.py:58
  66.3 4.7 %collective-permute-start.16 = (f32[2,6400]{1,0:T(2,128)S(1)}, f32[2,6400]{1,0:T(2,128)S(1)}, u32[]{:S(2)}, u32[]{:S(2)}) collective-permute-start(f32[2,6400]{1,0:T(2,128)S(1)} %add_add_fusion.1), channel_id=1, source_target_pairs={{0,24},{1,97},{2,26},{3,99},{4,28},{5,101},{6,30},{7,103},{8,0},{9... | collective-permute-start | bytes 153608 | tf_op jit(solution)/shard_map/ppermute | solution.py:58
  68.5 5.9 %collective-permute-start.15 = (f32[2,6400]{1,0:T(2,128)S(1)}, f32[2,6400]{1,0:T(2,128)S(1)}, u32[]{:S(2)}, u32[]{:S(2)}) collective-permute-start(f32[2,6400]{1,0:T(2,128)S(1)} %add_add_fusion.1), channel_id=1, source_target_pairs={{0,8},{1,33},{2,10},{3,35},{4,12},{5,37},{6,14},{7,39},{8,16},{9,4... | collective-permute-start | bytes 153608 | tf_op jit(solution)/shard_map/ppermute | solution.py:58
  68.5 5.9 %collective-permute-start.14 = (f32[2,6400]{1,0:T(2,128)S(1)}, f32[2,6400]{1,0:T(2,128)S(1)}, u32[]{:S(2)}, u32[]{:S(2)}) collective-permute-start(f32[2,6400]{1,0:T(2,128)S(1)} %add_add_fusion.1), channel_id=1, source_target_pairs={{0,16},{1,65},{2,18},{3,67},{4,20},{5,69},{6,22},{7,71},{8,24},{9,... | collective-permute-start | bytes 153608 | tf_op jit(solution)/shard_map/ppermute | solution.py:58

commit v2 on v1

v2 whole, which is shorter than its diff:
```python
import jax
import jax.numpy as jnp
from jax import lax
from jax.experimental import pallas as pl
from jax.experimental.pallas import tpu as pltpu
from jax.sharding import Mesh
from jax.sharding import PartitionSpec as P

STEP = 100

beta_first = 0.9
beta_second = 0.999
adam_epsilon = 1e-08
norm_epsilon = 1e-06
update_scale = 4.0

AXES = ("y", "x", "z", "core")
SIZES = (4, 4, 4, 2)
ALONG = ("y", "x")
ACROSS = ("z", "core")
F32 = jnp.float32
BF16 = jnp.bfloat16


def device_number(y, x, z, core):
    return ((y * 4 + x) * 4 + z) * 2 + core


def ring_pairs(shift, stage):
    pairs = []
    for y in range(4):
        for x in range(4):
            for z in range(4):
                for core in range(2):
                    source = device_number(y, x, z, core)
                    if (core == 0) == (stage == 0):
                        target = device_number(y, (x + shift) % 4, z, core)
                    else:
                        target = device_number((y + shift) % 4, x, z, core)
                    pairs.append((source, target))
    return pairs


def ring_send(value, shift, stage):
    return lax.ppermute(value, AXES, ring_pairs(shift, stage))


def z_swap(value, far):
    pairs = [(0, 3), (3, 0), (1, 2), (2, 1)] if far else [(0, 1), (1, 0), (2, 3), (3, 2)]
    return lax.ppermute(value, "z", pairs)


def core_send(value):
    return lax.ppermute(value, "core", [(0, 1), (1, 0)])


VMEM = pl.BlockSpec(memory_space=pltpu.VMEM)
HBM = pl.BlockSpec(memory_space=pltpu.HBM)


class Chain:
    def __init__(self):
        self.last = None

    def __call__(self, body, outs, *operands, in_specs=None, out_specs=None, scratch=(), limit=8):
        specs = [VMEM] * len(operands) if in_specs is None else list(in_specs)
        count, made = len(operands), len(outs)
        if self.last is not None:
            operands = operands + (self.last,)
            specs.append(VMEM)
        operands = [
            pltpu.with_memory_space_constraint(operand, spec.memory_space)
            for operand, spec in zip(operands, specs)
        ]

        def kernel(*refs):
            refs, token = refs[: len(operands)], refs[len(operands) :]
            token, rest = token[made], token[:made] + token[made + 1 :]
            token[...] = jnp.zeros_like(token)
            body(*refs[:count], *rest)

        *result, self.last = pl.pallas_call(
            kernel,
            out_shape=[*outs, pltpu.VMEM((8, 128), F32)],
            in_specs=specs,
            out_specs=[*([VMEM] * made if out_specs is None else out_specs), VMEM],
            scratch_shapes=scratch,
            compiler_params=pltpu.CompilerParams(vmem_limit_bytes=limit * 2**20),
            cost_estimate=pl.CostEstimate(flops=0, bytes_accessed=0, transcendentals=0),
        )(*operands)
        return result


def wide(*terms):
    total = terms[0].astype(F32)
    for term in terms[1:]:
        total = total + term.astype(F32)
    return total


def picked(rows, projection, contract):
    place = lax.broadcasted_iota(jnp.int32, (256, 256), 1)
    chosen = jnp.where(rows == place, 1.0, 0.0).astype(BF16)
    return lax.dot_general(chosen, projection, (((1,), (contract,)), ((), ())), preferred_element_type=F32).astype(BF16)


def fsdp_rows():
    y, x, core = lax.axis_index("y"), lax.axis_index("x"), lax.axis_index("core")
    step = lax.broadcasted_iota(jnp.int32, (256, 1), 0)
    outer, inner = step // 64, step // 16 % 4
    outer = jnp.where(outer == 0, 2, jnp.where(outer == 3, 0, jnp.where(outer == 1, 1, 3)))
    on_x, on_y = jnp.where(core == 0, outer, inner), jnp.where(core == 0, inner, outer)
    return ((y + on_y) % 4 * 4 + (x + on_x) % 4) * 16 + step % 16


def row_rows():
    z, core = lax.axis_index("z"), lax.axis_index("core")
    step = lax.broadcasted_iota(jnp.int32, (256, 1), 0)
    turn = step // 32 % 4
    to = jnp.where(turn % 2 == 0, z, 3 - z)
    to = jnp.where(turn < 2, to, to + 1 - to % 2 * 2)
    return (to * 2 + (core + step // 128) % 2) * 32 + step % 32


PARTS = tuple(range(0, 3200, 640))


def first_kernel(gate_proj, gate, up_proj, up, forth, back, gate_rest, up_rest, gate_kept, up_kept, projs, sems):
    copies = []
    for index, source in enumerate((gate_proj, up_proj)):
        copies.append(pltpu.make_async_copy(source, projs.at[index], sems.at[index]))
    for index, (source, target) in enumerate(((gate, gate_kept), (up, up_kept))):
        for number, at in enumerate(PARTS):
            to = pl.ds(at, 640)
            sem = sems.at[2 + index * 5 + number]
            copies.append(pltpu.make_async_copy(source.at[:, to], target.at[:, to], sem))
    for copy in copies:
        copy.start()
    rows = fsdp_rows()
    copies[0].wait()
    copies[1].wait()
    for index, (rest, kept) in enumerate(((gate_rest, gate_kept), (up_rest, up_kept))):
        ordered = picked(rows, projs[index], 1)
        rest[...] = ordered[64:]
        for number, at in enumerate(PARTS):
            copies[2 + index * 5 + number].wait()
            part = jnp.dot(ordered[:64], kept[:, at : at + 640], preferred_element_type=F32).astype(BF16)
            base = index * 3200 + at
            forth[:, base : base + 640] = part[:32]
            back[:, base : base + 640] = part[32:]


def rest_kernel(gate_rest, gate, up_rest, up, forth, back, near, far, keep):
    for rest, grad, base in ((gate_rest, gate, 0), (up_rest, up, 3200)):
        for at in range(0, 3200, 640):
            to = slice(base + at, base + at + 640)
            part = jnp.dot(rest[...], grad[:, at : at + 640], preferred_element_type=F32).astype(BF16)
            near[:, to] = part[:32]
            forth[:, to] = part[32:64]
            back[:, to] = part[64:96]
            far[:, to] = part[96:128]
            keep[:, to] = part[128:]


def pass_kernel(near, from_below, far, from_above, onward, backward):
    onward[...] = wide(near[...], from_below[...]).astype(BF16)
    backward[...] = wide(far[...], from_above[...]).astype(BF16)


def gather_kernel(keep, low_above, low_below, high_below, high_above, opposite, above, below, own):
    low = wide(keep[:32], low_above[...], low_below[...])
    high = wide(keep[32:], high_below[...], high_above[...])
    own[...] = low[:16]
    above[...] = low[16:].astype(BF16)
    opposite[...] = high[:16].astype(BF16)
    below[...] = high[16:].astype(BF16)


def moments(projected, first, second):
    return (
        beta_first * first[...] + (1.0 - beta_first) * projected,
        beta_second * second[...] + (1.0 - beta_second) * projected * projected,
    )


def channel_sums(projected, first, second):
    first_value, second_value = moments(projected, first, second)
    corrected = (
        first_value
        / (1.0 - beta_first**STEP)
        / (jnp.sqrt(second_value / (1.0 - beta_second**STEP)) + adam_epsilon)
    )
    return jnp.sum(corrected * corrected, 0, keepdims=True), jnp.sum(projected * projected, 0, keepdims=True)


def pair_sum_kernel(own, a, b, c, first_gate, second_gate, first_up, second_up, sums, total):
    projected = wide(own[...], a[...], b[...], c[...])
    total[...] = projected
    sums[0:1], sums[1:2] = channel_sums(projected[:, :3200], first_gate, second_gate)
    sums[2:3], sums[3:4] = channel_sums(projected[:, 3200:], first_up, second_up)


def pair_moment_kernel(total, first_gate, second_gate, first_up, second_up, *news):
    news[0][...], news[1][...] = moments(total[:, :3200], first_gate, second_gate)
    news[2][...], news[3][...] = moments(total[:, 3200:], first_up, second_up)


def down_sum_kernel(own, other, first, second, sums, total):
    projected = wide(own[...], other[...])
    total[...] = projected
    sums[0:1], sums[1:2] = channel_sums(projected, first, second)


def down_moment_kernel(total, first, second, *news):
    news[0][...], news[1][...] = moments(total[...], first, second)


def add_kernel(*refs):
    refs[-1][...] = wide(*(ref[...] for ref in refs[:-1]))


def scale_of(corrected_sq, projected_sq):
    return update_scale * (jnp.sqrt(corrected_sq) / (jnp.sqrt(projected_sq) + norm_epsilon))


def update_kernel(gate, up, a, b, c, d, gate_out, up_out, gate_made, up_made, sems):
    sums = wide(a[...], b[...], c[...], d[...])
    copies = []
    for index, (grad, made, out) in enumerate(((gate, gate_made, gate_out), (up, up_made, up_out))):
        scale = scale_of(sums[2 * index : 2 * index + 1], sums[2 * index + 1 : 2 * index + 2])
        for number in range(5):
            rows = pl.ds(number * 64, 64)
            made[rows, :] = (grad[rows, :].astype(F32) * scale).astype(BF16)
            copies.append(pltpu.make_async_copy(made.at[rows], out.at[rows], sems.at[index * 5 + number]))
            copies[-1].start()
    for copy in copies:
        copy.wait()


def down_kernel(proj, grad, own, other):
    ordered = picked(row_rows(), proj[...], 0)
    for at, size in ((0, 512), (512, 512), (1024, 576)):
        part = lax.dot_general(
            ordered, grad[at : at + size], (((1,), (1,)), ((), ())), preferred_element_type=F32
        ).astype(BF16)
        own[:, at : at + size] = part[:128]
        other[:, at : at + size] = part[128:]


def down_split_kernel(own, other, keep, send):
    total = wide(own[...], other[...])
    keep[...] = total[:64]
    send[...] = total[64:].astype(BF16)


def down_halve_kernel(own, other, keep, send):
    total = wide(own[...], other[...])
    keep[...] = total[:32]
    send[...] = total[32:].astype(BF16)


def down_update_kernel(grad, own, other, out, scale):
    sums = wide(own[...], other[...])
    scale[:, :1600] = scale_of(sums[0:1], sums[1:2])
    for at in range(0, 1600, 128):
        size = min(128, 1600 - at)
        column = jnp.broadcast_to(scale[:, at : at + 128], (128, 128)).T[:size]
        for lane in range(0, 640, 128):
            block = grad[at : at + size, lane : lane + 128].astype(F32) * column
            out[at : at + size, lane : lane + 128] = block.astype(BF16)


def per_device(
    grad_gate,
    grad_up,
    grad_down,
    proj_gate,
    proj_up,
    proj_down,
    first_gate,
    second_gate,
    first_up,
    second_up,
    first_down,
    second_down,
):
    gate, up, down = grad_gate.T, grad_up.T, grad_down.T
    run = Chain()
    half, piece = pltpu.VMEM((32, 6400), BF16), pltpu.VMEM((16, 6400), BF16)
    part, held = pltpu.VMEM((192, 320), BF16), pltpu.VMEM((320, 3200), BF16)
    row, pair_row = pltpu.VMEM((2, 1600), F32), pltpu.VMEM((4, 3200), F32)
    whole = jax.ShapeDtypeStruct((320, 3200), BF16)
    state, down_state = jax.ShapeDtypeStruct((16, 3200), F32), jax.ShapeDtypeStruct((32, 1600), F32)

    forth, back, rest_g, rest_u, gate, up = run(
        first_kernel,
        (half, half, part, part, held, held),
        proj_gate.T, gate, proj_up.T, up,
        in_specs=(HBM,) * 4,
        scratch=(pltpu.VMEM((2, 320, 256), BF16), pltpu.SemaphoreType.DMA((12,))),
    )
    from_below, from_above = ring_send(forth, 1, 0), ring_send(back, 3, 0)
    forth, back, near, far, keep = run(
        rest_kernel, (half, half, half, half, pltpu.VMEM((64, 6400), BF16)), rest_g, gate, rest_u, up
    )
    high_below, low_above = ring_send(forth, 1, 0), ring_send(back, 3, 0)

    own_down, other_down = run(down_kernel, (pltpu.VMEM((128, 1600), BF16),) * 2, proj_down, down)
    other_down = core_send(other_down)

    forth, back = run(pass_kernel, (half, half), near, from_below, far, from_above)
    low_below, high_above = ring_send(forth, 1, 0), ring_send(back, 3, 0)

    own_down, other_down = run(
        down_split_kernel, (pltpu.VMEM((64, 1600), F32), pltpu.VMEM((64, 1600), BF16)), own_down, other_down
    )
    other_down = z_swap(other_down, False)
    own_down, other_down = run(
        down_halve_kernel, (pltpu.VMEM((32, 1600), F32), pltpu.VMEM((32, 1600), BF16)), own_down, other_down
    )
    other_down = z_swap(other_down, True)
    sums_d, total_d = run(
        down_sum_kernel, (row, pltpu.VMEM((32, 1600), F32)), own_down, other_down, first_down, second_down
    )
    other_d = core_send(sums_d)

    opposite, above, below, own = run(
        gather_kernel,
        (piece, piece, piece, pltpu.VMEM((16, 6400), F32)),
        keep, low_above, low_below, high_below, high_above,
    )
    opposite, above, below = ring_send(opposite, 2, 1), ring_send(above, 1, 1), ring_send(below, 3, 1)

    (sums_d,) = run(add_kernel, (row,), sums_d, other_d)
    other_d = z_swap(sums_d, False)

    states = (first_gate, second_gate, first_up, second_up)
    sums, total = run(
        pair_sum_kernel, (pair_row, pltpu.VMEM((16, 6400), F32)), own, opposite, above, below, *states
    )
    sums_one = (sums, ring_send(sums, 2, 1), ring_send(sums, 1, 1), ring_send(sums, 3, 1))
    (sums_d,) = run(add_kernel, (row,), sums_d, other_d)
    other_d = z_swap(sums_d, True)
    first_gate_new, second_gate_new, first_up_new, second_up_new = run(
        pair_moment_kernel, (state, state, state, state), total, *states
    )
    (sums,) = run(add_kernel, (pair_row,), *sums_one)
    sums_two = (sums, ring_send(sums, 2, 0), ring_send(sums, 1, 0), ring_send(sums, 3, 0))
    (update_down,) = run(
        down_update_kernel,
        (jax.ShapeDtypeStruct((1600, 640), BF16),),
        down, sums_d, other_d,
        scratch=(pltpu.VMEM((1, 1664), F32),),
    )
    first_down_new, second_down_new = run(
        down_moment_kernel, (down_state, down_state), total_d, first_down, second_down
    )
    update_gate, update_up = run(
        update_kernel,
        (whole, whole),
        gate, up, *sums_two,
        out_specs=(HBM, HBM),
        scratch=(held, held, pltpu.SemaphoreType.DMA((10,))),
    )
    return (
        update_gate.T,
        update_up.T,
        update_down.T,
        first_gate_new,
        second_gate_new,
        first_up_new,
        second_up_new,
        first_down_new,
        second_down_new,
    )


def solution(mesh):
    fine = Mesh(mesh.devices.reshape(SIZES), AXES)
    gradient, state = P(ACROSS, ALONG), P(ALONG, ACROSS)
    return jax.shard_map(
        per_device,
        mesh=fine,
        in_specs=(
            gradient,
            gradient,
            gradient,
            P(None, ALONG),
            P(None, ALONG),
            P(None, ACROSS),
            state,
            state,
            state,
            state,
            gradient,
            gradient,
        ),
        out_specs=(
            gradient,
            gradient,
            gradient,
            state,
            state,
            state,
            state,
            gradient,
            gradient,
        ),
        check_vma=False,
    )
```

time: 78.4 us -> 67.1 us (0.86)
  the two profiles are of different devices: /device:TPU:0 before, /device:TPU:10 now
where the time goes in v2:
time: 67.1 us; the launch traced here: 67 us
  starting transfers between devices  32.1 us (48%)
  waiting for transfers between devices  19.7 us (29%)
  Pallas kernels  14.3 us (21%)
  between operations  0.84 us (1%)
    ppermute x15, starting transfers between devices, ring_send(): return lax.ppermute(value, AXES, ring_pairs(shift, stage))  22.7 us
    pallas_call x16, Pallas kernels, __call__(): pl.pallas_call(kernel, out_shape=[*outs, pltpu.VMEM((8, 128), F32)], in_s...  14.3 us
    ppermute x4, waiting for transfers between devices, z_swap(): return lax.ppermute(value, 'z', pairs)  12 us
    ppermute x4, starting transfers between devices, z_swap(): return lax.ppermute(value, 'z', pairs)  9.37 us
    ppermute x15, waiting for transfers between devices, ring_send(): return lax.ppermute(value, AXES, ring_pairs(shift, stage))  6.54 us
  transfers between devices with their start and end apart: 21, of which 9 were waited for; matrix products, arithmetic and copies ran while one was open for 0% of the time, Pallas kernels for 10%

profile of v2, /device:TPU:10, one launch (start us, length us, event | category | flops | bytes accessed | tf_op | source)
XLA Modules:
  0.0 67.0 jit_solution(17946569233793357934)
XLA Ops:
  0.6 3.6 %shard_map.187 = (bf16[32,6400]{1,0:T(8,128)(2,1)S(1)}, bf16[32,6400]{1,0:T(8,128)(2,1)S(1)}, bf16[192,320]{1,0:T(8,128)(2,1)S(1)}, bf16[192,320]{1,0:T(8,128)(2...) custom-call(bf16[320,256]{1,0:T(8,128)(2,1)} %bitcast.12, ...), custom_call_target="tpu_custom_call" | custom-call | tf_op jit(solution)/shard_map/pallas_call | solution.py:82
  4.3 1.6 %collective-permute-start.1 = (bf16[32,6400]{1,0:T(8,128)(2,1)S(1)}, bf16[32,6400]{1,0:T(8,128)(2,1)S(1)}, u32[]{:S(2)}, u32[]{:S(2)}) collective-permute-start(bf16[32,6400]{1,0:T(8,128)(2,1)S(1)} %get-tuple-element.71), channel_id=1, source_target_pairs={{0,8},{1,33},{2,10},{3,35},{4,12},{5,37},{6,14},{7,39},{8,16},{9,4... | collective-permute-start | bytes 1228808 | tf_op jit(solution)/shard_map/ppermute | solution.py:45
  5.8 0.5 collective-permute-start.2
  6.4 1.7 %shard_map.188 = (bf16[32,6400]{1,0:T(8,128)(2,1)S(1)}, bf16[32,6400]{1,0:T(8,128)(2,1)S(1)}, bf16[32,6400]{1,0:T(8,128)(2,1)S(1)}, bf16[32,6400]{1,0:T(8,128)(2...) custom-call(bf16[192,320]{1,0:T(8,128)(2,1)S(1)} %get-tuple-element.65.refs_0_, ...), custom_call_target="tpu_custom_call" | custom-call | tf_op jit(solution)/shard_map/pallas_call | solution.py:82
  8.1 1.1 %shard_map.189 = (bf16[128,1600]{1,0:T(8,128)(2,1)S(1)}, bf16[128,1600]{1,0:T(8,128)(2,1)S(1)}, f32[8,128]{1,0:T(8,128)S(1)}) custom-call(bf16[256,640]{1,0:T(8,128)(2,1)S(1)} %copy-done.7, bf16[1600,640]{1,0:T(8,128)(2,1)S(1)} %bitcast.8, f32[8,128]{1,0:T(8,128)S(1)} %get-tuple-element.74.refs_2_), custom_call_target="tpu_custom_call" | custom-call | tf_op jit(solution)/shard_map/pallas_call | solution.py:82
  9.2 0.0 copy-start.1
  9.2 0.0 copy-start.2
  9.2 0.1 collective-permute-start.6
  9.3 1.8 %collective-permute-start = (bf16[32,6400]{1,0:T(8,128)(2,1)S(1)}, bf16[32,6400]{1,0:T(8,128)(2,1)S(1)}, u32[]{:S(2)}, u32[]{:S(2)}) collective-permute-start(bf16[32,6400]{1,0:T(8,128)(2,1)S(1)} %get-tuple-element.69), channel_id=1, source_target_pairs={{0,24},{1,97},{2,26},{3,99},{4,28},{5,101},{6,30},{7,103},{8,0},{9... | collective-permute-start | bytes 1228808 | tf_op jit(solution)/shard_map/ppermute | solution.py:45
  11.1 0.3 collective-permute-start.4
  11.4 0.9 %collective-permute-done.1.refs_1_ = bf16[32,6400]{1,0:T(8,128)(2,1)S(1)} collective-permute-done((bf16[32,6400]{1,0:T(8,128)(2,1)S(1)}, bf16[32,6400]{1,0:T(8,128)(2,1)S(1)}, u32[]{:S(2)}, u32[]{:S(2)}) %collective-permute-start.1) | collective-permute-done | bytes 409632 | tf_op jit(solution)/shard_map/ppermute | solution.py:45
  12.3 1.5 %collective-permute-done.2.refs_3_ = bf16[32,6400]{1,0:T(8,128)(2,1)S(1)} collective-permute-done((bf16[32,6400]{1,0:T(8,128)(2,1)S(1)}, bf16[32,6400]{1,0:T(8,128)(2,1)S(1)}, u32[]{:S(2)}, u32[]{:S(2)}) %collective-permute-start.2) | collective-permute-done | bytes 409632 | tf_op jit(solution)/shard_map/ppermute | solution.py:45
  13.8 0.2 shard_map.190
  14.0 1.3 %collective-permute-start.3 = (bf16[32,6400]{1,0:T(8,128)(2,1)S(1)}, bf16[32,6400]{1,0:T(8,128)(2,1)S(1)}, u32[]{:S(2)}, u32[]{:S(2)}) collective-permute-start(bf16[32,6400]{1,0:T(8,128)(2,1)S(1)} %get-tuple-element.76), channel_id=1, source_target_pairs={{0,8},{1,33},{2,10},{3,35},{4,12},{5,37},{6,14},{7,39},{8,16},{9,4... | collective-permute-start | bytes 1228808 | tf_op jit(solution)/shard_map/ppermute | solution.py:45
  15.3 0.8 %collective-permute-start.5 = (bf16[32,6400]{1,0:T(8,128)(2,1)S(1)}, bf16[32,6400]{1,0:T(8,128)(2,1)S(1)}, u32[]{:S(2)}, u32[]{:S(2)}) collective-permute-start(bf16[32,6400]{1,0:T(8,128)(2,1)S(1)} %get-tuple-element.78), channel_id=1, source_target_pairs={{0,24},{1,97},{2,26},{3,99},{4,28},{5,101},{6,30},{7,103},{8,0},{9... | collective-permute-start | bytes 1228808 | tf_op jit(solution)/shard_map/ppermute | solution.py:45
  16.1 0.0 collective-permute-done.6.refs_1_
  16.1 0.1 shard_map.191
  16.2 0.0 copy-start.3
  16.2 0.0 copy-start.4
  16.2 0.0 copy-start.5
  16.2 0.0 copy-start.6
  16.2 2.0 %collective-permute-start.7 = (bf16[64,1600]{1,0:T(8,128)(2,1)S(1)}, bf16[64,1600]{1,0:T(8,128)(2,1)S(1)}, u32[]{:S(2)}, u32[]{:S(2)}) collective-permute-start(bf16[64,1600]{1,0:T(8,128)(2,1)S(1)} %get-tuple-element.83), channel_id=1, source_target_pairs={{0,2},{2,0},{4,6},{6,4},{1,3},{3,1},{5,7},{7,5},{8,10},{10,8},{12,... | collective-permute-start | bytes 614408 | tf_op jit(solution)/shard_map/ppermute | solution.py:50
  18.2 3.9 %collective-permute-done.7.refs_1_ = bf16[64,1600]{1,0:T(8,128)(2,1)S(1)} collective-permute-done((bf16[64,1600]{1,0:T(8,128)(2,1)S(1)}, bf16[64,1600]{1,0:T(8,128)(2,1)S(1)}, u32[]{:S(2)}, u32[]{:S(2)}) %collective-permute-start.7) | collective-permute-done | bytes 204832 | tf_op jit(solution)/shard_map/ppermute | solution.py:50
  22.2 4.1 %collective-permute-start.8 = (bf16[32,1600]{1,0:T(8,128)(2,1)S(1)}, bf16[32,1600]{1,0:T(8,128)(2,1)S(1)}, u32[]{:S(2)}, u32[]{:S(2)}) collective-permute-start(bf16[32,1600]{1,0:T(8,128)(2,1)S(1)} %get-tuple-element.86), channel_id=1, source_target_pairs={{0,6},{6,0},{2,4},{4,2},{1,7},{7,1},{3,5},{5,3},{8,14},{14,8},{10,... | collective-permute-start | bytes 307208 | tf_op jit(solution)/shard_map/ppermute | solution.py:50
  26.3 2.7 %collective-permute-done.8.refs_1_ = bf16[32,1600]{1,0:T(8,128)(2,1)S(1)} collective-permute-done((bf16[32,1600]{1,0:T(8,128)(2,1)S(1)}, bf16[32,1600]{1,0:T(8,128)(2,1)S(1)}, u32[]{:S(2)}, u32[]{:S(2)}) %collective-permute-start.8) | collective-permute-done | bytes 102432 | tf_op jit(solution)/shard_map/ppermute | solution.py:50
  29.0 0.3 shard_map.193
  29.3 0.0 collective-permute-done.refs_1_
  29.3 0.3 shard_map.194
  29.7 2.4 %collective-permute-start.9 = (bf16[16,6400]{1,0:T(8,128)(2,1)S(1)}, bf16[16,6400]{1,0:T(8,128)(2,1)S(1)}, u32[]{:S(2)}, u32[]{:S(2)}) collective-permute-start(bf16[16,6400]{1,0:T(8,128)(2,1)S(1)} %get-tuple-element.90), channel_id=1, source_target_pairs={{0,64},{1,17},{2,66},{3,19},{4,68},{5,21},{6,70},{7,23},{8,72},{9,... | collective-permute-start | bytes 614408 | tf_op jit(solution)/shard_map/ppermute | solution.py:45
  32.0 0.4 collective-permute-start.10
  32.4 1.6 %collective-permute-start.11 = (bf16[16,6400]{1,0:T(8,128)(2,1)S(1)}, bf16[16,6400]{1,0:T(8,128)(2,1)S(1)}, u32[]{:S(2)}, u32[]{:S(2)}) collective-permute-start(bf16[16,6400]{1,0:T(8,128)(2,1)S(1)} %get-tuple-element.92), channel_id=1, source_target_pairs={{0,96},{1,25},{2,98},{3,27},{4,100},{5,29},{6,102},{7,31},{8,104},... | collective-permute-start | bytes 614408 | tf_op jit(solution)/shard_map/ppermute | solution.py:45
  34.0 1.2 %collective-permute-done.12.refs_1_ = f32[2,1600]{1,0:T(2,128)S(1)} collective-permute-done((f32[2,1600]{1,0:T(2,128)S(1)}, f32[2,1600]{1,0:T(2,128)S(1)}, u32[]{:S(2)}, u32[]{:S(2)}) %collective-permute-start.12) | collective-permute-done | bytes 12832 | tf_op jit(solution)/shard_map/ppermute | solution.py:54
  35.2 1.9 %collective-permute-done.9.refs_1_ = bf16[16,6400]{1,0:T(8,128)(2,1)S(1)} collective-permute-done((bf16[16,6400]{1,0:T(8,128)(2,1)S(1)}, bf16[16,6400]{1,0:T(8,128)(2,1)S(1)}, u32[]{:S(2)}, u32[]{:S(2)}) %collective-permute-start.9) | collective-permute-done | bytes 204832 | tf_op jit(solution)/shard_map/ppermute | solution.py:45
  37.1 2.2 %collective-permute-done.10.refs_2_ = bf16[16,6400]{1,0:T(8,128)(2,1)S(1)} collective-permute-done((bf16[16,6400]{1,0:T(8,128)(2,1)S(1)}, bf16[16,6400]{1,0:T(8,128)(2,1)S(1)}, u32[]{:S(2)}, u32[]{:S(2)}) %collective-permute-start.10) | collective-permute-done | bytes 204832 | tf_op jit(solution)/shard_map/ppermute | solution.py:45
  39.4 0.6 shard_map.196
  39.9 1.1 %collective-permute-start.15 = (f32[4,3200]{1,0:T(4,128)S(1)}, f32[4,3200]{1,0:T(4,128)S(1)}, u32[]{:S(2)}, u32[]{:S(2)}) collective-permute-start(f32[4,3200]{1,0:T(4,128)S(1)} %get-tuple-element.96.refs_0_), channel_id=1, source_target_pairs={{0,96},{1,25},{2,98},{3,27},{4,100},{5,29},{6,102},{7,31},{8,104},... | collective-permute-start | bytes 153608 | tf_op jit(solution)/shard_map/ppermute | solution.py:45
  41.1 1.0 %collective-permute-start.14 = (f32[4,3200]{1,0:T(4,128)S(1)}, f32[4,3200]{1,0:T(4,128)S(1)}, u32[]{:S(2)}, u32[]{:S(2)}) collective-permute-start(f32[4,3200]{1,0:T(4,128)S(1)} %get-tuple-element.96.refs_0_), channel_id=1, source_target_pairs={{0,32},{1,9},{2,34},{3,11},{4,36},{5,13},{6,38},{7,15},{8,40},{9,1... | collective-permute-start | bytes 153608 | tf_op jit(solution)/shard_map/ppermute | solution.py:45
  42.0 4.3 %collective-permute-start.13 = (f32[4,3200]{1,0:T(4,128)S(1)}, f32[4,3200]{1,0:T(4,128)S(1)}, u32[]{:S(2)}, u32[]{:S(2)}) collective-permute-start(f32[4,3200]{1,0:T(4,128)S(1)} %get-tuple-element.96.refs_0_), channel_id=1, source_target_pairs={{0,64},{1,17},{2,66},{3,19},{4,68},{5,21},{6,70},{7,23},{8,72},{9,... | collective-permute-start | bytes 153608 | tf_op jit(solution)/shard_map/ppermute | solution.py:45
  46.3 3.7 %collective-permute-done.16.refs_1_ = f32[2,1600]{1,0:T(2,128)S(1)} collective-permute-done((f32[2,1600]{1,0:T(2,128)S(1)}, f32[2,1600]{1,0:T(2,128)S(1)}, u32[]{:S(2)}, u32[]{:S(2)}) %collective-permute-start.16) | collective-permute-done | bytes 12832 | tf_op jit(solution)/shard_map/ppermute | solution.py:50
  50.0 1.0 %shard_map.198 = (f32[16,3200]{1,0:T(8,128)}, f32[16,3200]{1,0:T(8,128)}, f32[16,3200]{1,0:T(8,128)}, f32[16,3200]{1,0:T(8,128)}, f32[8,128]{1,0:T(8,128)S(1)}) custom-call(f32[16,6400]{1,0:T(8,128)S(1)} %get-tuple-element.97.refs_0_, f32[16,3200]{1,0:T(8,128)S(1)} %copy-done.3, f32[16,3200]{1,0:T(8,128)S(1)} %copy-done.4, f32[16,3200]{1,0:T(8,128)S(1)} %copy-done.5, ...), custom_call_target="tpu_custom_call" | custom-call | tf_op jit(solution)/shard_map/pallas_call | solution.py:82
  51.1 1.8 %collective-permute-start.19 = (f32[4,3200]{1,0:T(4,128)S(1)}, f32[4,3200]{1,0:T(4,128)S(1)}, u32[]{:S(2)}, u32[]{:S(2)}) collective-permute-start(f32[4,3200]{1,0:T(4,128)S(1)} %get-tuple-element.102.refs_2_), channel_id=1, source_target_pairs={{0,24},{1,97},{2,26},{3,99},{4,28},{5,101},{6,30},{7,103},{8,0},{9... | collective-permute-start | bytes 153608 | tf_op jit(solution)/shard_map/ppermute | solution.py:45
  52.9 0.3 collective-permute-start.18
  53.1 3.5 %collective-permute-start.17 = (f32[4,3200]{1,0:T(4,128)S(1)}, f32[4,3200]{1,0:T(4,128)S(1)}, u32[]{:S(2)}, u32[]{:S(2)}) collective-permute-start(f32[4,3200]{1,0:T(4,128)S(1)} %get-tuple-element.102.refs_2_), channel_id=1, source_target_pairs={{0,16},{1,65},{2,18},{3,67},{4,20},{5,69},{6,22},{7,71},{8,24},{9,... | collective-permute-start | bytes 153608 | tf_op jit(solution)/shard_map/ppermute | solution.py:45
  56.7 3.2 %collective-permute-start.20 = (f32[2,1600]{1,0:T(2,128)S(1)}, f32[2,1600]{1,0:T(2,128)S(1)}, u32[]{:S(2)}, u32[]{:S(2)}) collective-permute-start(f32[2,1600]{1,0:T(2,128)S(1)} %get-tuple-element.104.refs_1_), channel_id=1, source_target_pairs={{0,6},{6,0},{2,4},{4,2},{1,7},{7,1},{3,5},{5,3},{8,14},{14,8},{10,... | collective-permute-start | bytes 38408 | tf_op jit(solution)/shard_map/ppermute | solution.py:50
  59.9 1.7 %collective-permute-done.20.refs_2_ = f32[2,1600]{1,0:T(2,128)S(1)} collective-permute-done((f32[2,1600]{1,0:T(2,128)S(1)}, f32[2,1600]{1,0:T(2,128)S(1)}, u32[]{:S(2)}, u32[]{:S(2)}) %collective-permute-start.20) | collective-permute-done | bytes 12832 | tf_op jit(solution)/shard_map/ppermute | solution.py:50
  61.6 1.8 %shard_map.200 = (bf16[1600,640]{1,0:T(8,128)(2,1)}, f32[8,128]{1,0:T(8,128)S(1)}) custom-call(bf16[1600,640]{1,0:T(8,128)(2,1)S(1)} %bitcast.9, f32[2,1600]{1,0:T(2,128)S(1)} %get-tuple-element.104.refs_1_, f32[2,1600]{1,0:T(2,128)S(1)} %collective-permute-done.20.refs_2_, f32[8,128]{1,0:T(8,128)S(1)} %get-tuple-element.105.refs_3_), custom_call_target="tpu_custom_call" | custom-call | tf_op jit(solution)/shard_map/pallas_call | solution.py:82
  63.4 0.8 %shard_map.201 = (f32[32,1600]{1,0:T(8,128)}, f32[32,1600]{1,0:T(8,128)}, f32[8,128]{1,0:T(8,128)S(1)}) custom-call(f32[32,1600]{1,0:T(8,128)S(1)} %get-tuple-element.103.refs_0_, f32[32,1600]{1,0:T(8,128)S(1)} %copy-done.1, f32[32,1600]{1,0:T(8,128)S(1)} %copy-done.2, f32[8,128]{1,0:T(8,128)S(1)} %get-tuple-element.106.refs_3_), custom_call_target="tpu_custom_call" | custom-call | tf_op jit(solution)/shard_map/pallas_call | solution.py:82
  64.2 2.8 %shard_map.202 = (bf16[320,3200]{1,0:T(8,128)(2,1)}, bf16[320,3200]{1,0:T(8,128)(2,1)}, f32[8,128]{1,0:T(8,128)}) custom-call(bf16[320,3200]{1,0:T(8,128)(2,1)S(1)} %get-tuple-element.63.refs_1_.refs_0_, bf16[320,3200]{1,0:T(8,128)(2,1)S(1)} %get-tuple-element.64.refs_3_.refs_1_, f32[4,3200]{1,0:T(4,128)S(1)} %get-tuple-element.102.refs_2_, ...), custom_call_target="tpu_custom_call" | custom-call | tf_op jit(solution)/shard_map/pallas_call | solution.py:82
  (26 shorter events, 0.1 us)
Async XLA Ops:
  4.3 8.0 %collective-permute-start.1 = (bf16[32,6400]{1,0:T(8,128)(2,1)S(1)}, bf16[32,6400]{1,0:T(8,128)(2,1)S(1)}, u32[]{:S(2)}, u32[]{:S(2)}) collective-permute-start(bf16[32,6400]{1,0:T(8,128)(2,1)S(1)} %get-tuple-element.71), channel_id=1, source_target_pairs={{0,8},{1,33},{2,10},{3,35},{4,12},{5,37},{6,14},{7,39},{8,16},{9,4... | collective-permute-start | bytes 1228808 | tf_op jit(solution)/shard_map/ppermute | solution.py:45
  5.8 8.0 %collective-permute-start.2 = (bf16[32,6400]{1,0:T(8,128)(2,1)S(1)}, bf16[32,6400]{1,0:T(8,128)(2,1)S(1)}, u32[]{:S(2)}, u32[]{:S(2)}) collective-permute-start(bf16[32,6400]{1,0:T(8,128)(2,1)S(1)} %get-tuple-element.73), channel_id=1, source_target_pairs={{0,24},{1,97},{2,26},{3,99},{4,28},{5,101},{6,30},{7,103},{8,0},{9... | collective-permute-start | bytes 1228808 | tf_op jit(solution)/shard_map/ppermute | solution.py:45
  6.4 1.7 %copy-start = (bf16[640,1600]{0,1:T(8,128)(2,1)S(1)}, bf16[640,1600]{0,1:T(8,128)(2,1)}, u32[]{:S(2)}) copy-start(bf16[640,1600]{0,1:T(8,128)(2,1)} %param.14) | copy-start | bytes 6144004
  6.4 1.7 %copy-start.7 = (bf16[256,640]{1,0:T(8,128)(2,1)S(1)}, bf16[256,640]{1,0:T(8,128)(2,1)}, u32[]{:S(2)}) copy-start(bf16[256,640]{1,0:T(8,128)(2,1)} %refs_0_.1) | copy-start | bytes 983044
  9.2 19.9 %copy-start.1 = (f32[32,1600]{1,0:T(8,128)S(1)}, f32[32,1600]{1,0:T(8,128)}, u32[]{:S(2)}) copy-start(f32[32,1600]{1,0:T(8,128)} %refs_1_.3) | copy-start | bytes 614404
  9.2 19.9 %copy-start.2 = (f32[32,1600]{1,0:T(8,128)S(1)}, f32[32,1600]{1,0:T(8,128)}, u32[]{:S(2)}) copy-start(f32[32,1600]{1,0:T(8,128)} %refs_2_.5) | copy-start | bytes 614404
  9.2 6.9 %collective-permute-start.6 = (bf16[128,1600]{1,0:T(8,128)(2,1)S(1)}, bf16[128,1600]{1,0:T(8,128)(2,1)S(1)}, u32[]{:S(2)}, u32[]{:S(2)}) collective-permute-start(bf16[128,1600]{1,0:T(8,128)(2,1)S(1)} %get-tuple-element.80), channel_id=1, source_target_pairs={{0,1},{1,0},{2,3},{3,2},{4,5},{5,4},{6,7},{7,6},{8,9},{9,8},{10,11... | collective-permute-start | bytes 1228808 | tf_op jit(solution)/shard_map/ppermute | solution.py:54
  9.3 20.0 %collective-permute-start = (bf16[32,6400]{1,0:T(8,128)(2,1)S(1)}, bf16[32,6400]{1,0:T(8,128)(2,1)S(1)}, u32[]{:S(2)}, u32[]{:S(2)}) collective-permute-start(bf16[32,6400]{1,0:T(8,128)(2,1)S(1)} %get-tuple-element.69), channel_id=1, source_target_pairs={{0,24},{1,97},{2,26},{3,99},{4,28},{5,101},{6,30},{7,103},{8,0},{9... | collective-permute-start | bytes 1228808 | tf_op jit(solution)/shard_map/ppermute | solution.py:45
  11.1 18.2 %collective-permute-start.4 = (bf16[32,6400]{1,0:T(8,128)(2,1)S(1)}, bf16[32,6400]{1,0:T(8,128)(2,1)S(1)}, u32[]{:S(2)}, u32[]{:S(2)}) collective-permute-start(bf16[32,6400]{1,0:T(8,128)(2,1)S(1)} %get-tuple-element.77), channel_id=1, source_target_pairs={{0,8},{1,33},{2,10},{3,35},{4,12},{5,37},{6,14},{7,39},{8,16},{9,4... | collective-permute-start | bytes 1228808 | tf_op jit(solution)/shard_map/ppermute | solution.py:45
  14.0 15.3 %collective-permute-start.3 = (bf16[32,6400]{1,0:T(8,128)(2,1)S(1)}, bf16[32,6400]{1,0:T(8,128)(2,1)S(1)}, u32[]{:S(2)}, u32[]{:S(2)}) collective-permute-start(bf16[32,6400]{1,0:T(8,128)(2,1)S(1)} %get-tuple-element.76), channel_id=1, source_target_pairs={{0,8},{1,33},{2,10},{3,35},{4,12},{5,37},{6,14},{7,39},{8,16},{9,4... | collective-permute-start | bytes 1228808 | tf_op jit(solution)/shard_map/ppermute | solution.py:45
  15.3 14.1 %collective-permute-start.5 = (bf16[32,6400]{1,0:T(8,128)(2,1)S(1)}, bf16[32,6400]{1,0:T(8,128)(2,1)S(1)}, u32[]{:S(2)}, u32[]{:S(2)}) collective-permute-start(bf16[32,6400]{1,0:T(8,128)(2,1)S(1)} %get-tuple-element.78), channel_id=1, source_target_pairs={{0,24},{1,97},{2,26},{3,99},{4,28},{5,101},{6,30},{7,103},{8,0},{9... | collective-permute-start | bytes 1228808 | tf_op jit(solution)/shard_map/ppermute | solution.py:45
  16.2 23.2 %copy-start.3 = (f32[16,3200]{1,0:T(8,128)S(1)}, f32[16,3200]{1,0:T(8,128)}, u32[]{:S(2)}) copy-start(f32[16,3200]{1,0:T(8,128)} %refs_1_.2) | copy-start | bytes 614404
  16.2 23.2 %copy-start.4 = (f32[16,3200]{1,0:T(8,128)S(1)}, f32[16,3200]{1,0:T(8,128)}, u32[]{:S(2)}) copy-start(f32[16,3200]{1,0:T(8,128)} %refs_2_.4) | copy-start | bytes 614404
  16.2 23.1 %copy-start.5 = (f32[16,3200]{1,0:T(8,128)S(1)}, f32[16,3200]{1,0:T(8,128)}, u32[]{:S(2)}) copy-start(f32[16,3200]{1,0:T(8,128)} %refs_3_.3) | copy-start | bytes 614404
  16.2 23.1 %copy-start.6 = (f32[16,3200]{1,0:T(8,128)S(1)}, f32[16,3200]{1,0:T(8,128)}, u32[]{:S(2)}) copy-start(f32[16,3200]{1,0:T(8,128)} %refs_4_.3) | copy-start | bytes 614404
  16.2 5.9 %collective-permute-start.7 = (bf16[64,1600]{1,0:T(8,128)(2,1)S(1)}, bf16[64,1600]{1,0:T(8,128)(2,1)S(1)}, u32[]{:S(2)}, u32[]{:S(2)}) collective-permute-start(bf16[64,1600]{1,0:T(8,128)(2,1)S(1)} %get-tuple-element.83), channel_id=1, source_target_pairs={{0,2},{2,0},{4,6},{6,4},{1,3},{3,1},{5,7},{7,5},{8,10},{10,8},{12,... | collective-permute-start | bytes 614408 | tf_op jit(solution)/shard_map/ppermute | solution.py:50
  22.2 6.8 %collective-permute-start.8 = (bf16[32,1600]{1,0:T(8,128)(2,1)S(1)}, bf16[32,1600]{1,0:T(8,128)(2,1)S(1)}, u32[]{:S(2)}, u32[]{:S(2)}) collective-permute-start(bf16[32,1600]{1,0:T(8,128)(2,1)S(1)} %get-tuple-element.86), channel_id=1, source_target_pairs={{0,6},{6,0},{2,4},{4,2},{1,7},{7,1},{3,5},{5,3},{8,14},{14,8},{10,... | collective-permute-start | bytes 307208 | tf_op jit(solution)/shard_map/ppermute | solution.py:50
  29.7 7.4 %collective-permute-start.9 = (bf16[16,6400]{1,0:T(8,128)(2,1)S(1)}, bf16[16,6400]{1,0:T(8,128)(2,1)S(1)}, u32[]{:S(2)}, u32[]{:S(2)}) collective-permute-start(bf16[16,6400]{1,0:T(8,128)(2,1)S(1)} %get-tuple-element.90), channel_id=1, source_target_pairs={{0,64},{1,17},{2,66},{3,19},{4,68},{5,21},{6,70},{7,23},{8,72},{9,... | collective-permute-start | bytes 614408 | tf_op jit(solution)/shard_map/ppermute | solution.py:45
  32.0 7.3 %collective-permute-start.10 = (bf16[16,6400]{1,0:T(8,128)(2,1)S(1)}, bf16[16,6400]{1,0:T(8,128)(2,1)S(1)}, u32[]{:S(2)}, u32[]{:S(2)}) collective-permute-start(bf16[16,6400]{1,0:T(8,128)(2,1)S(1)} %get-tuple-element.91), channel_id=1, source_target_pairs={{0,32},{1,9},{2,34},{3,11},{4,36},{5,13},{6,38},{7,15},{8,40},{9,1... | collective-permute-start | bytes 614408 | tf_op jit(solution)/shard_map/ppermute | solution.py:45
  32.4 6.9 %collective-permute-start.11 = (bf16[16,6400]{1,0:T(8,128)(2,1)S(1)}, bf16[16,6400]{1,0:T(8,128)(2,1)S(1)}, u32[]{:S(2)}, u32[]{:S(2)}) collective-permute-start(bf16[16,6400]{1,0:T(8,128)(2,1)S(1)} %get-tuple-element.92), channel_id=1, source_target_pairs={{0,96},{1,25},{2,98},{3,27},{4,100},{5,29},{6,102},{7,31},{8,104},... | collective-permute-start | bytes 614408 | tf_op jit(solution)/shard_map/ppermute | solution.py:45
  34.0 1.2 %collective-permute-start.12 = (f32[2,1600]{1,0:T(2,128)S(1)}, f32[2,1600]{1,0:T(2,128)S(1)}, u32[]{:S(2)}, u32[]{:S(2)}) collective-permute-start(f32[2,1600]{1,0:T(2,128)S(1)} %get-tuple-element.93.refs_0_), channel_id=1, source_target_pairs={{0,1},{1,0},{2,3},{3,2},{4,5},{5,4},{6,7},{7,6},{8,9},{9,8},{10,11... | collective-permute-start | bytes 38408 | tf_op jit(solution)/shard_map/ppermute | solution.py:54
  39.9 11.1 %collective-permute-start.15 = (f32[4,3200]{1,0:T(4,128)S(1)}, f32[4,3200]{1,0:T(4,128)S(1)}, u32[]{:S(2)}, u32[]{:S(2)}) collective-permute-start(f32[4,3200]{1,0:T(4,128)S(1)} %get-tuple-element.96.refs_0_), channel_id=1, source_target_pairs={{0,96},{1,25},{2,98},{3,27},{4,100},{5,29},{6,102},{7,31},{8,104},... | collective-permute-start | bytes 153608 | tf_op jit(solution)/shard_map/ppermute | solution.py:45
  41.1 10.0 %collective-permute-start.14 = (f32[4,3200]{1,0:T(4,128)S(1)}, f32[4,3200]{1,0:T(4,128)S(1)}, u32[]{:S(2)}, u32[]{:S(2)}) collective-permute-start(f32[4,3200]{1,0:T(4,128)S(1)} %get-tuple-element.96.refs_0_), channel_id=1, source_target_pairs={{0,32},{1,9},{2,34},{3,11},{4,36},{5,13},{6,38},{7,15},{8,40},{9,1... | collective-permute-start | bytes 153608 | tf_op jit(solution)/shard_map/ppermute | solution.py:45
  42.0 9.0 %collective-permute-start.13 = (f32[4,3200]{1,0:T(4,128)S(1)}, f32[4,3200]{1,0:T(4,128)S(1)}, u32[]{:S(2)}, u32[]{:S(2)}) collective-permute-start(f32[4,3200]{1,0:T(4,128)S(1)} %get-tuple-element.96.refs_0_), channel_id=1, source_target_pairs={{0,64},{1,17},{2,66},{3,19},{4,68},{5,21},{6,70},{7,23},{8,72},{9,... | collective-permute-start | bytes 153608 | tf_op jit(solution)/shard_map/ppermute | solution.py:45
  46.3 3.7 %collective-permute-start.16 = (f32[2,1600]{1,0:T(2,128)S(1)}, f32[2,1600]{1,0:T(2,128)S(1)}, u32[]{:S(2)}, u32[]{:S(2)}) collective-permute-start(f32[2,1600]{1,0:T(2,128)S(1)} %get-tuple-element.98.refs_0_), channel_id=1, source_target_pairs={{0,2},{2,0},{4,6},{6,4},{1,3},{3,1},{5,7},{7,5},{8,10},{10,8},{12,... | collective-permute-start | bytes 38408 | tf_op jit(solution)/shard_map/ppermute | solution.py:50
  51.1 13.2 %collective-permute-start.19 = (f32[4,3200]{1,0:T(4,128)S(1)}, f32[4,3200]{1,0:T(4,128)S(1)}, u32[]{:S(2)}, u32[]{:S(2)}) collective-permute-start(f32[4,3200]{1,0:T(4,128)S(1)} %get-tuple-element.102.refs_2_), channel_id=1, source_target_pairs={{0,24},{1,97},{2,26},{3,99},{4,28},{5,101},{6,30},{7,103},{8,0},{9... | collective-permute-start | bytes 153608 | tf_op jit(solution)/shard_map/ppermute | solution.py:45
  52.9 11.4 %collective-permute-start.18 = (f32[4,3200]{1,0:T(4,128)S(1)}, f32[4,3200]{1,0:T(4,128)S(1)}, u32[]{:S(2)}, u32[]{:S(2)}) collective-permute-start(f32[4,3200]{1,0:T(4,128)S(1)} %get-tuple-element.102.refs_2_), channel_id=1, source_target_pairs={{0,8},{1,33},{2,10},{3,35},{4,12},{5,37},{6,14},{7,39},{8,16},{9,4... | collective-permute-start | bytes 153608 | tf_op jit(solution)/shard_map/ppermute | solution.py:45
  53.1 11.1 %collective-permute-start.17 = (f32[4,3200]{1,0:T(4,128)S(1)}, f32[4,3200]{1,0:T(4,128)S(1)}, u32[]{:S(2)}, u32[]{:S(2)}) collective-permute-start(f32[4,3200]{1,0:T(4,128)S(1)} %get-tuple-element.102.refs_2_), channel_id=1, source_target_pairs={{0,16},{1,65},{2,18},{3,67},{4,20},{5,69},{6,22},{7,71},{8,24},{9,... | collective-permute-start | bytes 153608 | tf_op jit(solution)/shard_map/ppermute | solution.py:45
  56.7 4.9 %collective-permute-start.20 = (f32[2,1600]{1,0:T(2,128)S(1)}, f32[2,1600]{1,0:T(2,128)S(1)}, u32[]{:S(2)}, u32[]{:S(2)}) collective-permute-start(f32[2,1600]{1,0:T(2,128)S(1)} %get-tuple-element.104.refs_1_), channel_id=1, source_target_pairs={{0,6},{6,0},{2,4},{4,2},{1,7},{7,1},{3,5},{5,3},{8,14},{14,8},{10,... | collective-permute-start | bytes 38408 | tf_op jit(solution)/shard_map/ppermute | solution.py:50

commit v3 on v2

--- a/solution.py
+++ b/solution.py
@@ -81,6 +81,7 @@
 
         *result, self.last = pl.pallas_call(
             kernel,
+            name=body.__name__,
             out_shape=[*outs, pltpu.VMEM((8, 128), F32)],
             in_specs=specs,
             out_specs=[*([VMEM] * made if out_specs is None else out_specs), VMEM],
@@ -109,6 +110,7 @@
     step = lax.broadcasted_iota(jnp.int32, (256, 1), 0)
     outer, inner = step // 64, step // 16 % 4
     outer = jnp.where(outer == 0, 2, jnp.where(outer == 3, 0, jnp.where(outer == 1, 1, 3)))
+    inner = jnp.where(inner == 1, 2, jnp.where(inner == 2, 1, inner))
     on_x, on_y = jnp.where(core == 0, outer, inner), jnp.where(core == 0, inner, outer)
     return ((y + on_y) % 4 * 4 + (x + on_x) % 4) * 16 + step % 16
 
@@ -126,25 +128,24 @@
 
 
 def first_kernel(gate_proj, gate, up_proj, up, forth, back, gate_rest, up_rest, gate_kept, up_kept, projs, sems):
-    copies = []
-    for index, source in enumerate((gate_proj, up_proj)):
-        copies.append(pltpu.make_async_copy(source, projs.at[index], sems.at[index]))
-    for index, (source, target) in enumerate(((gate, gate_kept), (up, up_kept))):
-        for number, at in enumerate(PARTS):
-            to = pl.ds(at, 640)
-            sem = sems.at[2 + index * 5 + number]
-            copies.append(pltpu.make_async_copy(source.at[:, to], target.at[:, to], sem))
+    copies = [
+        pltpu.make_async_copy(source, target, sems.at[index])
+        for index, (source, target) in enumerate(
+            ((gate_proj, projs.at[0]), (up_proj, projs.at[1]), (gate, gate_kept), (up, up_kept))
+        )
+    ]
     for copy in copies:
         copy.start()
     rows = fsdp_rows()
-    copies[0].wait()
-    copies[1].wait()
-    for index, (rest, kept) in enumerate(((gate_rest, gate_kept), (up_rest, up_kept))):
-        ordered = picked(rows, projs[index], 1)
-        rest[...] = ordered[64:]
-        for number, at in enumerate(PARTS):
-            copies[2 + index * 5 + number].wait()
-            part = jnp.dot(ordered[:64], kept[:, at : at + 640], preferred_element_type=F32).astype(BF16)
+    ordered = []
+    for index, rest in enumerate((gate_rest, up_rest)):
+        copies[index].wait()
+        ordered.append(picked(rows, projs[index], 1))
+        rest[...] = ordered[index][64:]
+    for index, kept in enumerate((gate_kept, up_kept)):
+        copies[2 + index].wait()
+        for at in range(0, 3200, 640):
+            part = jnp.dot(ordered[index][:64], kept[:, at : at + 640], preferred_element_type=F32).astype(BF16)
             base = index * 3200 + at
             forth[:, base : base + 640] = part[:32]
             back[:, base : base + 640] = part[32:]
@@ -167,13 +168,21 @@
     backward[...] = wide(far[...], from_above[...]).astype(BF16)
 
 
-def gather_kernel(keep, low_above, low_below, high_below, high_above, opposite, above, below, own):
-    low = wide(keep[:32], low_above[...], low_below[...])
-    high = wide(keep[32:], high_below[...], high_above[...])
-    own[...] = low[:16]
-    above[...] = low[16:].astype(BF16)
-    opposite[...] = high[:16].astype(BF16)
-    below[...] = high[16:].astype(BF16)
+def collect_kernel(keep, low_above, high_below, low, high):
+    low[...] = wide(keep[:32], low_above[...])
+    high[...] = wide(keep[32:], high_below[...])
+
+
+def near_kernel(low, low_below, own, opposite):
+    total = wide(low[...], low_below[...])
+    own[...] = total[:16]
+    opposite[...] = total[16:].astype(BF16)
+
+
+def far_kernel(high, high_above, above, below):
+    total = wide(high[...], high_above[...]).astype(BF16)
+    above[...] = total[:16]
+    below[...] = total[16:]
 
 
 def moments(projected, first, second):
@@ -193,8 +202,8 @@
     return jnp.sum(corrected * corrected, 0, keepdims=True), jnp.sum(projected * projected, 0, keepdims=True)
 
 
-def pair_sum_kernel(own, a, b, c, first_gate, second_gate, first_up, second_up, sums, total):
-    projected = wide(own[...], a[...], b[...], c[...])
+def pair_sum_kernel(own, a, b, first_gate, second_gate, first_up, second_up, sums, total):
+    projected = wide(own[...], a[...], b[...])
     total[...] = projected
     sums[0:1], sums[1:2] = channel_sums(projected[:, :3200], first_gate, second_gate)
     sums[2:3], sums[3:4] = channel_sums(projected[:, 3200:], first_up, second_up)
@@ -208,6 +217,7 @@
 def down_sum_kernel(own, other, first, second, sums, total):
     projected = wide(own[...], other[...])
     total[...] = projected
+    sums[...] = jnp.zeros_like(sums)
     sums[0:1], sums[1:2] = channel_sums(projected, first, second)
 
 
@@ -228,11 +238,10 @@
     copies = []
     for index, (grad, made, out) in enumerate(((gate, gate_made, gate_out), (up, up_made, up_out))):
         scale = scale_of(sums[2 * index : 2 * index + 1], sums[2 * index + 1 : 2 * index + 2])
-        for number in range(5):
-            rows = pl.ds(number * 64, 64)
-            made[rows, :] = (grad[rows, :].astype(F32) * scale).astype(BF16)
-            copies.append(pltpu.make_async_copy(made.at[rows], out.at[rows], sems.at[index * 5 + number]))
-            copies[-1].start()
+        for at in range(0, 320, 64):
+            made[at : at + 64] = (grad[at : at + 64].astype(F32) * scale).astype(BF16)
+        copies.append(pltpu.make_async_copy(made, out, sems.at[index]))
+        copies[-1].start()
     for copy in copies:
         copy.wait()
 
@@ -288,7 +297,7 @@
     run = Chain()
     half, piece = pltpu.VMEM((32, 6400), BF16), pltpu.VMEM((16, 6400), BF16)
     part, held = pltpu.VMEM((192, 320), BF16), pltpu.VMEM((320, 3200), BF16)
-    row, pair_row = pltpu.VMEM((2, 1600), F32), pltpu.VMEM((4, 3200), F32)
+    row, pair_row = pltpu.VMEM((8, 1600), F32), pltpu.VMEM((4, 3200), F32)
     whole = jax.ShapeDtypeStruct((320, 3200), BF16)
     state, down_state = jax.ShapeDtypeStruct((16, 3200), F32), jax.ShapeDtypeStruct((32, 1600), F32)
 
@@ -297,70 +306,66 @@
         (half, half, part, part, held, held),
         proj_gate.T, gate, proj_up.T, up,
         in_specs=(HBM,) * 4,
-        scratch=(pltpu.VMEM((2, 320, 256), BF16), pltpu.SemaphoreType.DMA((12,))),
+        scratch=(pltpu.VMEM((2, 320, 256), BF16), pltpu.SemaphoreType.DMA((4,))),
     )
     from_below, from_above = ring_send(forth, 1, 0), ring_send(back, 3, 0)
+    own_down, other_down = run(down_kernel, (pltpu.VMEM((128, 1600), BF16),) * 2, proj_down, down)
+    other_down = core_send(other_down)
     forth, back, near, far, keep = run(
         rest_kernel, (half, half, half, half, pltpu.VMEM((64, 6400), BF16)), rest_g, gate, rest_u, up
     )
     high_below, low_above = ring_send(forth, 1, 0), ring_send(back, 3, 0)
-
-    own_down, other_down = run(down_kernel, (pltpu.VMEM((128, 1600), BF16),) * 2, proj_down, down)
-    other_down = core_send(other_down)
-
     forth, back = run(pass_kernel, (half, half), near, from_below, far, from_above)
     low_below, high_above = ring_send(forth, 1, 0), ring_send(back, 3, 0)
-
     own_down, other_down = run(
         down_split_kernel, (pltpu.VMEM((64, 1600), F32), pltpu.VMEM((64, 1600), BF16)), own_down, other_down
     )
     other_down = z_swap(other_down, False)
+    low, high = run(collect_kernel, (pltpu.VMEM((32, 6400), F32),) * 2, keep, low_above, high_below)
+
+    own, opposite = run(near_kernel, (pltpu.VMEM((16, 6400), F32), piece), low, low_below)
+    opposite = ring_send(opposite, 2, 1)
+    above, below = run(far_kernel, (piece, piece), high, high_above)
+    above, below = ring_send(above, 1, 1), ring_send(below, 3, 1)
     own_down, other_down = run(
         down_halve_kernel, (pltpu.VMEM((32, 1600), F32), pltpu.VMEM((32, 1600), BF16)), own_down, other_down
     )
     other_down = z_swap(other_down, True)
+
+    states = (first_gate, second_gate, first_up, second_up)
+    (own,) = run(add_kernel, (pltpu.VMEM((16, 6400), F32),), own, opposite)
+    sums, total = run(
+        pair_sum_kernel, (pair_row, pltpu.VMEM((16, 6400), F32)), own, above, below, *states
+    )
+    sums_one = (sums, ring_send(sums, 2, 1), ring_send(sums, 1, 1), ring_send(sums, 3, 1))
     sums_d, total_d = run(
         down_sum_kernel, (row, pltpu.VMEM((32, 1600), F32)), own_down, other_down, first_down, second_down
     )
-    other_d = core_send(sums_d)
-
-    opposite, above, below, own = run(
-        gather_kernel,
-        (piece, piece, piece, pltpu.VMEM((16, 6400), F32)),
-        keep, low_above, low_below, high_below, high_above,
-    )
-    opposite, above, below = ring_send(opposite, 2, 1), ring_send(above, 1, 1), ring_send(below, 3, 1)
-
-    (sums_d,) = run(add_kernel, (row,), sums_d, other_d)
     other_d = z_swap(sums_d, False)
-
-    states = (first_gate, second_gate, first_up, second_up)
-    sums, total = run(
-        pair_sum_kernel, (pair_row, pltpu.VMEM((16, 6400), F32)), own, opposite, above, below, *states
-    )
-    sums_one = (sums, ring_send(sums, 2, 1), ring_send(sums, 1, 1), ring_send(sums, 3, 1))
+    first_gate_new, second_gate_new, first_up_new, second_up_new = run(
+        pair_moment_kernel, (state, state, state, state), total, *states
+    )
+    (sums,) = run(add_kernel, (pair_row,), *sums_one)
+    sums_two = (sums, ring_send(sums, 2, 0), ring_send(sums, 1, 0), ring_send(sums, 3, 0))
     (sums_d,) = run(add_kernel, (row,), sums_d, other_d)
     other_d = z_swap(sums_d, True)
-    first_gate_new, second_gate_new, first_up_new, second_up_new = run(
-        pair_moment_kernel, (state, state, state, state), total, *states
-    )
-    (sums,) = run(add_kernel, (pair_row,), *sums_one)
-    sums_two = (sums, ring_send(sums, 2, 0), ring_send(sums, 1, 0), ring_send(sums, 3, 0))
+    first_down_new, second_down_new = run(
+        down_moment_kernel, (down_state, down_state), total_d, first_down, second_down
+    )
+    update_gate, update_up = run(
+        update_kernel,
+        (whole, whole),
+        gate, up, *sums_two,
+        out_specs=(HBM, HBM),
+        scratch=(held, held, pltpu.SemaphoreType.DMA((2,))),
+    )
+    (sums_d,) = run(add_kernel, (row,), sums_d, other_d)
+    other_d = core_send(sums_d)
     (update_down,) = run(
         down_update_kernel,
         (jax.ShapeDtypeStruct((1600, 640), BF16),),
         down, sums_d, other_d,
         scratch=(pltpu.VMEM((1, 1664), F32),),
-    )
-    first_down_new, second_down_new = run(
-        down_moment_kernel, (down_state, down_state), total_d, first_down, second_down
-    )
-    update_gate, update_up = run(
-        update_kernel,
-        (whole, whole),
-        gate, up, *sums_two,
-        out_specs=(HBM, HBM),
-        scratch=(held, held, pltpu.SemaphoreType.DMA((10,))),
     )
     return (
         update_gate.T,

time: 67.1 us -> 59 us (0.88)
  the two profiles are of different devices: /device:TPU:10 before, /device:TPU:0 now
where the time goes in v3:
time: 59 us; the launch traced here: 57.8 us
  starting transfers between devices  32.9 us (56%)
  Pallas kernels  13.3 us (23%)
  waiting for transfers between devices  10.7 us (18%)
  between operations  0.84 us (1%)
    ppermute x15, starting transfers between devices, ring_send(): return lax.ppermute(value, AXES, ring_pairs(shift, stage))  21.7 us
    pallas_call x19, Pallas kernels, __call__(): pl.pallas_call(kernel, name=body.__name__, out_shape=[*outs, pltpu.VMEM((...  13.3 us
    ppermute x4, starting transfers between devices, z_swap(): return lax.ppermute(value, 'z', pairs)  11.1 us
    ppermute x15, waiting for transfers between devices, ring_send(): return lax.ppermute(value, AXES, ring_pairs(shift, stage))  9.48 us
    ppermute x2, waiting for transfers between devices, core_send(): return lax.ppermute(value, 'core', [(0, 1), (1, 0)])  1.23 us
  transfers between devices with their start and end apart: 21, of which 7 were waited for; matrix products, arithmetic and copies ran while one was open for 0% of the time, Pallas kernels for 15%

profile of v3, /device:TPU:0, one launch (start us, length us, event | category | flops | bytes accessed | tf_op | source)
XLA Modules:
  0.0 57.8 jit_solution(4023115414025797595)
XLA Ops:
  0.7 3.1 %first_kernel.1 = (bf16[32,6400]{1,0:T(8,128)(2,1)S(1)}, bf16[32,6400]{1,0:T(8,128)(2,1)S(1)}, bf16[192,320]{1,0:T(8,128)(2,1)S(1)}, bf16[192,320]{1,0:T(8,128)(...) custom-call(bf16[320,256]{1,0:T(8,128)(2,1)} %bitcast.12, ...), custom_call_target="tpu_custom_call" | custom-call | tf_op jit(solution)/shard_map/first_kernel/pallas_call | solution.py:82
  3.8 1.6 %collective-permute-start.3 = (bf16[32,6400]{1,0:T(8,128)(2,1)S(1)}, bf16[32,6400]{1,0:T(8,128)(2,1)S(1)}, u32[]{:S(2)}, u32[]{:S(2)}) collective-permute-start(bf16[32,6400]{1,0:T(8,128)(2,1)S(1)} %get-tuple-element.81), channel_id=1, source_target_pairs={{0,8},{1,33},{2,10},{3,35},{4,12},{5,37},{6,14},{7,39},{8,16},{9,4... | collective-permute-start | bytes 1228808 | tf_op jit(solution)/shard_map/ppermute | solution.py:45
  5.4 1.7 %collective-permute-start.4 = (bf16[32,6400]{1,0:T(8,128)(2,1)S(1)}, bf16[32,6400]{1,0:T(8,128)(2,1)S(1)}, u32[]{:S(2)}, u32[]{:S(2)}) collective-permute-start(bf16[32,6400]{1,0:T(8,128)(2,1)S(1)} %get-tuple-element.83), channel_id=1, source_target_pairs={{0,24},{1,97},{2,26},{3,99},{4,28},{5,101},{6,30},{7,103},{8,0},{9... | collective-permute-start | bytes 1228808 | tf_op jit(solution)/shard_map/ppermute | solution.py:45
  7.1 1.1 %down_kernel.1 = (bf16[128,1600]{1,0:T(8,128)(2,1)S(1)}, bf16[128,1600]{1,0:T(8,128)(2,1)S(1)}, f32[8,128]{1,0:T(8,128)S(1)}) custom-call(bf16[256,640]{1,0:T(8,128)(2,1)S(1)} %copy-done.7, bf16[1600,640]{1,0:T(8,128)(2,1)S(1)} %bitcast.8, f32[8,128]{1,0:T(8,128)S(1)} %get-tuple-element.73.refs_2_), custom_call_target="tpu_custom_call" | custom-call | tf_op jit(solution)/shard_map/down_kernel/pallas_call | solution.py:82
  8.2 0.1 collective-permute-start.2
  8.3 1.6 %rest_kernel.1 = (bf16[32,6400]{1,0:T(8,128)(2,1)S(1)}, bf16[32,6400]{1,0:T(8,128)(2,1)S(1)}, bf16[32,6400]{1,0:T(8,128)(2,1)S(1)}, bf16[32,6400]{1,0:T(8,128)(2...) custom-call(bf16[192,320]{1,0:T(8,128)(2,1)S(1)} %get-tuple-element.71.refs_0_, ...), custom_call_target="tpu_custom_call" | custom-call | tf_op jit(solution)/shard_map/rest_kernel/pallas_call | solution.py:82
  9.9 2.3 %collective-permute-start = (bf16[32,6400]{1,0:T(8,128)(2,1)S(1)}, bf16[32,6400]{1,0:T(8,128)(2,1)S(1)}, u32[]{:S(2)}, u32[]{:S(2)}) collective-permute-start(bf16[32,6400]{1,0:T(8,128)(2,1)S(1)} %get-tuple-element.76), channel_id=1, source_target_pairs={{0,24},{1,97},{2,26},{3,99},{4,28},{5,101},{6,30},{7,103},{8,0},{9... | collective-permute-start | bytes 1228808 | tf_op jit(solution)/shard_map/ppermute | solution.py:45
  12.2 0.0 collective-permute-start.1
  12.2 0.8 %collective-permute-done.3.refs_1_ = bf16[32,6400]{1,0:T(8,128)(2,1)S(1)} collective-permute-done((bf16[32,6400]{1,0:T(8,128)(2,1)S(1)}, bf16[32,6400]{1,0:T(8,128)(2,1)S(1)}, u32[]{:S(2)}, u32[]{:S(2)}) %collective-permute-start.3) | collective-permute-done | bytes 409632 | tf_op jit(solution)/shard_map/ppermute | solution.py:45
  13.0 0.4 collective-permute-done.4.refs_3_
  13.4 0.2 pass_kernel.1
  13.6 1.6 %collective-permute-start.5 = (bf16[32,6400]{1,0:T(8,128)(2,1)S(1)}, bf16[32,6400]{1,0:T(8,128)(2,1)S(1)}, u32[]{:S(2)}, u32[]{:S(2)}) collective-permute-start(bf16[32,6400]{1,0:T(8,128)(2,1)S(1)} %get-tuple-element.88), channel_id=1, source_target_pairs={{0,8},{1,33},{2,10},{3,35},{4,12},{5,37},{6,14},{7,39},{8,16},{9,4... | collective-permute-start | bytes 1228808 | tf_op jit(solution)/shard_map/ppermute | solution.py:45
  15.1 1.7 %collective-permute-start.8 = (bf16[32,6400]{1,0:T(8,128)(2,1)S(1)}, bf16[32,6400]{1,0:T(8,128)(2,1)S(1)}, u32[]{:S(2)}, u32[]{:S(2)}) collective-permute-start(bf16[32,6400]{1,0:T(8,128)(2,1)S(1)} %get-tuple-element.95), channel_id=1, source_target_pairs={{0,24},{1,97},{2,26},{3,99},{4,28},{5,101},{6,30},{7,103},{8,0},{9... | collective-permute-start | bytes 1228808 | tf_op jit(solution)/shard_map/ppermute | solution.py:45
  16.9 0.0 collective-permute-done.2.refs_1_
  16.9 0.1 down_split_kernel.1
  17.0 2.0 %collective-permute-start.7 = (bf16[64,1600]{1,0:T(8,128)(2,1)S(1)}, bf16[64,1600]{1,0:T(8,128)(2,1)S(1)}, u32[]{:S(2)}, u32[]{:S(2)}) collective-permute-start(bf16[64,1600]{1,0:T(8,128)(2,1)S(1)} %get-tuple-element.93), channel_id=1, source_target_pairs={{0,2},{2,0},{4,6},{6,4},{1,3},{3,1},{5,7},{7,5},{8,10},{10,8},{12,... | collective-permute-start | bytes 614408 | tf_op jit(solution)/shard_map/ppermute | solution.py:50
  19.0 2.4 %collective-permute-done.1.refs_2_ = bf16[32,6400]{1,0:T(8,128)(2,1)S(1)} collective-permute-done((bf16[32,6400]{1,0:T(8,128)(2,1)S(1)}, bf16[32,6400]{1,0:T(8,128)(2,1)S(1)}, u32[]{:S(2)}, u32[]{:S(2)}) %collective-permute-start.1) | collective-permute-done | bytes 409632 | tf_op jit(solution)/shard_map/ppermute | solution.py:45
  21.4 0.2 collect_kernel.1
  21.5 0.0 copy-start.3
  21.6 0.0 copy-start.4
  21.6 0.0 copy-start.5
  21.6 0.0 copy-start.6
  21.6 4.2 %collective-permute-done.5.refs_1_ = bf16[32,6400]{1,0:T(8,128)(2,1)S(1)} collective-permute-done((bf16[32,6400]{1,0:T(8,128)(2,1)S(1)}, bf16[32,6400]{1,0:T(8,128)(2,1)S(1)}, u32[]{:S(2)}, u32[]{:S(2)}) %collective-permute-start.5) | collective-permute-done | bytes 409632 | tf_op jit(solution)/shard_map/ppermute | solution.py:45
  25.7 0.1 near_kernel.1
  25.8 2.7 %collective-permute-start.6 = (bf16[16,6400]{1,0:T(8,128)(2,1)S(1)}, bf16[16,6400]{1,0:T(8,128)(2,1)S(1)}, u32[]{:S(2)}, u32[]{:S(2)}) collective-permute-start(bf16[16,6400]{1,0:T(8,128)(2,1)S(1)} %get-tuple-element.91), channel_id=1, source_target_pairs={{0,64},{1,17},{2,66},{3,19},{4,68},{5,21},{6,70},{7,23},{8,72},{9,... | collective-permute-start | bytes 614408 | tf_op jit(solution)/shard_map/ppermute | solution.py:45
  28.5 0.1 far_kernel.1
  28.6 1.1 %collective-permute-start.10 = (bf16[16,6400]{1,0:T(8,128)(2,1)S(1)}, bf16[16,6400]{1,0:T(8,128)(2,1)S(1)}, u32[]{:S(2)}, u32[]{:S(2)}) collective-permute-start(bf16[16,6400]{1,0:T(8,128)(2,1)S(1)} %get-tuple-element.101), channel_id=1, source_target_pairs={{0,96},{1,25},{2,98},{3,27},{4,100},{5,29},{6,102},{7,31},{8,104},... | collective-permute-start | bytes 614408 | tf_op jit(solution)/shard_map/ppermute | solution.py:45
  29.7 1.0 %collective-permute-start.9 = (bf16[16,6400]{1,0:T(8,128)(2,1)S(1)}, bf16[16,6400]{1,0:T(8,128)(2,1)S(1)}, u32[]{:S(2)}, u32[]{:S(2)}) collective-permute-start(bf16[16,6400]{1,0:T(8,128)(2,1)S(1)} %get-tuple-element.100), channel_id=1, source_target_pairs={{0,32},{1,9},{2,34},{3,11},{4,36},{5,13},{6,38},{7,15},{8,40},{9,1... | collective-permute-start | bytes 614408 | tf_op jit(solution)/shard_map/ppermute | solution.py:45
  30.7 0.1 down_halve_kernel.1
  30.7 4.1 %collective-permute-start.14 = (bf16[32,1600]{1,0:T(8,128)(2,1)S(1)}, bf16[32,1600]{1,0:T(8,128)(2,1)S(1)}, u32[]{:S(2)}, u32[]{:S(2)}) collective-permute-start(bf16[32,1600]{1,0:T(8,128)(2,1)S(1)} %get-tuple-element.106), channel_id=1, source_target_pairs={{0,6},{6,0},{2,4},{4,2},{1,7},{7,1},{3,5},{5,3},{8,14},{14,8},{10,... | collective-permute-start | bytes 307208 | tf_op jit(solution)/shard_map/ppermute | solution.py:50
  34.9 0.2 collective-permute-done.10.refs_2_
  35.1 1.6 %collective-permute-done.9.refs_1_ = bf16[16,6400]{1,0:T(8,128)(2,1)S(1)} collective-permute-done((bf16[16,6400]{1,0:T(8,128)(2,1)S(1)}, bf16[16,6400]{1,0:T(8,128)(2,1)S(1)}, u32[]{:S(2)}, u32[]{:S(2)}) %collective-permute-start.9) | collective-permute-done | bytes 204832 | tf_op jit(solution)/shard_map/ppermute | solution.py:45
  36.7 0.6 pair_sum_kernel.1
  37.2 1.4 %collective-permute-start.11 = (f32[4,3200]{1,0:T(4,128)S(1)}, f32[4,3200]{1,0:T(4,128)S(1)}, u32[]{:S(2)}, u32[]{:S(2)}) collective-permute-start(f32[4,3200]{1,0:T(4,128)S(1)} %get-tuple-element.103.refs_0_), channel_id=1, source_target_pairs={{0,64},{1,17},{2,66},{3,19},{4,68},{5,21},{6,70},{7,23},{8,72},{9,... | collective-permute-start | bytes 153608 | tf_op jit(solution)/shard_map/ppermute | solution.py:45
  38.6 0.7 %collective-permute-start.12 = (f32[4,3200]{1,0:T(4,128)S(1)}, f32[4,3200]{1,0:T(4,128)S(1)}, u32[]{:S(2)}, u32[]{:S(2)}) collective-permute-start(f32[4,3200]{1,0:T(4,128)S(1)} %get-tuple-element.103.refs_0_), channel_id=1, source_target_pairs={{0,32},{1,9},{2,34},{3,11},{4,36},{5,13},{6,38},{7,15},{8,40},{9,1... | collective-permute-start | bytes 153608 | tf_op jit(solution)/shard_map/ppermute | solution.py:45
  39.3 2.5 %collective-permute-start.13 = (f32[4,3200]{1,0:T(4,128)S(1)}, f32[4,3200]{1,0:T(4,128)S(1)}, u32[]{:S(2)}, u32[]{:S(2)}) collective-permute-start(f32[4,3200]{1,0:T(4,128)S(1)} %get-tuple-element.103.refs_0_), channel_id=1, source_target_pairs={{0,96},{1,25},{2,98},{3,27},{4,100},{5,29},{6,102},{7,31},{8,104},... | collective-permute-start | bytes 153608 | tf_op jit(solution)/shard_map/ppermute | solution.py:45
  41.8 0.2 down_sum_kernel.1
  42.1 2.0 %collective-permute-start.18 = (f32[8,1600]{1,0:T(8,128)S(1)}, f32[8,1600]{1,0:T(8,128)S(1)}, u32[]{:S(2)}, u32[]{:S(2)}) collective-permute-start(f32[8,1600]{1,0:T(8,128)S(1)} %get-tuple-element.112.refs_0_), channel_id=1, source_target_pairs={{0,2},{2,0},{4,6},{6,4},{1,3},{3,1},{5,7},{7,5},{8,10},{10,8},{12,... | collective-permute-start | bytes 153608 | tf_op jit(solution)/shard_map/ppermute | solution.py:50
  44.1 1.0 %pair_moment_kernel.1 = (f32[16,3200]{1,0:T(8,128)}, f32[16,3200]{1,0:T(8,128)}, f32[16,3200]{1,0:T(8,128)}, f32[16,3200]{1,0:T(8,128)}, f32[8,128]{1,0:T(8,128)S(1)}) custom-call(f32[16,6400]{1,0:T(8,128)S(1)} %get-tuple-element.104.refs_0_, f32[16,3200]{1,0:T(8,128)S(1)} %copy-done.3, f32[16,3200]{1,0:T(8,128)S(1)} %copy-done.4, f32[16,3200]{1,0:T(8,128)S(1)} %copy-done.5, ...), custom_call_target="tpu_custom_call" | custom-call | tf_op jit(solution)/shard_map/pair_moment_kernel/pallas_call | solution.py:82
  45.1 0.1 collective-permute-start.15
  45.2 0.5 collective-permute-start.16
  45.7 2.8 %collective-permute-start.17 = (f32[4,3200]{1,0:T(4,128)S(1)}, f32[4,3200]{1,0:T(4,128)S(1)}, u32[]{:S(2)}, u32[]{:S(2)}) collective-permute-start(f32[4,3200]{1,0:T(4,128)S(1)} %get-tuple-element.110.refs_2_), channel_id=1, source_target_pairs={{0,24},{1,97},{2,26},{3,99},{4,28},{5,101},{6,30},{7,103},{8,0},{9... | collective-permute-start | bytes 153608 | tf_op jit(solution)/shard_map/ppermute | solution.py:45
  48.5 3.0 %collective-permute-start.19 = (f32[8,1600]{1,0:T(8,128)S(1)}, f32[8,1600]{1,0:T(8,128)S(1)}, u32[]{:S(2)}, u32[]{:S(2)}) collective-permute-start(f32[8,1600]{1,0:T(8,128)S(1)} %get-tuple-element.118.refs_0_), channel_id=1, source_target_pairs={{0,6},{6,0},{2,4},{4,2},{1,7},{7,1},{3,5},{5,3},{8,14},{14,8},{10,... | collective-permute-start | bytes 153608 | tf_op jit(solution)/shard_map/ppermute | solution.py:50
  51.5 0.8 %down_moment_kernel.1 = (f32[32,1600]{1,0:T(8,128)}, f32[32,1600]{1,0:T(8,128)}, f32[8,128]{1,0:T(8,128)S(1)}) custom-call(f32[32,1600]{1,0:T(8,128)S(1)} %get-tuple-element.111.refs_0_, f32[32,1600]{1,0:T(8,128)S(1)} %copy-done.1, f32[32,1600]{1,0:T(8,128)S(1)} %copy-done.2, f32[8,128]{1,0:T(8,128)S(1)} %get-tuple-element.114.refs_3_), custom_call_target="tpu_custom_call" | custom-call | tf_op jit(solution)/shard_map/down_moment_kernel/pallas_call | solution.py:82
  52.3 2.4 %update_kernel.1 = (bf16[320,3200]{1,0:T(8,128)(2,1)}, bf16[320,3200]{1,0:T(8,128)(2,1)}, f32[8,128]{1,0:T(8,128)S(1)}) custom-call(bf16[320,3200]{1,0:T(8,128)(2,1)S(1)} %get-tuple-element.69.refs_1_.refs_0_, bf16[320,3200]{1,0:T(8,128)(2,1)S(1)} %get-tuple-element.70.refs_3_.refs_1_, f32[4,3200]{1,0:T(4,128)S(1)} %get-tuple-element.110.refs_2_, ...), custom_call_target="tpu_custom_call" | custom-call | tf_op jit(solution)/shard_map/update_kernel/pallas_call | solution.py:82
  54.7 0.1 collective-permute-start.20
  54.8 1.2 %collective-permute-done.20.refs_2_ = f32[8,1600]{1,0:T(8,128)S(1)} collective-permute-done((f32[8,1600]{1,0:T(8,128)S(1)}, f32[8,1600]{1,0:T(8,128)S(1)}, u32[]{:S(2)}, u32[]{:S(2)}) %collective-permute-start.20) | collective-permute-done | bytes 51232 | tf_op jit(solution)/shard_map/ppermute | solution.py:54
  56.0 1.8 %down_update_kernel.1 = (bf16[1600,640]{1,0:T(8,128)(2,1)}, f32[8,128]{1,0:T(8,128)}) custom-call(bf16[1600,640]{1,0:T(8,128)(2,1)S(1)} %bitcast.9, f32[8,1600]{1,0:T(8,128)S(1)} %get-tuple-element.120.refs_1_, f32[8,1600]{1,0:T(8,128)S(1)} %collective-permute-done.20.refs_2_, f32[8,128]{1,0:T(8,128)S(1)} %get-tuple-element.121.refs_3_), custom_call_target="tpu_custom_call" | custom-call | tf_op jit(solution)/shard_map/down_update_kernel/pallas_call | solution.py:82
  (29 shorter events, 0.1 us)
Async XLA Ops:
  0.6 6.4 %copy-start = (bf16[640,1600]{0,1:T(8,128)(2,1)S(1)}, bf16[640,1600]{0,1:T(8,128)(2,1)}, u32[]{:S(2)}) copy-start(bf16[640,1600]{0,1:T(8,128)(2,1)} %param.14) | copy-start | bytes 6144004
  0.7 6.4 %copy-start.7 = (bf16[256,640]{1,0:T(8,128)(2,1)S(1)}, bf16[256,640]{1,0:T(8,128)(2,1)}, u32[]{:S(2)}) copy-start(bf16[256,640]{1,0:T(8,128)(2,1)} %refs_0_.1) | copy-start | bytes 983044
  3.8 9.2 %collective-permute-start.3 = (bf16[32,6400]{1,0:T(8,128)(2,1)S(1)}, bf16[32,6400]{1,0:T(8,128)(2,1)S(1)}, u32[]{:S(2)}, u32[]{:S(2)}) collective-permute-start(bf16[32,6400]{1,0:T(8,128)(2,1)S(1)} %get-tuple-element.81), channel_id=1, source_target_pairs={{0,8},{1,33},{2,10},{3,35},{4,12},{5,37},{6,14},{7,39},{8,16},{9,4... | collective-permute-start | bytes 1228808 | tf_op jit(solution)/shard_map/ppermute | solution.py:45
  5.4 8.0 %collective-permute-start.4 = (bf16[32,6400]{1,0:T(8,128)(2,1)S(1)}, bf16[32,6400]{1,0:T(8,128)(2,1)S(1)}, u32[]{:S(2)}, u32[]{:S(2)}) collective-permute-start(bf16[32,6400]{1,0:T(8,128)(2,1)S(1)} %get-tuple-element.83), channel_id=1, source_target_pairs={{0,24},{1,97},{2,26},{3,99},{4,28},{5,101},{6,30},{7,103},{8,0},{9... | collective-permute-start | bytes 1228808 | tf_op jit(solution)/shard_map/ppermute | solution.py:45
  8.2 8.7 %collective-permute-start.2 = (bf16[128,1600]{1,0:T(8,128)(2,1)S(1)}, bf16[128,1600]{1,0:T(8,128)(2,1)S(1)}, u32[]{:S(2)}, u32[]{:S(2)}) collective-permute-start(bf16[128,1600]{1,0:T(8,128)(2,1)S(1)} %get-tuple-element.79), channel_id=1, source_target_pairs={{0,1},{1,0},{2,3},{3,2},{4,5},{5,4},{6,7},{7,6},{8,9},{9,8},{10,11... | collective-permute-start | bytes 1228808 | tf_op jit(solution)/shard_map/ppermute | solution.py:54
  9.9 9.1 %collective-permute-start = (bf16[32,6400]{1,0:T(8,128)(2,1)S(1)}, bf16[32,6400]{1,0:T(8,128)(2,1)S(1)}, u32[]{:S(2)}, u32[]{:S(2)}) collective-permute-start(bf16[32,6400]{1,0:T(8,128)(2,1)S(1)} %get-tuple-element.76), channel_id=1, source_target_pairs={{0,24},{1,97},{2,26},{3,99},{4,28},{5,101},{6,30},{7,103},{8,0},{9... | collective-permute-start | bytes 1228808 | tf_op jit(solution)/shard_map/ppermute | solution.py:45
  12.2 9.2 %collective-permute-start.1 = (bf16[32,6400]{1,0:T(8,128)(2,1)S(1)}, bf16[32,6400]{1,0:T(8,128)(2,1)S(1)}, u32[]{:S(2)}, u32[]{:S(2)}) collective-permute-start(bf16[32,6400]{1,0:T(8,128)(2,1)S(1)} %get-tuple-element.77), channel_id=1, source_target_pairs={{0,8},{1,33},{2,10},{3,35},{4,12},{5,37},{6,14},{7,39},{8,16},{9,4... | collective-permute-start | bytes 1228808 | tf_op jit(solution)/shard_map/ppermute | solution.py:45
  13.6 12.2 %collective-permute-start.5 = (bf16[32,6400]{1,0:T(8,128)(2,1)S(1)}, bf16[32,6400]{1,0:T(8,128)(2,1)S(1)}, u32[]{:S(2)}, u32[]{:S(2)}) collective-permute-start(bf16[32,6400]{1,0:T(8,128)(2,1)S(1)} %get-tuple-element.88), channel_id=1, source_target_pairs={{0,8},{1,33},{2,10},{3,35},{4,12},{5,37},{6,14},{7,39},{8,16},{9,4... | collective-permute-start | bytes 1228808 | tf_op jit(solution)/shard_map/ppermute | solution.py:45
  15.1 13.3 %collective-permute-start.8 = (bf16[32,6400]{1,0:T(8,128)(2,1)S(1)}, bf16[32,6400]{1,0:T(8,128)(2,1)S(1)}, u32[]{:S(2)}, u32[]{:S(2)}) collective-permute-start(bf16[32,6400]{1,0:T(8,128)(2,1)S(1)} %get-tuple-element.95), channel_id=1, source_target_pairs={{0,24},{1,97},{2,26},{3,99},{4,28},{5,101},{6,30},{7,103},{8,0},{9... | collective-permute-start | bytes 1228808 | tf_op jit(solution)/shard_map/ppermute | solution.py:45
  17.0 13.7 %collective-permute-start.7 = (bf16[64,1600]{1,0:T(8,128)(2,1)S(1)}, bf16[64,1600]{1,0:T(8,128)(2,1)S(1)}, u32[]{:S(2)}, u32[]{:S(2)}) collective-permute-start(bf16[64,1600]{1,0:T(8,128)(2,1)S(1)} %get-tuple-element.93), channel_id=1, source_target_pairs={{0,2},{2,0},{4,6},{6,4},{1,3},{3,1},{5,7},{7,5},{8,10},{10,8},{12,... | collective-permute-start | bytes 614408 | tf_op jit(solution)/shard_map/ppermute | solution.py:50
  21.5 15.1 %copy-start.3 = (f32[16,3200]{1,0:T(8,128)S(1)}, f32[16,3200]{1,0:T(8,128)}, u32[]{:S(2)}) copy-start(f32[16,3200]{1,0:T(8,128)} %refs_1_.2) | copy-start | bytes 614404
  21.6 15.1 %copy-start.4 = (f32[16,3200]{1,0:T(8,128)S(1)}, f32[16,3200]{1,0:T(8,128)}, u32[]{:S(2)}) copy-start(f32[16,3200]{1,0:T(8,128)} %refs_2_.4) | copy-start | bytes 614404
  21.6 15.1 %copy-start.5 = (f32[16,3200]{1,0:T(8,128)S(1)}, f32[16,3200]{1,0:T(8,128)}, u32[]{:S(2)}) copy-start(f32[16,3200]{1,0:T(8,128)} %refs_3_.5) | copy-start | bytes 614404
  21.6 15.1 %copy-start.6 = (f32[16,3200]{1,0:T(8,128)S(1)}, f32[16,3200]{1,0:T(8,128)}, u32[]{:S(2)}) copy-start(f32[16,3200]{1,0:T(8,128)} %refs_4_.3) | copy-start | bytes 614404
  25.8 9.0 %collective-permute-start.6 = (bf16[16,6400]{1,0:T(8,128)(2,1)S(1)}, bf16[16,6400]{1,0:T(8,128)(2,1)S(1)}, u32[]{:S(2)}, u32[]{:S(2)}) collective-permute-start(bf16[16,6400]{1,0:T(8,128)(2,1)S(1)} %get-tuple-element.91), channel_id=1, source_target_pairs={{0,64},{1,17},{2,66},{3,19},{4,68},{5,21},{6,70},{7,23},{8,72},{9,... | collective-permute-start | bytes 614408 | tf_op jit(solution)/shard_map/ppermute | solution.py:45
  28.5 13.4 %copy-start.1 = (f32[32,1600]{1,0:T(8,128)S(1)}, f32[32,1600]{1,0:T(8,128)}, u32[]{:S(2)}) copy-start(f32[32,1600]{1,0:T(8,128)} %refs_1_.3) | copy-start | bytes 614404
  28.5 13.4 %copy-start.2 = (f32[32,1600]{1,0:T(8,128)S(1)}, f32[32,1600]{1,0:T(8,128)}, u32[]{:S(2)}) copy-start(f32[32,1600]{1,0:T(8,128)} %refs_2_.5) | copy-start | bytes 614404
  28.6 6.5 %collective-permute-start.10 = (bf16[16,6400]{1,0:T(8,128)(2,1)S(1)}, bf16[16,6400]{1,0:T(8,128)(2,1)S(1)}, u32[]{:S(2)}, u32[]{:S(2)}) collective-permute-start(bf16[16,6400]{1,0:T(8,128)(2,1)S(1)} %get-tuple-element.101), channel_id=1, source_target_pairs={{0,96},{1,25},{2,98},{3,27},{4,100},{5,29},{6,102},{7,31},{8,104},... | collective-permute-start | bytes 614408 | tf_op jit(solution)/shard_map/ppermute | solution.py:45
  29.7 7.0 %collective-permute-start.9 = (bf16[16,6400]{1,0:T(8,128)(2,1)S(1)}, bf16[16,6400]{1,0:T(8,128)(2,1)S(1)}, u32[]{:S(2)}, u32[]{:S(2)}) collective-permute-start(bf16[16,6400]{1,0:T(8,128)(2,1)S(1)} %get-tuple-element.100), channel_id=1, source_target_pairs={{0,32},{1,9},{2,34},{3,11},{4,36},{5,13},{6,38},{7,15},{8,40},{9,1... | collective-permute-start | bytes 614408 | tf_op jit(solution)/shard_map/ppermute | solution.py:45
  30.7 11.1 %collective-permute-start.14 = (bf16[32,1600]{1,0:T(8,128)(2,1)S(1)}, bf16[32,1600]{1,0:T(8,128)(2,1)S(1)}, u32[]{:S(2)}, u32[]{:S(2)}) collective-permute-start(bf16[32,1600]{1,0:T(8,128)(2,1)S(1)} %get-tuple-element.106), channel_id=1, source_target_pairs={{0,6},{6,0},{2,4},{4,2},{1,7},{7,1},{3,5},{5,3},{8,14},{14,8},{10,... | collective-permute-start | bytes 307208 | tf_op jit(solution)/shard_map/ppermute | solution.py:50
  37.2 7.8 %collective-permute-start.11 = (f32[4,3200]{1,0:T(4,128)S(1)}, f32[4,3200]{1,0:T(4,128)S(1)}, u32[]{:S(2)}, u32[]{:S(2)}) collective-permute-start(f32[4,3200]{1,0:T(4,128)S(1)} %get-tuple-element.103.refs_0_), channel_id=1, source_target_pairs={{0,64},{1,17},{2,66},{3,19},{4,68},{5,21},{6,70},{7,23},{8,72},{9,... | collective-permute-start | bytes 153608 | tf_op jit(solution)/shard_map/ppermute | solution.py:45
  38.6 6.5 %collective-permute-start.12 = (f32[4,3200]{1,0:T(4,128)S(1)}, f32[4,3200]{1,0:T(4,128)S(1)}, u32[]{:S(2)}, u32[]{:S(2)}) collective-permute-start(f32[4,3200]{1,0:T(4,128)S(1)} %get-tuple-element.103.refs_0_), channel_id=1, source_target_pairs={{0,32},{1,9},{2,34},{3,11},{4,36},{5,13},{6,38},{7,15},{8,40},{9,1... | collective-permute-start | bytes 153608 | tf_op jit(solution)/shard_map/ppermute | solution.py:45
  39.3 5.8 %collective-permute-start.13 = (f32[4,3200]{1,0:T(4,128)S(1)}, f32[4,3200]{1,0:T(4,128)S(1)}, u32[]{:S(2)}, u32[]{:S(2)}) collective-permute-start(f32[4,3200]{1,0:T(4,128)S(1)} %get-tuple-element.103.refs_0_), channel_id=1, source_target_pairs={{0,96},{1,25},{2,98},{3,27},{4,100},{5,29},{6,102},{7,31},{8,104},... | collective-permute-start | bytes 153608 | tf_op jit(solution)/shard_map/ppermute | solution.py:45
  42.1 6.4 %collective-permute-start.18 = (f32[8,1600]{1,0:T(8,128)S(1)}, f32[8,1600]{1,0:T(8,128)S(1)}, u32[]{:S(2)}, u32[]{:S(2)}) collective-permute-start(f32[8,1600]{1,0:T(8,128)S(1)} %get-tuple-element.112.refs_0_), channel_id=1, source_target_pairs={{0,2},{2,0},{4,6},{6,4},{1,3},{3,1},{5,7},{7,5},{8,10},{10,8},{12,... | collective-permute-start | bytes 153608 | tf_op jit(solution)/shard_map/ppermute | solution.py:50
  45.1 7.2 %collective-permute-start.15 = (f32[4,3200]{1,0:T(4,128)S(1)}, f32[4,3200]{1,0:T(4,128)S(1)}, u32[]{:S(2)}, u32[]{:S(2)}) collective-permute-start(f32[4,3200]{1,0:T(4,128)S(1)} %get-tuple-element.110.refs_2_), channel_id=1, source_target_pairs={{0,16},{1,65},{2,18},{3,67},{4,20},{5,69},{6,22},{7,71},{8,24},{9,... | collective-permute-start | bytes 153608 | tf_op jit(solution)/shard_map/ppermute | solution.py:45
  45.2 7.1 %collective-permute-start.16 = (f32[4,3200]{1,0:T(4,128)S(1)}, f32[4,3200]{1,0:T(4,128)S(1)}, u32[]{:S(2)}, u32[]{:S(2)}) collective-permute-start(f32[4,3200]{1,0:T(4,128)S(1)} %get-tuple-element.110.refs_2_), channel_id=1, source_target_pairs={{0,8},{1,33},{2,10},{3,35},{4,12},{5,37},{6,14},{7,39},{8,16},{9,4... | collective-permute-start | bytes 153608 | tf_op jit(solution)/shard_map/ppermute | solution.py:45
  45.7 6.6 %collective-permute-start.17 = (f32[4,3200]{1,0:T(4,128)S(1)}, f32[4,3200]{1,0:T(4,128)S(1)}, u32[]{:S(2)}, u32[]{:S(2)}) collective-permute-start(f32[4,3200]{1,0:T(4,128)S(1)} %get-tuple-element.110.refs_2_), channel_id=1, source_target_pairs={{0,24},{1,97},{2,26},{3,99},{4,28},{5,101},{6,30},{7,103},{8,0},{9... | collective-permute-start | bytes 153608 | tf_op jit(solution)/shard_map/ppermute | solution.py:45
  48.5 6.1 %collective-permute-start.19 = (f32[8,1600]{1,0:T(8,128)S(1)}, f32[8,1600]{1,0:T(8,128)S(1)}, u32[]{:S(2)}, u32[]{:S(2)}) collective-permute-start(f32[8,1600]{1,0:T(8,128)S(1)} %get-tuple-element.118.refs_0_), channel_id=1, source_target_pairs={{0,6},{6,0},{2,4},{4,2},{1,7},{7,1},{3,5},{5,3},{8,14},{14,8},{10,... | collective-permute-start | bytes 153608 | tf_op jit(solution)/shard_map/ppermute | solution.py:50
  54.7 1.3 %collective-permute-start.20 = (f32[8,1600]{1,0:T(8,128)S(1)}, f32[8,1600]{1,0:T(8,128)S(1)}, u32[]{:S(2)}, u32[]{:S(2)}) collective-permute-start(f32[8,1600]{1,0:T(8,128)S(1)} %get-tuple-element.120.refs_1_), channel_id=1, source_target_pairs={{0,1},{1,0},{2,3},{3,2},{4,5},{5,4},{6,7},{7,6},{8,9},{9,8},{10,11... | collective-permute-start | bytes 153608 | tf_op jit(solution)/shard_map/ppermute | solution.py:54

commit v4 on v3

--- a/solution.py
+++ b/solution.py
@@ -45,6 +45,21 @@
     return lax.ppermute(value, AXES, ring_pairs(shift, stage))
 
 
+def ring_swap(value, far, stage):
+    pairs = []
+    for y in range(4):
+        for x in range(4):
+            for z in range(4):
+                for core in range(2):
+                    source = device_number(y, x, z, core)
+                    if (core == 0) == (stage == 0):
+                        target = device_number(y, 3 - x if far else x ^ 1, z, core)
+                    else:
+                        target = device_number(3 - y if far else y ^ 1, x, z, core)
+                    pairs.append((source, target))
+    return lax.ppermute(value, AXES, pairs)
+
+
 def z_swap(value, far):
     pairs = [(0, 3), (3, 0), (1, 2), (2, 1)] if far else [(0, 1), (1, 0), (2, 3), (3, 2)]
     return lax.ppermute(value, "z", pairs)
@@ -128,27 +143,32 @@
 
 
 def first_kernel(gate_proj, gate, up_proj, up, forth, back, gate_rest, up_rest, gate_kept, up_kept, projs, sems):
-    copies = [
-        pltpu.make_async_copy(source, target, sems.at[index])
-        for index, (source, target) in enumerate(
-            ((gate_proj, projs.at[0]), (up_proj, projs.at[1]), (gate, gate_kept), (up, up_kept))
-        )
+    proj_copies = [
+        pltpu.make_async_copy(source, projs.at[index], sems.at[index]) for index, source in enumerate((gate_proj, up_proj))
     ]
-    for copy in copies:
+    parts = ((0, 0, 1664), (0, 1664, 1536), (1, 0, 1664), (1, 1664, 1536))
+    copies = []
+    for number, (index, at, size) in enumerate(parts):
+        source, target = ((gate, gate_kept), (up, up_kept))[index]
+        to = pl.ds(at, size)
+        copies.append(pltpu.make_async_copy(source.at[:, to], target.at[:, to], sems.at[2 + number]))
+    for copy in proj_copies + copies:
         copy.start()
     rows = fsdp_rows()
     ordered = []
     for index, rest in enumerate((gate_rest, up_rest)):
-        copies[index].wait()
+        proj_copies[index].wait()
         ordered.append(picked(rows, projs[index], 1))
         rest[...] = ordered[index][64:]
-    for index, kept in enumerate((gate_kept, up_kept)):
-        copies[2 + index].wait()
-        for at in range(0, 3200, 640):
-            part = jnp.dot(ordered[index][:64], kept[:, at : at + 640], preferred_element_type=F32).astype(BF16)
+    for copy, (index, start, size) in zip(copies, parts):
+        copy.wait()
+        kept = (gate_kept, up_kept)[index]
+        for at in range(start, start + size, 512):
+            width = min(512, start + size - at)
+            part = jnp.dot(ordered[index][:64], kept[:, at : at + width], preferred_element_type=F32).astype(BF16)
             base = index * 3200 + at
-            forth[:, base : base + 640] = part[:32]
-            back[:, base : base + 640] = part[32:]
+            forth[:, base : base + width] = part[:32]
+            back[:, base : base + width] = part[32:]
 
 
 def rest_kernel(gate_rest, gate, up_rest, up, forth, back, near, far, keep):
@@ -168,7 +188,7 @@
     backward[...] = wide(far[...], from_above[...]).astype(BF16)
 
 
-def collect_kernel(keep, low_above, high_below, low, high):
+def collect_kernel(keep, high_below, low_above, low, high):
     low[...] = wide(keep[:32], low_above[...])
     high[...] = wide(keep[32:], high_below[...])
 
@@ -202,44 +222,52 @@
     return jnp.sum(corrected * corrected, 0, keepdims=True), jnp.sum(projected * projected, 0, keepdims=True)
 
 
-def pair_sum_kernel(own, a, b, first_gate, second_gate, first_up, second_up, sums, total):
+def pair_sum_kernel(own, a, b, first_gate, second_gate, first_up, second_up, sums, sent, total):
     projected = wide(own[...], a[...], b[...])
     total[...] = projected
     sums[0:1], sums[1:2] = channel_sums(projected[:, :3200], first_gate, second_gate)
     sums[2:3], sums[3:4] = channel_sums(projected[:, 3200:], first_up, second_up)
-
-
-def pair_moment_kernel(total, first_gate, second_gate, first_up, second_up, *news):
+    sent[...] = sums[...].astype(BF16)
+
+
+def moment_kernel(total, total_d, first_gate, second_gate, first_up, second_up, first_down, second_down, *news):
     news[0][...], news[1][...] = moments(total[:, :3200], first_gate, second_gate)
     news[2][...], news[3][...] = moments(total[:, 3200:], first_up, second_up)
-
-
-def down_sum_kernel(own, other, first, second, sums, total):
+    news[4][...], news[5][...] = moments(total_d[...], first_down, second_down)
+
+
+def down_sum_kernel(own, other, first, second, sums, sent, total):
     projected = wide(own[...], other[...])
     total[...] = projected
     sums[...] = jnp.zeros_like(sums)
     sums[0:1], sums[1:2] = channel_sums(projected, first, second)
-
-
-def down_moment_kernel(total, first, second, *news):
-    news[0][...], news[1][...] = moments(total[...], first, second)
+    sent[...] = sums[...].astype(BF16)
 
 
 def add_kernel(*refs):
     refs[-1][...] = wide(*(ref[...] for ref in refs[:-1]))
 
 
+def sum_kernel(*refs):
+    total = wide(*(ref[...] for ref in refs[:-2]))
+    refs[-2][...] = total
+    refs[-1][...] = total.astype(BF16)
+
+
 def scale_of(corrected_sq, projected_sq):
     return update_scale * (jnp.sqrt(corrected_sq) / (jnp.sqrt(projected_sq) + norm_epsilon))
 
 
-def update_kernel(gate, up, a, b, c, d, gate_out, up_out, gate_made, up_made, sems):
-    sums = wide(a[...], b[...], c[...], d[...])
+def scale_kernel(own, other, scale):
+    sums = wide(own[...], other[...])
+    scale[0:1] = scale_of(sums[0:1], sums[1:2])
+    scale[1:2] = scale_of(sums[2:3], sums[3:4])
+
+
+def update_kernel(gate, up, scale, gate_out, up_out, gate_made, up_made, sems):
     copies = []
     for index, (grad, made, out) in enumerate(((gate, gate_made, gate_out), (up, up_made, up_out))):
-        scale = scale_of(sums[2 * index : 2 * index + 1], sums[2 * index + 1 : 2 * index + 2])
-        for at in range(0, 320, 64):
-            made[at : at + 64] = (grad[at : at + 64].astype(F32) * scale).astype(BF16)
+        made[...] = (grad[...].astype(F32) * scale[index : index + 1]).astype(BF16)
         copies.append(pltpu.make_async_copy(made, out, sems.at[index]))
         copies[-1].start()
     for copy in copies:
@@ -298,6 +326,7 @@
     half, piece = pltpu.VMEM((32, 6400), BF16), pltpu.VMEM((16, 6400), BF16)
     part, held = pltpu.VMEM((192, 320), BF16), pltpu.VMEM((320, 3200), BF16)
     row, pair_row = pltpu.VMEM((8, 1600), F32), pltpu.VMEM((4, 3200), F32)
+    sent_row, sent_pair = pltpu.VMEM((8, 1600), BF16), pltpu.VMEM((4, 3200), BF16)
     whole = jax.ShapeDtypeStruct((320, 3200), BF16)
     state, down_state = jax.ShapeDtypeStruct((16, 3200), F32), jax.ShapeDtypeStruct((32, 1600), F32)
 
@@ -306,22 +335,22 @@
         (half, half, part, part, held, held),
         proj_gate.T, gate, proj_up.T, up,
         in_specs=(HBM,) * 4,
-        scratch=(pltpu.VMEM((2, 320, 256), BF16), pltpu.SemaphoreType.DMA((4,))),
+        scratch=(pltpu.VMEM((2, 320, 256), BF16), pltpu.SemaphoreType.DMA((6,))),
     )
     from_below, from_above = ring_send(forth, 1, 0), ring_send(back, 3, 0)
+    forth, back, near, far, keep = run(
+        rest_kernel, (half, half, half, half, pltpu.VMEM((64, 6400), BF16)), rest_g, gate, rest_u, up
+    )
+    high_below, low_above = ring_send(forth, 1, 0), ring_send(back, 3, 0)
     own_down, other_down = run(down_kernel, (pltpu.VMEM((128, 1600), BF16),) * 2, proj_down, down)
     other_down = core_send(other_down)
-    forth, back, near, far, keep = run(
-        rest_kernel, (half, half, half, half, pltpu.VMEM((64, 6400), BF16)), rest_g, gate, rest_u, up
-    )
-    high_below, low_above = ring_send(forth, 1, 0), ring_send(back, 3, 0)
     forth, back = run(pass_kernel, (half, half), near, from_below, far, from_above)
     low_below, high_above = ring_send(forth, 1, 0), ring_send(back, 3, 0)
+    low, high = run(collect_kernel, (pltpu.VMEM((32, 6400), F32),) * 2, keep, high_below, low_above)
     own_down, other_down = run(
         down_split_kernel, (pltpu.VMEM((64, 1600), F32), pltpu.VMEM((64, 1600), BF16)), own_down, other_down
     )
     other_down = z_swap(other_down, False)
-    low, high = run(collect_kernel, (pltpu.VMEM((32, 6400), F32),) * 2, keep, low_above, high_below)
 
     own, opposite = run(near_kernel, (pltpu.VMEM((16, 6400), F32), piece), low, low_below)
     opposite = ring_send(opposite, 2, 1)
@@ -334,49 +363,44 @@
 
     states = (first_gate, second_gate, first_up, second_up)
     (own,) = run(add_kernel, (pltpu.VMEM((16, 6400), F32),), own, opposite)
-    sums, total = run(
-        pair_sum_kernel, (pair_row, pltpu.VMEM((16, 6400), F32)), own, above, below, *states
-    )
-    sums_one = (sums, ring_send(sums, 2, 1), ring_send(sums, 1, 1), ring_send(sums, 3, 1))
-    sums_d, total_d = run(
-        down_sum_kernel, (row, pltpu.VMEM((32, 1600), F32)), own_down, other_down, first_down, second_down
-    )
-    other_d = z_swap(sums_d, False)
-    first_gate_new, second_gate_new, first_up_new, second_up_new = run(
-        pair_moment_kernel, (state, state, state, state), total, *states
-    )
-    (sums,) = run(add_kernel, (pair_row,), *sums_one)
-    sums_two = (sums, ring_send(sums, 2, 0), ring_send(sums, 1, 0), ring_send(sums, 3, 0))
-    (sums_d,) = run(add_kernel, (row,), sums_d, other_d)
-    other_d = z_swap(sums_d, True)
-    first_down_new, second_down_new = run(
-        down_moment_kernel, (down_state, down_state), total_d, first_down, second_down
-    )
-    update_gate, update_up = run(
-        update_kernel,
-        (whole, whole),
-        gate, up, *sums_two,
-        out_specs=(HBM, HBM),
-        scratch=(held, held, pltpu.SemaphoreType.DMA((2,))),
-    )
-    (sums_d,) = run(add_kernel, (row,), sums_d, other_d)
-    other_d = core_send(sums_d)
+    sums, sent, total = run(
+        pair_sum_kernel, (pair_row, sent_pair, pltpu.VMEM((16, 6400), F32)), own, above, below, *states
+    )
+    other = ring_swap(sent, False, 1)
+    sums_d, sent_d, total_d = run(
+        down_sum_kernel, (row, sent_row, pltpu.VMEM((32, 1600), F32)), own_down, other_down, first_down, second_down
+    )
+    other_d = z_swap(sent_d, False)
+    sums, sent = run(sum_kernel, (pair_row, sent_pair), sums, other)
+    other = ring_swap(sent, True, 1)
+    sums_d, sent_d = run(sum_kernel, (row, sent_row), sums_d, other_d)
+    other_d = z_swap(sent_d, True)
+    sums, sent = run(sum_kernel, (pair_row, sent_pair), sums, other)
+    other = ring_swap(sent, False, 0)
+    sums_d, sent_d = run(sum_kernel, (row, sent_row), sums_d, other_d)
+    other_d = core_send(sent_d)
+    news = run(moment_kernel, (state,) * 4 + (down_state,) * 2, total, total_d, *states, first_down, second_down)
+    sums, sent = run(sum_kernel, (pair_row, sent_pair), sums, other)
+    other = ring_swap(sent, True, 0)
     (update_down,) = run(
         down_update_kernel,
         (jax.ShapeDtypeStruct((1600, 640), BF16),),
         down, sums_d, other_d,
         scratch=(pltpu.VMEM((1, 1664), F32),),
     )
+    (scale,) = run(scale_kernel, (pltpu.VMEM((2, 3200), F32),), sums, other)
+    update_gate, update_up = run(
+        update_kernel,
+        (whole, whole),
+        gate, up, scale,
+        out_specs=(HBM, HBM),
+        scratch=(held, held, pltpu.SemaphoreType.DMA((2,))),
+    )
     return (
         update_gate.T,
         update_up.T,
         update_down.T,
-        first_gate_new,
-        second_gate_new,
-        first_up_new,
-        second_up_new,
-        first_down_new,
-        second_down_new,
+        *news,
     )
 
 

time: 59 us -> 57.3 us (0.971); the launches traced: 57.8 us -> 57.2 us
  waiting for transfers between devices: 10.7 us -> 10 us
    ppermute x15 -> x9, waiting for transfers between devices: 9.48 us -> 3.65 us  [ring_send(): return lax.ppermute(value, AXES, ring_pairs(shift, stage))]
    ppermute x0 -> x4, starting transfers between devices: none -> 5.4 us  [ring_swap(): return lax.ppermute(value, AXES, pairs)]
    ppermute x15 -> x9, starting transfers between devices: 21.7 us -> 16.5 us  [ring_send(): return lax.ppermute(value, AXES, ring_pairs(shift, stage))]
    ppermute x0 -> x4, waiting for transfers between devices: none -> 3.43 us  [ring_swap(): return lax.ppermute(value, AXES, pairs)]
    ppermute x4, waiting for transfers between devices: 0.01 us -> 2.92 us  [z_swap(): return lax.ppermute(value, 'z', pairs)]
    ppermute x2, waiting for transfers between devices: 1.23 us -> 0.01 us  [core_send(): return lax.ppermute(value, 'core', [(0, 1), (1, 0)])]
    pallas_call x19 -> x21, Pallas kernels: 13.3 us -> 13.4 us  [__call__(): pl.pallas_call(kernel, name=body.__name__, out_shape=[*outs, pltpu.VMEM((...]
  transfers between devices with their start and end apart: 21 -> 19, of which waited for: 7 -> 8; matrix products, arithmetic and copies ran while one was open for 0% -> 0% of each run, Pallas kernels for 15% -> 13%
where the time goes in v4:
time: 57.3 us; the launch traced here: 57.2 us
  starting transfers between devices  32.9 us (57%)
  Pallas kernels  13.4 us (23%)
  waiting for transfers between devices  10 us (17%)
  between operations  0.84 us (1%)
    ppermute x9, starting transfers between devices, ring_send(): return lax.ppermute(value, AXES, ring_pairs(shift, stage))  16.5 us
    pallas_call x21, Pallas kernels, __call__(): pl.pallas_call(kernel, name=body.__name__, out_shape=[*outs, pltpu.VMEM((...  13.4 us
    ppermute x4, starting transfers between devices, z_swap(): return lax.ppermute(value, 'z', pairs)  10.8 us
    ppermute x4, starting transfers between devices, ring_swap(): return lax.ppermute(value, AXES, pairs)  5.4 us
    ppermute x9, waiting for transfers between devices, ring_send(): return lax.ppermute(value, AXES, ring_pairs(shift, stage))  3.65 us
    ppermute x4, waiting for transfers between devices, ring_swap(): return lax.ppermute(value, AXES, pairs)  3.43 us
    ppermute x4, waiting for transfers between devices, z_swap(): return lax.ppermute(value, 'z', pairs)  2.92 us
  transfers between devices with their start and end apart: 19, of which 8 were waited for; matrix products, arithmetic and copies ran while one was open for 0% of the time, Pallas kernels for 13%

profile of v4, /device:TPU:0, one launch (start us, length us, event | category | flops | bytes accessed | tf_op | source)
XLA Modules:
  0.0 57.2 jit_solution(13898978899750677980)
XLA Ops:
  0.6 2.8 %first_kernel.1 = (bf16[32,6400]{1,0:T(8,128)(2,1)S(1)}, bf16[32,6400]{1,0:T(8,128)(2,1)S(1)}, bf16[192,320]{1,0:T(8,128)(2,1)S(1)}, bf16[192,320]{1,0:T(8,128)(...) custom-call(bf16[320,256]{1,0:T(8,128)(2,1)} %bitcast.12, ...), custom_call_target="tpu_custom_call" | custom-call | tf_op jit(solution)/shard_map/first_kernel/pallas_call | solution.py:97
  3.5 1.6 %collective-permute-start.2 = (bf16[32,6400]{1,0:T(8,128)(2,1)S(1)}, bf16[32,6400]{1,0:T(8,128)(2,1)S(1)}, u32[]{:S(2)}, u32[]{:S(2)}) collective-permute-start(bf16[32,6400]{1,0:T(8,128)(2,1)S(1)} %get-tuple-element.90), channel_id=1, source_target_pairs={{0,8},{1,33},{2,10},{3,35},{4,12},{5,37},{6,14},{7,39},{8,16},{9,4... | collective-permute-start | bytes 1228808 | tf_op jit(solution)/shard_map/ppermute | solution.py:45
  5.1 1.7 %collective-permute-start.3 = (bf16[32,6400]{1,0:T(8,128)(2,1)S(1)}, bf16[32,6400]{1,0:T(8,128)(2,1)S(1)}, u32[]{:S(2)}, u32[]{:S(2)}) collective-permute-start(bf16[32,6400]{1,0:T(8,128)(2,1)S(1)} %get-tuple-element.92), channel_id=1, source_target_pairs={{0,24},{1,97},{2,26},{3,99},{4,28},{5,101},{6,30},{7,103},{8,0},{9... | collective-permute-start | bytes 1228808 | tf_op jit(solution)/shard_map/ppermute | solution.py:45
  6.8 1.6 %rest_kernel.1 = (bf16[32,6400]{1,0:T(8,128)(2,1)S(1)}, bf16[32,6400]{1,0:T(8,128)(2,1)S(1)}, bf16[32,6400]{1,0:T(8,128)(2,1)S(1)}, bf16[32,6400]{1,0:T(8,128)(2...) custom-call(bf16[192,320]{1,0:T(8,128)(2,1)S(1)} %get-tuple-element.83.refs_0_, ...), custom_call_target="tpu_custom_call" | custom-call | tf_op jit(solution)/shard_map/rest_kernel/pallas_call | solution.py:97
  8.4 0.4 collective-permute-start
  8.8 2.9 %collective-permute-start.1 = (bf16[32,6400]{1,0:T(8,128)(2,1)S(1)}, bf16[32,6400]{1,0:T(8,128)(2,1)S(1)}, u32[]{:S(2)}, u32[]{:S(2)}) collective-permute-start(bf16[32,6400]{1,0:T(8,128)(2,1)S(1)} %get-tuple-element.88), channel_id=1, source_target_pairs={{0,24},{1,97},{2,26},{3,99},{4,28},{5,101},{6,30},{7,103},{8,0},{9... | collective-permute-start | bytes 1228808 | tf_op jit(solution)/shard_map/ppermute | solution.py:45
  11.7 1.1 %down_kernel.1 = (bf16[128,1600]{1,0:T(8,128)(2,1)S(1)}, bf16[128,1600]{1,0:T(8,128)(2,1)S(1)}, f32[8,128]{1,0:T(8,128)S(1)}) custom-call(bf16[256,640]{1,0:T(8,128)(2,1)S(1)} %copy-done.7, bf16[1600,640]{1,0:T(8,128)(2,1)S(1)} %bitcast.8, f32[8,128]{1,0:T(8,128)S(1)} %get-tuple-element.93.refs_2_), custom_call_target="tpu_custom_call" | custom-call | tf_op jit(solution)/shard_map/down_kernel/pallas_call | solution.py:97
  12.8 0.1 collective-permute-start.5
  12.9 0.2 collective-permute-done.3.refs_3_
  13.1 0.2 pass_kernel.1
  13.3 1.6 %collective-permute-start.4 = (bf16[32,6400]{1,0:T(8,128)(2,1)S(1)}, bf16[32,6400]{1,0:T(8,128)(2,1)S(1)}, u32[]{:S(2)}, u32[]{:S(2)}) collective-permute-start(bf16[32,6400]{1,0:T(8,128)(2,1)S(1)} %get-tuple-element.97), channel_id=1, source_target_pairs={{0,8},{1,33},{2,10},{3,35},{4,12},{5,37},{6,14},{7,39},{8,16},{9,4... | collective-permute-start | bytes 1228808 | tf_op jit(solution)/shard_map/ppermute | solution.py:45
  14.8 1.7 %collective-permute-start.8 = (bf16[32,6400]{1,0:T(8,128)(2,1)S(1)}, bf16[32,6400]{1,0:T(8,128)(2,1)S(1)}, u32[]{:S(2)}, u32[]{:S(2)}) collective-permute-start(bf16[32,6400]{1,0:T(8,128)(2,1)S(1)} %get-tuple-element.107), channel_id=1, source_target_pairs={{0,24},{1,97},{2,26},{3,99},{4,28},{5,101},{6,30},{7,103},{8,0},{9... | collective-permute-start | bytes 1228808 | tf_op jit(solution)/shard_map/ppermute | solution.py:45
  16.6 1.0 %collective-permute-done.refs_1_ = bf16[32,6400]{1,0:T(8,128)(2,1)S(1)} collective-permute-done((bf16[32,6400]{1,0:T(8,128)(2,1)S(1)}, bf16[32,6400]{1,0:T(8,128)(2,1)S(1)}, u32[]{:S(2)}, u32[]{:S(2)}) %collective-permute-start) | collective-permute-done | bytes 409632 | tf_op jit(solution)/shard_map/ppermute | solution.py:45
  17.6 0.0 collective-permute-done.1.refs_2_
  17.6 0.2 collect_kernel.1
  17.8 0.1 down_split_kernel.1
  17.9 0.0 copy-start.3
  18.0 0.0 copy-start.4
  18.0 0.0 copy-start.5
  18.0 0.0 copy-start.6
  18.0 2.1 %collective-permute-start.7 = (bf16[64,1600]{1,0:T(8,128)(2,1)S(1)}, bf16[64,1600]{1,0:T(8,128)(2,1)S(1)}, u32[]{:S(2)}, u32[]{:S(2)}) collective-permute-start(bf16[64,1600]{1,0:T(8,128)(2,1)S(1)} %get-tuple-element.105), channel_id=1, source_target_pairs={{0,2},{2,0},{4,6},{6,4},{1,3},{3,1},{5,7},{7,5},{8,10},{10,8},{12,... | collective-permute-start | bytes 614408 | tf_op jit(solution)/shard_map/ppermute | solution.py:65
  20.1 2.4 %collective-permute-done.4.refs_1_ = bf16[32,6400]{1,0:T(8,128)(2,1)S(1)} collective-permute-done((bf16[32,6400]{1,0:T(8,128)(2,1)S(1)}, bf16[32,6400]{1,0:T(8,128)(2,1)S(1)}, u32[]{:S(2)}, u32[]{:S(2)}) %collective-permute-start.4) | collective-permute-done | bytes 409632 | tf_op jit(solution)/shard_map/ppermute | solution.py:45
  22.5 0.1 near_kernel.1
  22.6 3.3 %collective-permute-start.6 = (bf16[16,6400]{1,0:T(8,128)(2,1)S(1)}, bf16[16,6400]{1,0:T(8,128)(2,1)S(1)}, u32[]{:S(2)}, u32[]{:S(2)}) collective-permute-start(bf16[16,6400]{1,0:T(8,128)(2,1)S(1)} %get-tuple-element.103), channel_id=1, source_target_pairs={{0,64},{1,17},{2,66},{3,19},{4,68},{5,21},{6,70},{7,23},{8,72},{9,... | collective-permute-start | bytes 614408 | tf_op jit(solution)/shard_map/ppermute | solution.py:45
  25.9 0.0 collective-permute-done.8.refs_1_
  25.9 0.1 far_kernel.1
  26.0 0.7 %collective-permute-start.9 = (bf16[16,6400]{1,0:T(8,128)(2,1)S(1)}, bf16[16,6400]{1,0:T(8,128)(2,1)S(1)}, u32[]{:S(2)}, u32[]{:S(2)}) collective-permute-start(bf16[16,6400]{1,0:T(8,128)(2,1)S(1)} %get-tuple-element.112), channel_id=1, source_target_pairs={{0,32},{1,9},{2,34},{3,11},{4,36},{5,13},{6,38},{7,15},{8,40},{9,1... | collective-permute-start | bytes 614408 | tf_op jit(solution)/shard_map/ppermute | solution.py:45
  26.7 2.6 %collective-permute-start.10 = (bf16[16,6400]{1,0:T(8,128)(2,1)S(1)}, bf16[16,6400]{1,0:T(8,128)(2,1)S(1)}, u32[]{:S(2)}, u32[]{:S(2)}) collective-permute-start(bf16[16,6400]{1,0:T(8,128)(2,1)S(1)} %get-tuple-element.113), channel_id=1, source_target_pairs={{0,96},{1,25},{2,98},{3,27},{4,100},{5,29},{6,102},{7,31},{8,104},... | collective-permute-start | bytes 614408 | tf_op jit(solution)/shard_map/ppermute | solution.py:45
  29.3 0.0 collective-permute-done.7.refs_1_
  29.3 0.1 down_halve_kernel.1
  29.3 4.1 %collective-permute-start.12 = (bf16[32,1600]{1,0:T(8,128)(2,1)S(1)}, bf16[32,1600]{1,0:T(8,128)(2,1)S(1)}, u32[]{:S(2)}, u32[]{:S(2)}) collective-permute-start(bf16[32,1600]{1,0:T(8,128)(2,1)S(1)} %get-tuple-element.118), channel_id=1, source_target_pairs={{0,6},{6,0},{2,4},{4,2},{1,7},{7,1},{3,5},{5,3},{8,14},{14,8},{10,... | collective-permute-start | bytes 307208 | tf_op jit(solution)/shard_map/ppermute | solution.py:65
  33.6 0.7 %pair_sum_kernel.1 = (f32[4,3200]{1,0:T(4,128)S(1)}, bf16[4,3200]{1,0:T(4,128)(2,1)S(1)}, f32[16,6400]{1,0:T(8,128)S(1)}, f32[8,128]{1,0:T(8,128)S(1)}) custom-call(f32[16,6400]{1,0:T(8,128)S(1)} %get-tuple-element.111.refs_0_, bf16[16,6400]{1,0:T(8,128)(2,1)S(1)} %collective-permute-done.9.refs_1_, bf16[16,6400]{1,0:T(8,128)(2,1)S(1)} %collective-permute-done.10.refs_2_, ...), custom_call_target="tpu_custom_call" | custom-call | tf_op jit(solution)/shard_map/pair_sum_kernel/pallas_call | solution.py:97
  34.2 0.4 collective-permute-start.11
  34.7 1.5 %collective-permute-done.12.refs_1_ = bf16[32,1600]{1,0:T(8,128)(2,1)S(1)} collective-permute-done((bf16[32,1600]{1,0:T(8,128)(2,1)S(1)}, bf16[32,1600]{1,0:T(8,128)(2,1)S(1)}, u32[]{:S(2)}, u32[]{:S(2)}) %collective-permute-start.12) | collective-permute-done | bytes 102432 | tf_op jit(solution)/shard_map/ppermute | solution.py:65
  36.1 0.3 down_sum_kernel.1
  36.5 0.5 collective-permute-start.14
  37.0 1.2 %collective-permute-done.11.refs_1_ = bf16[4,3200]{1,0:T(4,128)(2,1)S(1)} collective-permute-done((bf16[4,3200]{1,0:T(4,128)(2,1)S(1)}, bf16[4,3200]{1,0:T(4,128)(2,1)S(1)}, u32[]{:S(2)}, u32[]{:S(2)}) %collective-permute-start.11) | collective-permute-done | bytes 25632 | tf_op jit(solution)/shard_map/ppermute | solution.py:60
  38.2 2.8 %collective-permute-start.13 = (bf16[4,3200]{1,0:T(4,128)(2,1)S(1)}, bf16[4,3200]{1,0:T(4,128)(2,1)S(1)}, u32[]{:S(2)}, u32[]{:S(2)}) collective-permute-start(bf16[4,3200]{1,0:T(4,128)(2,1)S(1)} %get-tuple-element.122), channel_id=1, source_target_pairs={{0,96},{1,25},{2,98},{3,27},{4,100},{5,29},{6,102},{7,31},{8,104},... | collective-permute-start | bytes 76808 | tf_op jit(solution)/shard_map/ppermute | solution.py:60
  41.0 4.1 %collective-permute-start.16 = (bf16[8,1600]{1,0:T(8,128)(2,1)S(1)}, bf16[8,1600]{1,0:T(8,128)(2,1)S(1)}, u32[]{:S(2)}, u32[]{:S(2)}) collective-permute-start(bf16[8,1600]{1,0:T(8,128)(2,1)S(1)} %get-tuple-element.132), channel_id=1, source_target_pairs={{0,6},{6,0},{2,4},{4,2},{1,7},{7,1},{3,5},{5,3},{8,14},{14,8},{10,... | collective-permute-start | bytes 76808 | tf_op jit(solution)/shard_map/ppermute | solution.py:65
  45.1 0.4 collective-permute-start.15
  45.5 1.4 %collective-permute-done.16.refs_1_ = bf16[8,1600]{1,0:T(8,128)(2,1)S(1)} collective-permute-done((bf16[8,1600]{1,0:T(8,128)(2,1)S(1)}, bf16[8,1600]{1,0:T(8,128)(2,1)S(1)}, u32[]{:S(2)}, u32[]{:S(2)}) %collective-permute-start.16) | collective-permute-done | bytes 25632 | tf_op jit(solution)/shard_map/ppermute | solution.py:65
  46.9 0.1 collective-permute-start.18
  47.0 1.2 %moment_kernel.1 = (f32[16,3200]{1,0:T(8,128)}, f32[16,3200]{1,0:T(8,128)}, f32[16,3200]{1,0:T(8,128)}, f32[16,3200]{1,0:T(8,128)}, f32[32,1600]{1,0:T(8,128)}, ...) custom-call(f32[16,6400]{1,0:T(8,128)S(1)} %get-tuple-element.129.refs_0_, f32[32,1600]{1,0:T(8,128)S(1)} %get-tuple-element.130.refs_1_, ...), custom_call_target="tpu_custom_call" | custom-call | tf_op jit(solution)/shard_map/moment_kernel/pallas_call | solution.py:97
  48.3 0.8 %collective-permute-done.15.refs_1_ = bf16[4,3200]{1,0:T(4,128)(2,1)S(1)} collective-permute-done((bf16[4,3200]{1,0:T(4,128)(2,1)S(1)}, bf16[4,3200]{1,0:T(4,128)(2,1)S(1)}, u32[]{:S(2)}, u32[]{:S(2)}) %collective-permute-start.15) | collective-permute-done | bytes 25632 | tf_op jit(solution)/shard_map/ppermute | solution.py:60
  49.1 1.8 %collective-permute-start.17 = (bf16[4,3200]{1,0:T(4,128)(2,1)S(1)}, bf16[4,3200]{1,0:T(4,128)(2,1)S(1)}, u32[]{:S(2)}, u32[]{:S(2)}) collective-permute-start(bf16[4,3200]{1,0:T(4,128)(2,1)S(1)} %get-tuple-element.137), channel_id=1, source_target_pairs={{0,24},{1,97},{2,26},{3,99},{4,28},{5,101},{6,30},{7,103},{8,16},{... | collective-permute-start | bytes 76808 | tf_op jit(solution)/shard_map/ppermute | solution.py:60
  50.9 1.8 %down_update_kernel.1 = (bf16[1600,640]{1,0:T(8,128)(2,1)}, f32[8,128]{1,0:T(8,128)S(1)}) custom-call(bf16[1600,640]{1,0:T(8,128)(2,1)S(1)} %bitcast.9, f32[8,1600]{1,0:T(8,128)S(1)} %get-tuple-element.138.refs_1_, bf16[8,1600]{1,0:T(8,128)(2,1)S(1)} %collective-permute-done.18.refs_2_, f32[8,128]{1,0:T(8,128)S(1)} %get-tuple-element.140.refs_3_), custom_call_target="tpu_custom_call" | custom-call | tf_op jit(solution)/shard_map/down_update_kernel/pallas_call | solution.py:97
  52.7 1.5 %collective-permute-done.17.refs_1_ = bf16[4,3200]{1,0:T(4,128)(2,1)S(1)} collective-permute-done((bf16[4,3200]{1,0:T(4,128)(2,1)S(1)}, bf16[4,3200]{1,0:T(4,128)(2,1)S(1)}, u32[]{:S(2)}, u32[]{:S(2)}) %collective-permute-start.17) | collective-permute-done | bytes 25632 | tf_op jit(solution)/shard_map/ppermute | solution.py:60
  54.2 2.9 %update_kernel.1 = (bf16[320,3200]{1,0:T(8,128)(2,1)}, bf16[320,3200]{1,0:T(8,128)(2,1)}, f32[8,128]{1,0:T(8,128)}) custom-call(bf16[320,3200]{1,0:T(8,128)(2,1)S(1)} %get-tuple-element.81.refs_1_.refs_0_, bf16[320,3200]{1,0:T(8,128)(2,1)S(1)} %get-tuple-element.82.refs_3_.refs_1_, f32[2,3200]{1,0:T(2,128)S(1)} %get-tuple-element.142.refs_2_, ...), custom_call_target="tpu_custom_call" | custom-call | tf_op jit(solution)/shard_map/update_kernel/pallas_call | solution.py:97
  (27 shorter events, 0.2 us)
Async XLA Ops:
  3.5 9.4 %collective-permute-start.2 = (bf16[32,6400]{1,0:T(8,128)(2,1)S(1)}, bf16[32,6400]{1,0:T(8,128)(2,1)S(1)}, u32[]{:S(2)}, u32[]{:S(2)}) collective-permute-start(bf16[32,6400]{1,0:T(8,128)(2,1)S(1)} %get-tuple-element.90), channel_id=1, source_target_pairs={{0,8},{1,33},{2,10},{3,35},{4,12},{5,37},{6,14},{7,39},{8,16},{9,4... | collective-permute-start | bytes 1228808 | tf_op jit(solution)/shard_map/ppermute | solution.py:45
  5.1 8.0 %collective-permute-start.3 = (bf16[32,6400]{1,0:T(8,128)(2,1)S(1)}, bf16[32,6400]{1,0:T(8,128)(2,1)S(1)}, u32[]{:S(2)}, u32[]{:S(2)}) collective-permute-start(bf16[32,6400]{1,0:T(8,128)(2,1)S(1)} %get-tuple-element.92), channel_id=1, source_target_pairs={{0,24},{1,97},{2,26},{3,99},{4,28},{5,101},{6,30},{7,103},{8,0},{9... | collective-permute-start | bytes 1228808 | tf_op jit(solution)/shard_map/ppermute | solution.py:45
  6.8 4.9 %copy-start = (bf16[640,1600]{0,1:T(8,128)(2,1)S(1)}, bf16[640,1600]{0,1:T(8,128)(2,1)}, u32[]{:S(2)}) copy-start(bf16[640,1600]{0,1:T(8,128)(2,1)} %param.14) | copy-start | bytes 6144004
  6.8 4.9 %copy-start.7 = (bf16[256,640]{1,0:T(8,128)(2,1)S(1)}, bf16[256,640]{1,0:T(8,128)(2,1)}, u32[]{:S(2)}) copy-start(bf16[256,640]{1,0:T(8,128)(2,1)} %refs_0_.1) | copy-start | bytes 983044
  8.4 9.2 %collective-permute-start = (bf16[32,6400]{1,0:T(8,128)(2,1)S(1)}, bf16[32,6400]{1,0:T(8,128)(2,1)S(1)}, u32[]{:S(2)}, u32[]{:S(2)}) collective-permute-start(bf16[32,6400]{1,0:T(8,128)(2,1)S(1)} %get-tuple-element.87), channel_id=1, source_target_pairs={{0,8},{1,33},{2,10},{3,35},{4,12},{5,37},{6,14},{7,39},{8,16},{9,4... | collective-permute-start | bytes 1228808 | tf_op jit(solution)/shard_map/ppermute | solution.py:45
  8.8 8.8 %collective-permute-start.1 = (bf16[32,6400]{1,0:T(8,128)(2,1)S(1)}, bf16[32,6400]{1,0:T(8,128)(2,1)S(1)}, u32[]{:S(2)}, u32[]{:S(2)}) collective-permute-start(bf16[32,6400]{1,0:T(8,128)(2,1)S(1)} %get-tuple-element.88), channel_id=1, source_target_pairs={{0,24},{1,97},{2,26},{3,99},{4,28},{5,101},{6,30},{7,103},{8,0},{9... | collective-permute-start | bytes 1228808 | tf_op jit(solution)/shard_map/ppermute | solution.py:45
  12.8 5.0 %collective-permute-start.5 = (bf16[128,1600]{1,0:T(8,128)(2,1)S(1)}, bf16[128,1600]{1,0:T(8,128)(2,1)S(1)}, u32[]{:S(2)}, u32[]{:S(2)}) collective-permute-start(bf16[128,1600]{1,0:T(8,128)(2,1)S(1)} %get-tuple-element.99), channel_id=1, source_target_pairs={{0,1},{1,0},{2,3},{3,2},{4,5},{5,4},{6,7},{7,6},{8,9},{9,8},{10,11... | collective-permute-start | bytes 1228808 | tf_op jit(solution)/shard_map/ppermute | solution.py:69
  13.3 9.2 %collective-permute-start.4 = (bf16[32,6400]{1,0:T(8,128)(2,1)S(1)}, bf16[32,6400]{1,0:T(8,128)(2,1)S(1)}, u32[]{:S(2)}, u32[]{:S(2)}) collective-permute-start(bf16[32,6400]{1,0:T(8,128)(2,1)S(1)} %get-tuple-element.97), channel_id=1, source_target_pairs={{0,8},{1,33},{2,10},{3,35},{4,12},{5,37},{6,14},{7,39},{8,16},{9,4... | collective-permute-start | bytes 1228808 | tf_op jit(solution)/shard_map/ppermute | solution.py:45
  14.8 11.1 %collective-permute-start.8 = (bf16[32,6400]{1,0:T(8,128)(2,1)S(1)}, bf16[32,6400]{1,0:T(8,128)(2,1)S(1)}, u32[]{:S(2)}, u32[]{:S(2)}) collective-permute-start(bf16[32,6400]{1,0:T(8,128)(2,1)S(1)} %get-tuple-element.107), channel_id=1, source_target_pairs={{0,24},{1,97},{2,26},{3,99},{4,28},{5,101},{6,30},{7,103},{8,0},{9... | collective-permute-start | bytes 1228808 | tf_op jit(solution)/shard_map/ppermute | solution.py:45
  17.9 15.6 %copy-start.3 = (f32[16,3200]{1,0:T(8,128)S(1)}, f32[16,3200]{1,0:T(8,128)}, u32[]{:S(2)}) copy-start(f32[16,3200]{1,0:T(8,128)} %refs_2_.3) | copy-start | bytes 614404
  18.0 15.6 %copy-start.4 = (f32[16,3200]{1,0:T(8,128)S(1)}, f32[16,3200]{1,0:T(8,128)}, u32[]{:S(2)}) copy-start(f32[16,3200]{1,0:T(8,128)} %refs_3_.5) | copy-start | bytes 614404
  18.0 15.6 %copy-start.5 = (f32[16,3200]{1,0:T(8,128)S(1)}, f32[16,3200]{1,0:T(8,128)}, u32[]{:S(2)}) copy-start(f32[16,3200]{1,0:T(8,128)} %refs_4_.3) | copy-start | bytes 614404
  18.0 15.6 %copy-start.6 = (f32[16,3200]{1,0:T(8,128)S(1)}, f32[16,3200]{1,0:T(8,128)}, u32[]{:S(2)}) copy-start(f32[16,3200]{1,0:T(8,128)} %refs_5_.3) | copy-start | bytes 614404
  18.0 11.3 %collective-permute-start.7 = (bf16[64,1600]{1,0:T(8,128)(2,1)S(1)}, bf16[64,1600]{1,0:T(8,128)(2,1)S(1)}, u32[]{:S(2)}, u32[]{:S(2)}) collective-permute-start(bf16[64,1600]{1,0:T(8,128)(2,1)S(1)} %get-tuple-element.105), channel_id=1, source_target_pairs={{0,2},{2,0},{4,6},{6,4},{1,3},{3,1},{5,7},{7,5},{8,10},{10,8},{12,... | collective-permute-start | bytes 614408 | tf_op jit(solution)/shard_map/ppermute | solution.py:65
  22.6 10.9 %collective-permute-start.6 = (bf16[16,6400]{1,0:T(8,128)(2,1)S(1)}, bf16[16,6400]{1,0:T(8,128)(2,1)S(1)}, u32[]{:S(2)}, u32[]{:S(2)}) collective-permute-start(bf16[16,6400]{1,0:T(8,128)(2,1)S(1)} %get-tuple-element.103), channel_id=1, source_target_pairs={{0,64},{1,17},{2,66},{3,19},{4,68},{5,21},{6,70},{7,23},{8,72},{9,... | collective-permute-start | bytes 614408 | tf_op jit(solution)/shard_map/ppermute | solution.py:45
  25.9 10.3 %copy-start.1 = (f32[32,1600]{1,0:T(8,128)S(1)}, f32[32,1600]{1,0:T(8,128)}, u32[]{:S(2)}) copy-start(f32[32,1600]{1,0:T(8,128)} %refs_6_.3) | copy-start | bytes 614404
  25.9 10.3 %copy-start.2 = (f32[32,1600]{1,0:T(8,128)S(1)}, f32[32,1600]{1,0:T(8,128)}, u32[]{:S(2)}) copy-start(f32[32,1600]{1,0:T(8,128)} %refs_7_.1) | copy-start | bytes 614404
  26.0 7.5 %collective-permute-start.9 = (bf16[16,6400]{1,0:T(8,128)(2,1)S(1)}, bf16[16,6400]{1,0:T(8,128)(2,1)S(1)}, u32[]{:S(2)}, u32[]{:S(2)}) collective-permute-start(bf16[16,6400]{1,0:T(8,128)(2,1)S(1)} %get-tuple-element.112), channel_id=1, source_target_pairs={{0,32},{1,9},{2,34},{3,11},{4,36},{5,13},{6,38},{7,15},{8,40},{9,1... | collective-permute-start | bytes 614408 | tf_op jit(solution)/shard_map/ppermute | solution.py:45
  26.7 6.8 %collective-permute-start.10 = (bf16[16,6400]{1,0:T(8,128)(2,1)S(1)}, bf16[16,6400]{1,0:T(8,128)(2,1)S(1)}, u32[]{:S(2)}, u32[]{:S(2)}) collective-permute-start(bf16[16,6400]{1,0:T(8,128)(2,1)S(1)} %get-tuple-element.113), channel_id=1, source_target_pairs={{0,96},{1,25},{2,98},{3,27},{4,100},{5,29},{6,102},{7,31},{8,104},... | collective-permute-start | bytes 614408 | tf_op jit(solution)/shard_map/ppermute | solution.py:45
  29.3 6.8 %collective-permute-start.12 = (bf16[32,1600]{1,0:T(8,128)(2,1)S(1)}, bf16[32,1600]{1,0:T(8,128)(2,1)S(1)}, u32[]{:S(2)}, u32[]{:S(2)}) collective-permute-start(bf16[32,1600]{1,0:T(8,128)(2,1)S(1)} %get-tuple-element.118), channel_id=1, source_target_pairs={{0,6},{6,0},{2,4},{4,2},{1,7},{7,1},{3,5},{5,3},{8,14},{14,8},{10,... | collective-permute-start | bytes 307208 | tf_op jit(solution)/shard_map/ppermute | solution.py:65
  34.2 3.9 %collective-permute-start.11 = (bf16[4,3200]{1,0:T(4,128)(2,1)S(1)}, bf16[4,3200]{1,0:T(4,128)(2,1)S(1)}, u32[]{:S(2)}, u32[]{:S(2)}) collective-permute-start(bf16[4,3200]{1,0:T(4,128)(2,1)S(1)} %get-tuple-element.116), channel_id=1, source_target_pairs={{0,32},{1,9},{2,34},{3,11},{4,36},{5,13},{6,38},{7,15},{8,40},{9,1... | collective-permute-start | bytes 76808 | tf_op jit(solution)/shard_map/ppermute | solution.py:60
  36.5 4.5 %collective-permute-start.14 = (bf16[8,1600]{1,0:T(8,128)(2,1)S(1)}, bf16[8,1600]{1,0:T(8,128)(2,1)S(1)}, u32[]{:S(2)}, u32[]{:S(2)}) collective-permute-start(bf16[8,1600]{1,0:T(8,128)(2,1)S(1)} %get-tuple-element.124), channel_id=1, source_target_pairs={{0,2},{2,0},{4,6},{6,4},{1,3},{3,1},{5,7},{7,5},{8,10},{10,8},{12,... | collective-permute-start | bytes 76808 | tf_op jit(solution)/shard_map/ppermute | solution.py:65
  38.2 6.9 %collective-permute-start.13 = (bf16[4,3200]{1,0:T(4,128)(2,1)S(1)}, bf16[4,3200]{1,0:T(4,128)(2,1)S(1)}, u32[]{:S(2)}, u32[]{:S(2)}) collective-permute-start(bf16[4,3200]{1,0:T(4,128)(2,1)S(1)} %get-tuple-element.122), channel_id=1, source_target_pairs={{0,96},{1,25},{2,98},{3,27},{4,100},{5,29},{6,102},{7,31},{8,104},... | collective-permute-start | bytes 76808 | tf_op jit(solution)/shard_map/ppermute | solution.py:60
  41.0 5.9 %collective-permute-start.16 = (bf16[8,1600]{1,0:T(8,128)(2,1)S(1)}, bf16[8,1600]{1,0:T(8,128)(2,1)S(1)}, u32[]{:S(2)}, u32[]{:S(2)}) collective-permute-start(bf16[8,1600]{1,0:T(8,128)(2,1)S(1)} %get-tuple-element.132), channel_id=1, source_target_pairs={{0,6},{6,0},{2,4},{4,2},{1,7},{7,1},{3,5},{5,3},{8,14},{14,8},{10,... | collective-permute-start | bytes 76808 | tf_op jit(solution)/shard_map/ppermute | solution.py:65
  45.1 3.9 %collective-permute-start.15 = (bf16[4,3200]{1,0:T(4,128)(2,1)S(1)}, bf16[4,3200]{1,0:T(4,128)(2,1)S(1)}, u32[]{:S(2)}, u32[]{:S(2)}) collective-permute-start(bf16[4,3200]{1,0:T(4,128)(2,1)S(1)} %get-tuple-element.128), channel_id=1, source_target_pairs={{0,8},{1,33},{2,10},{3,35},{4,12},{5,37},{6,14},{7,39},{8,0},{9,41... | collective-permute-start | bytes 76808 | tf_op jit(solution)/shard_map/ppermute | solution.py:60
  46.9 3.9 %collective-permute-start.18 = (bf16[8,1600]{1,0:T(8,128)(2,1)S(1)}, bf16[8,1600]{1,0:T(8,128)(2,1)S(1)}, u32[]{:S(2)}, u32[]{:S(2)}) collective-permute-start(bf16[8,1600]{1,0:T(8,128)(2,1)S(1)} %get-tuple-element.139), channel_id=1, source_target_pairs={{0,1},{1,0},{2,3},{3,2},{4,5},{5,4},{6,7},{7,6},{8,9},{9,8},{10,11... | collective-permute-start | bytes 76808 | tf_op jit(solution)/shard_map/ppermute | solution.py:69
  49.1 5.1 %collective-permute-start.17 = (bf16[4,3200]{1,0:T(4,128)(2,1)S(1)}, bf16[4,3200]{1,0:T(4,128)(2,1)S(1)}, u32[]{:S(2)}, u32[]{:S(2)}) collective-permute-start(bf16[4,3200]{1,0:T(4,128)(2,1)S(1)} %get-tuple-element.137), channel_id=1, source_target_pairs={{0,24},{1,97},{2,26},{3,99},{4,28},{5,101},{6,30},{7,103},{8,16},{... | collective-permute-start | bytes 76808 | tf_op jit(solution)/shard_map/ppermute | solution.py:60

commit v5 on v4

--- a/solution.py
+++ b/solution.py
@@ -77,7 +77,7 @@
     def __init__(self):
         self.last = None
 
-    def __call__(self, body, outs, *operands, in_specs=None, out_specs=None, scratch=(), limit=8):
+    def __call__(self, body, outs, *operands, in_specs=None, out_specs=None, scratch=(), limit=8, cost=0, last=False):
         specs = [VMEM] * len(operands) if in_specs is None else list(in_specs)
         count, made = len(operands), len(outs)
         if self.last is not None:
@@ -89,21 +89,25 @@
         ]
 
         def kernel(*refs):
-            refs, token = refs[: len(operands)], refs[len(operands) :]
-            token, rest = token[made], token[:made] + token[made + 1 :]
-            token[...] = jnp.zeros_like(token)
-            body(*refs[:count], *rest)
-
-        *result, self.last = pl.pallas_call(
+            given, rest = refs[:count], refs[len(operands) :]
+            if not last:
+                token, rest = rest[made], rest[:made] + rest[made + 1 :]
+                token[...] = jnp.zeros_like(token)
+            body(*given, *rest)
+
+        token_out, token_spec = ([], []) if last else ([pltpu.VMEM((8, 128), F32)], [VMEM])
+        result = pl.pallas_call(
             kernel,
             name=body.__name__,
-            out_shape=[*outs, pltpu.VMEM((8, 128), F32)],
+            out_shape=[*outs, *token_out],
             in_specs=specs,
-            out_specs=[*([VMEM] * made if out_specs is None else out_specs), VMEM],
+            out_specs=[*([VMEM] * made if out_specs is None else out_specs), *token_spec],
             scratch_shapes=scratch,
             compiler_params=pltpu.CompilerParams(vmem_limit_bytes=limit * 2**20),
-            cost_estimate=pl.CostEstimate(flops=0, bytes_accessed=0, transcendentals=0),
+            cost_estimate=pl.CostEstimate(flops=cost, bytes_accessed=0, transcendentals=0),
         )(*operands)
+        if not last:
+            *result, self.last = result
         return result
 
 
@@ -214,10 +218,8 @@
 
 def channel_sums(projected, first, second):
     first_value, second_value = moments(projected, first, second)
-    corrected = (
-        first_value
-        / (1.0 - beta_first**STEP)
-        / (jnp.sqrt(second_value / (1.0 - beta_second**STEP)) + adam_epsilon)
+    corrected = (first_value * (1.0 / (1.0 - beta_first**STEP))) / (
+        jnp.sqrt(second_value * (1.0 / (1.0 - beta_second**STEP))) + adam_epsilon
     )
     return jnp.sum(corrected * corrected, 0, keepdims=True), jnp.sum(projected * projected, 0, keepdims=True)
 
@@ -237,10 +239,12 @@
 
 
 def down_sum_kernel(own, other, first, second, sums, sent, total):
-    projected = wide(own[...], other[...])
-    total[...] = projected
+    projected = wide(own[...], other[:64])
+    total[...] = projected[:32]
+    near = channel_sums(projected[:32], first, second)
+    far = channel_sums(projected[32:], other[64:96].astype(F32), other[96:].astype(F32))
     sums[...] = jnp.zeros_like(sums)
-    sums[0:1], sums[1:2] = channel_sums(projected, first, second)
+    sums[0:1], sums[1:2] = near[0] + far[0], near[1] + far[1]
     sent[...] = sums[...].astype(BF16)
 
 
@@ -258,16 +262,12 @@
     return update_scale * (jnp.sqrt(corrected_sq) / (jnp.sqrt(projected_sq) + norm_epsilon))
 
 
-def scale_kernel(own, other, scale):
+def update_kernel(gate, up, own, other, gate_out, up_out, gate_made, up_made, sems):
     sums = wide(own[...], other[...])
-    scale[0:1] = scale_of(sums[0:1], sums[1:2])
-    scale[1:2] = scale_of(sums[2:3], sums[3:4])
-
-
-def update_kernel(gate, up, scale, gate_out, up_out, gate_made, up_made, sems):
     copies = []
     for index, (grad, made, out) in enumerate(((gate, gate_made, gate_out), (up, up_made, up_out))):
-        made[...] = (grad[...].astype(F32) * scale[index : index + 1]).astype(BF16)
+        scale = scale_of(sums[2 * index : 2 * index + 1], sums[2 * index + 1 : 2 * index + 2])
+        made[...] = (grad[...].astype(F32) * scale).astype(BF16)
         copies.append(pltpu.make_async_copy(made, out, sems.at[index]))
         copies[-1].start()
     for copy in copies:
@@ -290,10 +290,13 @@
     send[...] = total[64:].astype(BF16)
 
 
-def down_halve_kernel(own, other, keep, send):
+def down_halve_kernel(own, other, first, second, keep, send):
     total = wide(own[...], other[...])
-    keep[...] = total[:32]
-    send[...] = total[32:].astype(BF16)
+    keep[...] = total
+    send[:32] = total[32:].astype(BF16)
+    send[32:64] = total[:32].astype(BF16)
+    send[64:96] = first[...].astype(BF16)
+    send[96:] = second[...].astype(BF16)
 
 
 def down_update_kernel(grad, own, other, out, scale):
@@ -357,24 +360,25 @@
     above, below = run(far_kernel, (piece, piece), high, high_above)
     above, below = ring_send(above, 1, 1), ring_send(below, 3, 1)
     own_down, other_down = run(
-        down_halve_kernel, (pltpu.VMEM((32, 1600), F32), pltpu.VMEM((32, 1600), BF16)), own_down, other_down
+        down_halve_kernel,
+        (pltpu.VMEM((64, 1600), F32), pltpu.VMEM((128, 1600), BF16)),
+        own_down, other_down, first_down, second_down,
     )
     other_down = z_swap(other_down, True)
 
     states = (first_gate, second_gate, first_up, second_up)
     (own,) = run(add_kernel, (pltpu.VMEM((16, 6400), F32),), own, opposite)
     sums, sent, total = run(
-        pair_sum_kernel, (pair_row, sent_pair, pltpu.VMEM((16, 6400), F32)), own, above, below, *states
+        pair_sum_kernel, (pair_row, sent_pair, pltpu.VMEM((16, 6400), F32)), own, above, below, *states,
+        cost=8 * 10**9,
     )
     other = ring_swap(sent, False, 1)
+    sums, sent = run(sum_kernel, (pair_row, sent_pair), sums, other)
+    other = ring_swap(sent, True, 1)
     sums_d, sent_d, total_d = run(
         down_sum_kernel, (row, sent_row, pltpu.VMEM((32, 1600), F32)), own_down, other_down, first_down, second_down
     )
     other_d = z_swap(sent_d, False)
-    sums, sent = run(sum_kernel, (pair_row, sent_pair), sums, other)
-    other = ring_swap(sent, True, 1)
-    sums_d, sent_d = run(sum_kernel, (row, sent_row), sums_d, other_d)
-    other_d = z_swap(sent_d, True)
     sums, sent = run(sum_kernel, (pair_row, sent_pair), sums, other)
     other = ring_swap(sent, False, 0)
     sums_d, sent_d = run(sum_kernel, (row, sent_row), sums_d, other_d)
@@ -388,13 +392,13 @@
         down, sums_d, other_d,
         scratch=(pltpu.VMEM((1, 1664), F32),),
     )
-    (scale,) = run(scale_kernel, (pltpu.VMEM((2, 3200), F32),), sums, other)
     update_gate, update_up = run(
         update_kernel,
         (whole, whole),
-        gate, up, scale,
+        gate, up, sums, other,
         out_specs=(HBM, HBM),
         scratch=(held, held, pltpu.SemaphoreType.DMA((2,))),
+        last=True,
     )
     return (
         update_gate.T,

time: 57.3 us -> 55.1 us (0.962)
  starting transfers between devices: 32.9 us -> 30.2 us
  waiting for transfers between devices: 10 us -> 10.9 us
    ppermute x4 -> x3, starting transfers between devices: 10.8 us -> 8.18 us  [z_swap(): return lax.ppermute(value, 'z', pairs)]
    ppermute x4, waiting for transfers between devices: 3.43 us -> 5.67 us  [ring_swap(): return lax.ppermute(value, AXES, pairs)]
    ppermute x4 -> x3, waiting for transfers between devices: 2.92 us -> 1.56 us  [z_swap(): return lax.ppermute(value, 'z', pairs)]
    pallas_call x21 -> x19, Pallas kernels: 13.4 us -> 13.1 us  [__call__(): pl.pallas_call(kernel, name=body.__name__, out_shape=[*outs, *token_out],...]
  transfers between devices with their start and end apart: 19 -> 18, of which waited for: 8 -> 7; matrix products, arithmetic and copies ran while one was open for 0% -> 0% of each run, Pallas kernels for 13% -> 14%
where the time goes in v5:
time: 55.1 us; the launch traced here: 55 us
  starting transfers between devices  30.2 us (55%)
  Pallas kernels  13.1 us (24%)
  waiting for transfers between devices  10.9 us (20%)
  between operations  0.83 us (2%)
    ppermute x9, starting transfers between devices, ring_send(): return lax.ppermute(value, AXES, ring_pairs(shift, stage))  16.5 us
    pallas_call x19, Pallas kernels, __call__(): pl.pallas_call(kernel, name=body.__name__, out_shape=[*outs, *token_out],...  13.1 us
    ppermute x3, starting transfers between devices, z_swap(): return lax.ppermute(value, 'z', pairs)  8.18 us
    ppermute x4, waiting for transfers between devices, ring_swap(): return lax.ppermute(value, AXES, pairs)  5.67 us
    ppermute x4, starting transfers between devices, ring_swap(): return lax.ppermute(value, AXES, pairs)  5.32 us
    ppermute x9, waiting for transfers between devices, ring_send(): return lax.ppermute(value, AXES, ring_pairs(shift, stage))  3.67 us
    ppermute x3, waiting for transfers between devices, z_swap(): return lax.ppermute(value, 'z', pairs)  1.56 us
  transfers between devices with their start and end apart: 18, of which 7 were waited for; matrix products, arithmetic and copies ran while one was open for 0% of the time, Pallas kernels for 14%

profile of v5, /device:TPU:0, one launch (start us, length us, event | category | flops | bytes accessed | tf_op | source)
XLA Modules:
  0.0 55.0 jit_solution(4795232391554054658)
XLA Ops:
  0.6 2.8 %first_kernel.1 = (bf16[32,6400]{1,0:T(8,128)(2,1)S(1)}, bf16[32,6400]{1,0:T(8,128)(2,1)S(1)}, bf16[192,320]{1,0:T(8,128)(2,1)S(1)}, bf16[192,320]{1,0:T(8,128)(...) custom-call(bf16[320,256]{1,0:T(8,128)(2,1)} %bitcast.12, ...), custom_call_target="tpu_custom_call" | custom-call | tf_op jit(solution)/shard_map/first_kernel/pallas_call | solution.py:99
  3.5 1.6 %collective-permute-start.2 = (bf16[32,6400]{1,0:T(8,128)(2,1)S(1)}, bf16[32,6400]{1,0:T(8,128)(2,1)S(1)}, u32[]{:S(2)}, u32[]{:S(2)}) collective-permute-start(bf16[32,6400]{1,0:T(8,128)(2,1)S(1)} %get-tuple-element.85), channel_id=1, source_target_pairs={{0,8},{1,33},{2,10},{3,35},{4,12},{5,37},{6,14},{7,39},{8,16},{9,4... | collective-permute-start | bytes 1228808 | tf_op jit(solution)/shard_map/ppermute | solution.py:45
  5.1 1.7 %collective-permute-start.3 = (bf16[32,6400]{1,0:T(8,128)(2,1)S(1)}, bf16[32,6400]{1,0:T(8,128)(2,1)S(1)}, u32[]{:S(2)}, u32[]{:S(2)}) collective-permute-start(bf16[32,6400]{1,0:T(8,128)(2,1)S(1)} %get-tuple-element.87), channel_id=1, source_target_pairs={{0,24},{1,97},{2,26},{3,99},{4,28},{5,101},{6,30},{7,103},{8,0},{9... | collective-permute-start | bytes 1228808 | tf_op jit(solution)/shard_map/ppermute | solution.py:45
  6.8 1.6 %rest_kernel.1 = (bf16[32,6400]{1,0:T(8,128)(2,1)S(1)}, bf16[32,6400]{1,0:T(8,128)(2,1)S(1)}, bf16[32,6400]{1,0:T(8,128)(2,1)S(1)}, bf16[32,6400]{1,0:T(8,128)(2...) custom-call(bf16[192,320]{1,0:T(8,128)(2,1)S(1)} %get-tuple-element.78.refs_0_, ...), custom_call_target="tpu_custom_call" | custom-call | tf_op jit(solution)/shard_map/rest_kernel/pallas_call | solution.py:99
  8.4 0.4 collective-permute-start
  8.8 2.9 %collective-permute-start.1 = (bf16[32,6400]{1,0:T(8,128)(2,1)S(1)}, bf16[32,6400]{1,0:T(8,128)(2,1)S(1)}, u32[]{:S(2)}, u32[]{:S(2)}) collective-permute-start(bf16[32,6400]{1,0:T(8,128)(2,1)S(1)} %get-tuple-element.83), channel_id=1, source_target_pairs={{0,24},{1,97},{2,26},{3,99},{4,28},{5,101},{6,30},{7,103},{8,0},{9... | collective-permute-start | bytes 1228808 | tf_op jit(solution)/shard_map/ppermute | solution.py:45
  11.7 1.1 %down_kernel.1 = (bf16[128,1600]{1,0:T(8,128)(2,1)S(1)}, bf16[128,1600]{1,0:T(8,128)(2,1)S(1)}, f32[8,128]{1,0:T(8,128)S(1)}) custom-call(bf16[256,640]{1,0:T(8,128)(2,1)S(1)} %copy-done.3, bf16[1600,640]{1,0:T(8,128)(2,1)S(1)} %bitcast.8, f32[8,128]{1,0:T(8,128)S(1)} %get-tuple-element.88.refs_2_), custom_call_target="tpu_custom_call" | custom-call | tf_op jit(solution)/shard_map/down_kernel/pallas_call | solution.py:99
  12.8 0.1 collective-permute-start.5
  12.9 0.0 collective-permute-done.2.refs_1_
  12.9 0.2 collective-permute-done.3.refs_3_
  13.1 0.2 pass_kernel.1
  13.3 1.6 %collective-permute-start.4 = (bf16[32,6400]{1,0:T(8,128)(2,1)S(1)}, bf16[32,6400]{1,0:T(8,128)(2,1)S(1)}, u32[]{:S(2)}, u32[]{:S(2)}) collective-permute-start(bf16[32,6400]{1,0:T(8,128)(2,1)S(1)} %get-tuple-element.92), channel_id=1, source_target_pairs={{0,8},{1,33},{2,10},{3,35},{4,12},{5,37},{6,14},{7,39},{8,16},{9,4... | collective-permute-start | bytes 1228808 | tf_op jit(solution)/shard_map/ppermute | solution.py:45
  14.8 1.7 %collective-permute-start.8 = (bf16[32,6400]{1,0:T(8,128)(2,1)S(1)}, bf16[32,6400]{1,0:T(8,128)(2,1)S(1)}, u32[]{:S(2)}, u32[]{:S(2)}) collective-permute-start(bf16[32,6400]{1,0:T(8,128)(2,1)S(1)} %get-tuple-element.102), channel_id=1, source_target_pairs={{0,24},{1,97},{2,26},{3,99},{4,28},{5,101},{6,30},{7,103},{8,0},{9... | collective-permute-start | bytes 1228808 | tf_op jit(solution)/shard_map/ppermute | solution.py:45
  16.6 1.0 %collective-permute-done.refs_1_ = bf16[32,6400]{1,0:T(8,128)(2,1)S(1)} collective-permute-done((bf16[32,6400]{1,0:T(8,128)(2,1)S(1)}, bf16[32,6400]{1,0:T(8,128)(2,1)S(1)}, u32[]{:S(2)}, u32[]{:S(2)}) %collective-permute-start) | collective-permute-done | bytes 409632 | tf_op jit(solution)/shard_map/ppermute | solution.py:45
  17.6 0.0 collective-permute-done.1.refs_2_
  17.6 0.2 collect_kernel.1
  17.8 0.0 copy-start.1
  17.8 0.0 copy-start.2
  17.9 0.0 collective-permute-done.5.refs_1_
  17.9 0.1 down_split_kernel.1
  18.0 2.1 %collective-permute-start.7 = (bf16[64,1600]{1,0:T(8,128)(2,1)S(1)}, bf16[64,1600]{1,0:T(8,128)(2,1)S(1)}, u32[]{:S(2)}, u32[]{:S(2)}) collective-permute-start(bf16[64,1600]{1,0:T(8,128)(2,1)S(1)} %get-tuple-element.100), channel_id=1, source_target_pairs={{0,2},{2,0},{4,6},{6,4},{1,3},{3,1},{5,7},{7,5},{8,10},{10,8},{12,... | collective-permute-start | bytes 614408 | tf_op jit(solution)/shard_map/ppermute | solution.py:65
  20.0 2.4 %collective-permute-done.4.refs_1_ = bf16[32,6400]{1,0:T(8,128)(2,1)S(1)} collective-permute-done((bf16[32,6400]{1,0:T(8,128)(2,1)S(1)}, bf16[32,6400]{1,0:T(8,128)(2,1)S(1)}, u32[]{:S(2)}, u32[]{:S(2)}) %collective-permute-start.4) | collective-permute-done | bytes 409632 | tf_op jit(solution)/shard_map/ppermute | solution.py:45
  22.5 0.1 near_kernel.1
  22.6 3.3 %collective-permute-start.6 = (bf16[16,6400]{1,0:T(8,128)(2,1)S(1)}, bf16[16,6400]{1,0:T(8,128)(2,1)S(1)}, u32[]{:S(2)}, u32[]{:S(2)}) collective-permute-start(bf16[16,6400]{1,0:T(8,128)(2,1)S(1)} %get-tuple-element.98), channel_id=1, source_target_pairs={{0,64},{1,17},{2,66},{3,19},{4,68},{5,21},{6,70},{7,23},{8,72},{9,... | collective-permute-start | bytes 614408 | tf_op jit(solution)/shard_map/ppermute | solution.py:45
  25.9 0.0 collective-permute-done.8.refs_1_
  25.9 0.1 far_kernel.1
  25.9 0.7 %collective-permute-start.9 = (bf16[16,6400]{1,0:T(8,128)(2,1)S(1)}, bf16[16,6400]{1,0:T(8,128)(2,1)S(1)}, u32[]{:S(2)}, u32[]{:S(2)}) collective-permute-start(bf16[16,6400]{1,0:T(8,128)(2,1)S(1)} %get-tuple-element.107), channel_id=1, source_target_pairs={{0,32},{1,9},{2,34},{3,11},{4,36},{5,13},{6,38},{7,15},{8,40},{9,1... | collective-permute-start | bytes 614408 | tf_op jit(solution)/shard_map/ppermute | solution.py:45
  26.7 2.6 %collective-permute-start.10 = (bf16[16,6400]{1,0:T(8,128)(2,1)S(1)}, bf16[16,6400]{1,0:T(8,128)(2,1)S(1)}, u32[]{:S(2)}, u32[]{:S(2)}) collective-permute-start(bf16[16,6400]{1,0:T(8,128)(2,1)S(1)} %get-tuple-element.108), channel_id=1, source_target_pairs={{0,96},{1,25},{2,98},{3,27},{4,100},{5,29},{6,102},{7,31},{8,104},... | collective-permute-start | bytes 614408 | tf_op jit(solution)/shard_map/ppermute | solution.py:45
  29.2 0.0 collective-permute-done.7.refs_1_
  29.3 0.1 down_halve_kernel.1
  29.4 4.1 %collective-permute-start.13 = (bf16[128,1600]{1,0:T(8,128)(2,1)S(1)}, bf16[128,1600]{1,0:T(8,128)(2,1)S(1)}, u32[]{:S(2)}, u32[]{:S(2)}) collective-permute-start(bf16[128,1600]{1,0:T(8,128)(2,1)S(1)} %get-tuple-element.116), channel_id=1, source_target_pairs={{0,6},{6,0},{2,4},{4,2},{1,7},{7,1},{3,5},{5,3},{8,14},{14,8},{10,... | collective-permute-start | bytes 1228808 | tf_op jit(solution)/shard_map/ppermute | solution.py:65
  33.5 0.0 collective-permute-done.10.refs_2_
  33.6 0.7 %pair_sum_kernel.1 = (f32[4,3200]{1,0:T(4,128)S(1)}, bf16[4,3200]{1,0:T(4,128)(2,1)S(1)}, f32[16,6400]{1,0:T(8,128)S(1)}, f32[8,128]{1,0:T(8,128)S(1)}) custom-call(f32[16,6400]{1,0:T(8,128)S(1)} %get-tuple-element.106.refs_0_, bf16[16,6400]{1,0:T(8,128)(2,1)S(1)} %collective-permute-done.9.refs_1_, bf16[16,6400]{1,0:T(8,128)(2,1)S(1)} %collective-permute-done.10.refs_2_, ...), custom_call_target="tpu_custom_call" | custom-call | flops 8000000000 | tf_op jit(solution)/shard_map/pair_sum_kernel/pallas_call | solution.py:99
  34.3 0.4 collective-permute-start.11
  34.7 3.5 %collective-permute-done.11.refs_1_ = bf16[4,3200]{1,0:T(4,128)(2,1)S(1)} collective-permute-done((bf16[4,3200]{1,0:T(4,128)(2,1)S(1)}, bf16[4,3200]{1,0:T(4,128)(2,1)S(1)}, u32[]{:S(2)}, u32[]{:S(2)}) %collective-permute-start.11) | collective-permute-done | bytes 25632 | tf_op jit(solution)/shard_map/ppermute | solution.py:60
  38.2 2.7 %collective-permute-start.12 = (bf16[4,3200]{1,0:T(4,128)(2,1)S(1)}, bf16[4,3200]{1,0:T(4,128)(2,1)S(1)}, u32[]{:S(2)}, u32[]{:S(2)}) collective-permute-start(bf16[4,3200]{1,0:T(4,128)(2,1)S(1)} %get-tuple-element.114), channel_id=1, source_target_pairs={{0,96},{1,25},{2,98},{3,27},{4,100},{5,29},{6,102},{7,31},{8,104},... | collective-permute-start | bytes 76808 | tf_op jit(solution)/shard_map/ppermute | solution.py:60
  41.0 0.6 %down_sum_kernel.1 = (f32[8,1600]{1,0:T(8,128)S(1)}, bf16[8,1600]{1,0:T(8,128)(2,1)S(1)}, f32[32,1600]{1,0:T(8,128)S(1)}, f32[8,128]{1,0:T(8,128)S(1)}) custom-call(f32[64,1600]{1,0:T(8,128)S(1)} %get-tuple-element.115.refs_0_, bf16[128,1600]{1,0:T(8,128)(2,1)S(1)} %collective-permute-done.13.refs_1_, f32[32,1600]{1,0:T(8,128)S(1)} %copy-done.1, ...), custom_call_target="tpu_custom_call" | custom-call | tf_op jit(solution)/shard_map/down_sum_kernel/pallas_call | solution.py:99
  41.6 2.0 %collective-permute-start.15 = (bf16[8,1600]{1,0:T(8,128)(2,1)S(1)}, bf16[8,1600]{1,0:T(8,128)(2,1)S(1)}, u32[]{:S(2)}, u32[]{:S(2)}) collective-permute-start(bf16[8,1600]{1,0:T(8,128)(2,1)S(1)} %get-tuple-element.124), channel_id=1, source_target_pairs={{0,2},{2,0},{4,6},{6,4},{1,3},{3,1},{5,7},{7,5},{8,10},{10,8},{12,... | collective-permute-start | bytes 76808 | tf_op jit(solution)/shard_map/ppermute | solution.py:65
  43.6 0.4 collective-permute-start.14
  43.9 1.6 %collective-permute-done.15.refs_1_ = bf16[8,1600]{1,0:T(8,128)(2,1)S(1)} collective-permute-done((bf16[8,1600]{1,0:T(8,128)(2,1)S(1)}, bf16[8,1600]{1,0:T(8,128)(2,1)S(1)}, u32[]{:S(2)}, u32[]{:S(2)}) %collective-permute-start.15) | collective-permute-done | bytes 25632 | tf_op jit(solution)/shard_map/ppermute | solution.py:65
  45.5 0.1 collective-permute-start.17
  45.6 1.2 %moment_kernel.1 = (f32[16,3200]{1,0:T(8,128)}, f32[16,3200]{1,0:T(8,128)}, f32[16,3200]{1,0:T(8,128)}, f32[16,3200]{1,0:T(8,128)}, f32[32,1600]{1,0:T(8,128)}, ...) custom-call(f32[16,6400]{1,0:T(8,128)S(1)} %get-tuple-element.121.refs_0_, f32[32,1600]{1,0:T(8,128)S(1)} %get-tuple-element.122.refs_1_, ...), custom_call_target="tpu_custom_call" | custom-call | tf_op jit(solution)/shard_map/moment_kernel/pallas_call | solution.py:99
  46.8 0.7 %collective-permute-done.14.refs_1_ = bf16[4,3200]{1,0:T(4,128)(2,1)S(1)} collective-permute-done((bf16[4,3200]{1,0:T(4,128)(2,1)S(1)}, bf16[4,3200]{1,0:T(4,128)(2,1)S(1)}, u32[]{:S(2)}, u32[]{:S(2)}) %collective-permute-start.14) | collective-permute-done | bytes 25632 | tf_op jit(solution)/shard_map/ppermute | solution.py:60
  47.5 1.8 %collective-permute-start.16 = (bf16[4,3200]{1,0:T(4,128)(2,1)S(1)}, bf16[4,3200]{1,0:T(4,128)(2,1)S(1)}, u32[]{:S(2)}, u32[]{:S(2)}) collective-permute-start(bf16[4,3200]{1,0:T(4,128)(2,1)S(1)} %get-tuple-element.129), channel_id=1, source_target_pairs={{0,24},{1,97},{2,26},{3,99},{4,28},{5,101},{6,30},{7,103},{8,16},{... | collective-permute-start | bytes 76808 | tf_op jit(solution)/shard_map/ppermute | solution.py:60
  49.4 0.0 collective-permute-done.17.refs_2_
  49.4 1.8 %down_update_kernel.1 = (bf16[1600,640]{1,0:T(8,128)(2,1)}, f32[8,128]{1,0:T(8,128)S(1)}) custom-call(bf16[1600,640]{1,0:T(8,128)(2,1)S(1)} %bitcast.9, f32[8,1600]{1,0:T(8,128)S(1)} %get-tuple-element.130.refs_1_, bf16[8,1600]{1,0:T(8,128)(2,1)S(1)} %collective-permute-done.17.refs_2_, f32[8,128]{1,0:T(8,128)S(1)} %get-tuple-element.132.refs_3_), custom_call_target="tpu_custom_call" | custom-call | tf_op jit(solution)/shard_map/down_update_kernel/pallas_call | solution.py:99
  51.2 1.5 %collective-permute-done.16.refs_3_ = bf16[4,3200]{1,0:T(4,128)(2,1)S(1)} collective-permute-done((bf16[4,3200]{1,0:T(4,128)(2,1)S(1)}, bf16[4,3200]{1,0:T(4,128)(2,1)S(1)}, u32[]{:S(2)}, u32[]{:S(2)}) %collective-permute-start.16) | collective-permute-done | bytes 25632 | tf_op jit(solution)/shard_map/ppermute | solution.py:60
  52.7 2.4 %update_kernel.1 = (bf16[320,3200]{1,0:T(8,128)(2,1)}, bf16[320,3200]{1,0:T(8,128)(2,1)}) custom-call(bf16[320,3200]{1,0:T(8,128)(2,1)S(1)} %get-tuple-element.76.refs_1_.refs_0_, bf16[320,3200]{1,0:T(8,128)(2,1)S(1)} %get-tuple-element.77.refs_3_.refs_1_, f32[4,3200]{1,0:T(4,128)S(1)} %get-tuple-element.128.refs_2_, ...), custom_call_target="tpu_custom_call" | custom-call | tf_op jit(solution)/shard_map/update_kernel/pallas_call | solution.py:99
  (23 shorter events, 0.1 us)
Async XLA Ops:
  3.5 9.4 %collective-permute-start.2 = (bf16[32,6400]{1,0:T(8,128)(2,1)S(1)}, bf16[32,6400]{1,0:T(8,128)(2,1)S(1)}, u32[]{:S(2)}, u32[]{:S(2)}) collective-permute-start(bf16[32,6400]{1,0:T(8,128)(2,1)S(1)} %get-tuple-element.85), channel_id=1, source_target_pairs={{0,8},{1,33},{2,10},{3,35},{4,12},{5,37},{6,14},{7,39},{8,16},{9,4... | collective-permute-start | bytes 1228808 | tf_op jit(solution)/shard_map/ppermute | solution.py:45
  5.1 8.0 %collective-permute-start.3 = (bf16[32,6400]{1,0:T(8,128)(2,1)S(1)}, bf16[32,6400]{1,0:T(8,128)(2,1)S(1)}, u32[]{:S(2)}, u32[]{:S(2)}) collective-permute-start(bf16[32,6400]{1,0:T(8,128)(2,1)S(1)} %get-tuple-element.87), channel_id=1, source_target_pairs={{0,24},{1,97},{2,26},{3,99},{4,28},{5,101},{6,30},{7,103},{8,0},{9... | collective-permute-start | bytes 1228808 | tf_op jit(solution)/shard_map/ppermute | solution.py:45
  6.8 4.9 %copy-start = (bf16[640,1600]{0,1:T(8,128)(2,1)S(1)}, bf16[640,1600]{0,1:T(8,128)(2,1)}, u32[]{:S(2)}) copy-start(bf16[640,1600]{0,1:T(8,128)(2,1)} %param.14) | copy-start | bytes 6144004
  6.8 4.9 %copy-start.3 = (bf16[256,640]{1,0:T(8,128)(2,1)S(1)}, bf16[256,640]{1,0:T(8,128)(2,1)}, u32[]{:S(2)}) copy-start(bf16[256,640]{1,0:T(8,128)(2,1)} %refs_0_.1) | copy-start | bytes 983044
  8.4 9.2 %collective-permute-start = (bf16[32,6400]{1,0:T(8,128)(2,1)S(1)}, bf16[32,6400]{1,0:T(8,128)(2,1)S(1)}, u32[]{:S(2)}, u32[]{:S(2)}) collective-permute-start(bf16[32,6400]{1,0:T(8,128)(2,1)S(1)} %get-tuple-element.82), channel_id=1, source_target_pairs={{0,8},{1,33},{2,10},{3,35},{4,12},{5,37},{6,14},{7,39},{8,16},{9,4... | collective-permute-start | bytes 1228808 | tf_op jit(solution)/shard_map/ppermute | solution.py:45
  8.8 8.8 %collective-permute-start.1 = (bf16[32,6400]{1,0:T(8,128)(2,1)S(1)}, bf16[32,6400]{1,0:T(8,128)(2,1)S(1)}, u32[]{:S(2)}, u32[]{:S(2)}) collective-permute-start(bf16[32,6400]{1,0:T(8,128)(2,1)S(1)} %get-tuple-element.83), channel_id=1, source_target_pairs={{0,24},{1,97},{2,26},{3,99},{4,28},{5,101},{6,30},{7,103},{8,0},{9... | collective-permute-start | bytes 1228808 | tf_op jit(solution)/shard_map/ppermute | solution.py:45
  12.8 5.1 %collective-permute-start.5 = (bf16[128,1600]{1,0:T(8,128)(2,1)S(1)}, bf16[128,1600]{1,0:T(8,128)(2,1)S(1)}, u32[]{:S(2)}, u32[]{:S(2)}) collective-permute-start(bf16[128,1600]{1,0:T(8,128)(2,1)S(1)} %get-tuple-element.94), channel_id=1, source_target_pairs={{0,1},{1,0},{2,3},{3,2},{4,5},{5,4},{6,7},{7,6},{8,9},{9,8},{10,11... | collective-permute-start | bytes 1228808 | tf_op jit(solution)/shard_map/ppermute | solution.py:69
  13.3 9.2 %collective-permute-start.4 = (bf16[32,6400]{1,0:T(8,128)(2,1)S(1)}, bf16[32,6400]{1,0:T(8,128)(2,1)S(1)}, u32[]{:S(2)}, u32[]{:S(2)}) collective-permute-start(bf16[32,6400]{1,0:T(8,128)(2,1)S(1)} %get-tuple-element.92), channel_id=1, source_target_pairs={{0,8},{1,33},{2,10},{3,35},{4,12},{5,37},{6,14},{7,39},{8,16},{9,4... | collective-permute-start | bytes 1228808 | tf_op jit(solution)/shard_map/ppermute | solution.py:45
  14.8 11.0 %collective-permute-start.8 = (bf16[32,6400]{1,0:T(8,128)(2,1)S(1)}, bf16[32,6400]{1,0:T(8,128)(2,1)S(1)}, u32[]{:S(2)}, u32[]{:S(2)}) collective-permute-start(bf16[32,6400]{1,0:T(8,128)(2,1)S(1)} %get-tuple-element.102), channel_id=1, source_target_pairs={{0,24},{1,97},{2,26},{3,99},{4,28},{5,101},{6,30},{7,103},{8,0},{9... | collective-permute-start | bytes 1228808 | tf_op jit(solution)/shard_map/ppermute | solution.py:45
  17.8 11.4 %copy-start.1 = (f32[32,1600]{1,0:T(8,128)S(1)}, f32[32,1600]{1,0:T(8,128)}, u32[]{:S(2)}) copy-start(f32[32,1600]{1,0:T(8,128)} %refs_6_.3) | copy-start | bytes 614404
  17.8 11.4 %copy-start.2 = (f32[32,1600]{1,0:T(8,128)S(1)}, f32[32,1600]{1,0:T(8,128)}, u32[]{:S(2)}) copy-start(f32[32,1600]{1,0:T(8,128)} %refs_7_.1) | copy-start | bytes 614404
  18.0 11.3 %collective-permute-start.7 = (bf16[64,1600]{1,0:T(8,128)(2,1)S(1)}, bf16[64,1600]{1,0:T(8,128)(2,1)S(1)}, u32[]{:S(2)}, u32[]{:S(2)}) collective-permute-start(bf16[64,1600]{1,0:T(8,128)(2,1)S(1)} %get-tuple-element.100), channel_id=1, source_target_pairs={{0,2},{2,0},{4,6},{6,4},{1,3},{3,1},{5,7},{7,5},{8,10},{10,8},{12,... | collective-permute-start | bytes 614408 | tf_op jit(solution)/shard_map/ppermute | solution.py:65
  22.5 11.0 %copy-start.4 = (f32[16,3200]{1,0:T(8,128)S(1)}, f32[16,3200]{1,0:T(8,128)}, u32[]{:S(2)}) copy-start(f32[16,3200]{1,0:T(8,128)} %refs_2_.5) | copy-start | bytes 614404
  22.5 11.1 %copy-start.5 = (f32[16,3200]{1,0:T(8,128)S(1)}, f32[16,3200]{1,0:T(8,128)}, u32[]{:S(2)}) copy-start(f32[16,3200]{1,0:T(8,128)} %refs_3_.7) | copy-start | bytes 614404
  22.5 11.1 %copy-start.6 = (f32[16,3200]{1,0:T(8,128)S(1)}, f32[16,3200]{1,0:T(8,128)}, u32[]{:S(2)}) copy-start(f32[16,3200]{1,0:T(8,128)} %refs_4_.3) | copy-start | bytes 614404
  22.5 11.1 %copy-start.7 = (f32[16,3200]{1,0:T(8,128)S(1)}, f32[16,3200]{1,0:T(8,128)}, u32[]{:S(2)}) copy-start(f32[16,3200]{1,0:T(8,128)} %refs_5_.3) | copy-start | bytes 614404
  22.6 10.9 %collective-permute-start.6 = (bf16[16,6400]{1,0:T(8,128)(2,1)S(1)}, bf16[16,6400]{1,0:T(8,128)(2,1)S(1)}, u32[]{:S(2)}, u32[]{:S(2)}) collective-permute-start(bf16[16,6400]{1,0:T(8,128)(2,1)S(1)} %get-tuple-element.98), channel_id=1, source_target_pairs={{0,64},{1,17},{2,66},{3,19},{4,68},{5,21},{6,70},{7,23},{8,72},{9,... | collective-permute-start | bytes 614408 | tf_op jit(solution)/shard_map/ppermute | solution.py:45
  25.9 7.6 %collective-permute-start.9 = (bf16[16,6400]{1,0:T(8,128)(2,1)S(1)}, bf16[16,6400]{1,0:T(8,128)(2,1)S(1)}, u32[]{:S(2)}, u32[]{:S(2)}) collective-permute-start(bf16[16,6400]{1,0:T(8,128)(2,1)S(1)} %get-tuple-element.107), channel_id=1, source_target_pairs={{0,32},{1,9},{2,34},{3,11},{4,36},{5,13},{6,38},{7,15},{8,40},{9,1... | collective-permute-start | bytes 614408 | tf_op jit(solution)/shard_map/ppermute | solution.py:45
  26.7 6.8 %collective-permute-start.10 = (bf16[16,6400]{1,0:T(8,128)(2,1)S(1)}, bf16[16,6400]{1,0:T(8,128)(2,1)S(1)}, u32[]{:S(2)}, u32[]{:S(2)}) collective-permute-start(bf16[16,6400]{1,0:T(8,128)(2,1)S(1)} %get-tuple-element.108), channel_id=1, source_target_pairs={{0,96},{1,25},{2,98},{3,27},{4,100},{5,29},{6,102},{7,31},{8,104},... | collective-permute-start | bytes 614408 | tf_op jit(solution)/shard_map/ppermute | solution.py:45
  29.4 11.6 %collective-permute-start.13 = (bf16[128,1600]{1,0:T(8,128)(2,1)S(1)}, bf16[128,1600]{1,0:T(8,128)(2,1)S(1)}, u32[]{:S(2)}, u32[]{:S(2)}) collective-permute-start(bf16[128,1600]{1,0:T(8,128)(2,1)S(1)} %get-tuple-element.116), channel_id=1, source_target_pairs={{0,6},{6,0},{2,4},{4,2},{1,7},{7,1},{3,5},{5,3},{8,14},{14,8},{10,... | collective-permute-start | bytes 1228808 | tf_op jit(solution)/shard_map/ppermute | solution.py:65
  34.3 3.9 %collective-permute-start.11 = (bf16[4,3200]{1,0:T(4,128)(2,1)S(1)}, bf16[4,3200]{1,0:T(4,128)(2,1)S(1)}, u32[]{:S(2)}, u32[]{:S(2)}) collective-permute-start(bf16[4,3200]{1,0:T(4,128)(2,1)S(1)} %get-tuple-element.111), channel_id=1, source_target_pairs={{0,32},{1,9},{2,34},{3,11},{4,36},{5,13},{6,38},{7,15},{8,40},{9,1... | collective-permute-start | bytes 76808 | tf_op jit(solution)/shard_map/ppermute | solution.py:60
  38.2 5.4 %collective-permute-start.12 = (bf16[4,3200]{1,0:T(4,128)(2,1)S(1)}, bf16[4,3200]{1,0:T(4,128)(2,1)S(1)}, u32[]{:S(2)}, u32[]{:S(2)}) collective-permute-start(bf16[4,3200]{1,0:T(4,128)(2,1)S(1)} %get-tuple-element.114), channel_id=1, source_target_pairs={{0,96},{1,25},{2,98},{3,27},{4,100},{5,29},{6,102},{7,31},{8,104},... | collective-permute-start | bytes 76808 | tf_op jit(solution)/shard_map/ppermute | solution.py:60
  41.6 3.9 %collective-permute-start.15 = (bf16[8,1600]{1,0:T(8,128)(2,1)S(1)}, bf16[8,1600]{1,0:T(8,128)(2,1)S(1)}, u32[]{:S(2)}, u32[]{:S(2)}) collective-permute-start(bf16[8,1600]{1,0:T(8,128)(2,1)S(1)} %get-tuple-element.124), channel_id=1, source_target_pairs={{0,2},{2,0},{4,6},{6,4},{1,3},{3,1},{5,7},{7,5},{8,10},{10,8},{12,... | collective-permute-start | bytes 76808 | tf_op jit(solution)/shard_map/ppermute | solution.py:65
  43.6 3.9 %collective-permute-start.14 = (bf16[4,3200]{1,0:T(4,128)(2,1)S(1)}, bf16[4,3200]{1,0:T(4,128)(2,1)S(1)}, u32[]{:S(2)}, u32[]{:S(2)}) collective-permute-start(bf16[4,3200]{1,0:T(4,128)(2,1)S(1)} %get-tuple-element.120), channel_id=1, source_target_pairs={{0,8},{1,33},{2,10},{3,35},{4,12},{5,37},{6,14},{7,39},{8,0},{9,41... | collective-permute-start | bytes 76808 | tf_op jit(solution)/shard_map/ppermute | solution.py:60
  45.5 3.8 %collective-permute-start.17 = (bf16[8,1600]{1,0:T(8,128)(2,1)S(1)}, bf16[8,1600]{1,0:T(8,128)(2,1)S(1)}, u32[]{:S(2)}, u32[]{:S(2)}) collective-permute-start(bf16[8,1600]{1,0:T(8,128)(2,1)S(1)} %get-tuple-element.131), channel_id=1, source_target_pairs={{0,1},{1,0},{2,3},{3,2},{4,5},{5,4},{6,7},{7,6},{8,9},{9,8},{10,11... | collective-permute-start | bytes 76808 | tf_op jit(solution)/shard_map/ppermute | solution.py:69
  47.5 5.1 %collective-permute-start.16 = (bf16[4,3200]{1,0:T(4,128)(2,1)S(1)}, bf16[4,3200]{1,0:T(4,128)(2,1)S(1)}, u32[]{:S(2)}, u32[]{:S(2)}) collective-permute-start(bf16[4,3200]{1,0:T(4,128)(2,1)S(1)} %get-tuple-element.129), channel_id=1, source_target_pairs={{0,24},{1,97},{2,26},{3,99},{4,28},{5,101},{6,30},{7,103},{8,16},{... | collective-permute-start | bytes 76808 | tf_op jit(solution)/shard_map/ppermute | solution.py:60

commit v6 on v5

--- a/solution.py
+++ b/solution.py
@@ -129,7 +129,6 @@
     step = lax.broadcasted_iota(jnp.int32, (256, 1), 0)
     outer, inner = step // 64, step // 16 % 4
     outer = jnp.where(outer == 0, 2, jnp.where(outer == 3, 0, jnp.where(outer == 1, 1, 3)))
-    inner = jnp.where(inner == 1, 2, jnp.where(inner == 2, 1, inner))
     on_x, on_y = jnp.where(core == 0, outer, inner), jnp.where(core == 0, inner, outer)
     return ((y + on_y) % 4 * 4 + (x + on_x) % 4) * 16 + step % 16
 
@@ -197,15 +196,15 @@
     high[...] = wide(keep[32:], high_below[...])
 
 
-def near_kernel(low, low_below, own, opposite):
+def near_kernel(low, low_below, own, above):
     total = wide(low[...], low_below[...])
     own[...] = total[:16]
-    opposite[...] = total[16:].astype(BF16)
-
-
-def far_kernel(high, high_above, above, below):
+    above[...] = total[16:].astype(BF16)
+
+
+def far_kernel(high, high_above, opposite, below):
     total = wide(high[...], high_above[...]).astype(BF16)
-    above[...] = total[:16]
+    opposite[...] = total[:16]
     below[...] = total[16:]
 
 
@@ -355,10 +354,10 @@
     )
     other_down = z_swap(other_down, False)
 
-    own, opposite = run(near_kernel, (pltpu.VMEM((16, 6400), F32), piece), low, low_below)
-    opposite = ring_send(opposite, 2, 1)
-    above, below = run(far_kernel, (piece, piece), high, high_above)
-    above, below = ring_send(above, 1, 1), ring_send(below, 3, 1)
+    own, above = run(near_kernel, (pltpu.VMEM((16, 6400), F32), piece), low, low_below)
+    above = ring_send(above, 1, 1)
+    opposite, below = run(far_kernel, (piece, piece), high, high_above)
+    opposite, below = ring_send(opposite, 2, 1), ring_send(below, 3, 1)
     own_down, other_down = run(
         down_halve_kernel,
         (pltpu.VMEM((64, 1600), F32), pltpu.VMEM((128, 1600), BF16)),
@@ -367,9 +366,9 @@
     other_down = z_swap(other_down, True)
 
     states = (first_gate, second_gate, first_up, second_up)
-    (own,) = run(add_kernel, (pltpu.VMEM((16, 6400), F32),), own, opposite)
+    (own,) = run(add_kernel, (pltpu.VMEM((16, 6400), F32),), own, above)
     sums, sent, total = run(
-        pair_sum_kernel, (pair_row, sent_pair, pltpu.VMEM((16, 6400), F32)), own, above, below, *states,
+        pair_sum_kernel, (pair_row, sent_pair, pltpu.VMEM((16, 6400), F32)), own, below, opposite, *states,
         cost=8 * 10**9,
     )
     other = ring_swap(sent, False, 1)

time: 55.1 us -> 54.7 us (level)
  waiting for transfers between devices: 10.9 us -> 9.5 us
  starting transfers between devices: 30.2 us -> 31.1 us
    ppermute x4, starting transfers between devices: 5.32 us -> 7.49 us  [ring_swap(): return lax.ppermute(value, AXES, pairs)]
    ppermute x3, waiting for transfers between devices: 1.56 us -> 0.22 us  [z_swap(): return lax.ppermute(value, 'z', pairs)]
    ppermute x9, starting transfers between devices: 16.5 us -> 15.3 us  [ring_send(): return lax.ppermute(value, AXES, ring_pairs(shift, stage))]
    ppermute x4, waiting for transfers between devices: 5.67 us -> 4.61 us  [ring_swap(): return lax.ppermute(value, AXES, pairs)]
    ppermute x9, waiting for transfers between devices: 3.67 us -> 4.67 us  [ring_send(): return lax.ppermute(value, AXES, ring_pairs(shift, stage))]
  transfers between devices with their start and end apart: 18 -> 18, of which waited for: 7 -> 9; matrix products, arithmetic and copies ran while one was open for 0% -> 0% of each run, Pallas kernels for 14% -> 15%
where the time goes in v6:
time: 54.7 us; the launch traced here: 54.5 us
  starting transfers between devices  31.1 us (57%)
  Pallas kernels  13.1 us (24%)
  waiting for transfers between devices  9.5 us (17%)
  between operations  0.81 us (1%)
    ppermute x9, starting transfers between devices, ring_send(): return lax.ppermute(value, AXES, ring_pairs(shift, stage))  15.3 us
    pallas_call x19, Pallas kernels, __call__(): pl.pallas_call(kernel, name=body.__name__, out_shape=[*outs, *token_out],...  13.1 us
    ppermute x3, starting transfers between devices, z_swap(): return lax.ppermute(value, 'z', pairs)  8.18 us
    ppermute x4, starting transfers between devices, ring_swap(): return lax.ppermute(value, AXES, pairs)  7.49 us
    ppermute x9, waiting for transfers between devices, ring_send(): return lax.ppermute(value, AXES, ring_pairs(shift, stage))  4.67 us
    ppermute x4, waiting for transfers between devices, ring_swap(): return lax.ppermute(value, AXES, pairs)  4.61 us
  transfers between devices with their start and end apart: 18, of which 9 were waited for; matrix products, arithmetic and copies ran while one was open for 0% of the time, Pallas kernels for 15%

profile of v6, /device:TPU:0, one launch (start us, length us, event | category | flops | bytes accessed | tf_op | source)
XLA Modules:
  0.0 54.5 jit_solution(10489623620380953111)
XLA Ops:
  0.6 2.8 %first_kernel.1 = (bf16[32,6400]{1,0:T(8,128)(2,1)S(1)}, bf16[32,6400]{1,0:T(8,128)(2,1)S(1)}, bf16[192,320]{1,0:T(8,128)(2,1)S(1)}, bf16[192,320]{1,0:T(8,128)(...) custom-call(bf16[320,256]{1,0:T(8,128)(2,1)} %bitcast.12, ...), custom_call_target="tpu_custom_call" | custom-call | tf_op jit(solution)/shard_map/first_kernel/pallas_call | solution.py:99
  3.5 1.6 %collective-permute-start.2 = (bf16[32,6400]{1,0:T(8,128)(2,1)S(1)}, bf16[32,6400]{1,0:T(8,128)(2,1)S(1)}, u32[]{:S(2)}, u32[]{:S(2)}) collective-permute-start(bf16[32,6400]{1,0:T(8,128)(2,1)S(1)} %get-tuple-element.85), channel_id=1, source_target_pairs={{0,8},{1,33},{2,10},{3,35},{4,12},{5,37},{6,14},{7,39},{8,16},{9,4... | collective-permute-start | bytes 1228808 | tf_op jit(solution)/shard_map/ppermute | solution.py:45
  5.1 1.7 %collective-permute-start.3 = (bf16[32,6400]{1,0:T(8,128)(2,1)S(1)}, bf16[32,6400]{1,0:T(8,128)(2,1)S(1)}, u32[]{:S(2)}, u32[]{:S(2)}) collective-permute-start(bf16[32,6400]{1,0:T(8,128)(2,1)S(1)} %get-tuple-element.87), channel_id=1, source_target_pairs={{0,24},{1,97},{2,26},{3,99},{4,28},{5,101},{6,30},{7,103},{8,0},{9... | collective-permute-start | bytes 1228808 | tf_op jit(solution)/shard_map/ppermute | solution.py:45
  6.8 1.6 %rest_kernel.1 = (bf16[32,6400]{1,0:T(8,128)(2,1)S(1)}, bf16[32,6400]{1,0:T(8,128)(2,1)S(1)}, bf16[32,6400]{1,0:T(8,128)(2,1)S(1)}, bf16[32,6400]{1,0:T(8,128)(2...) custom-call(bf16[192,320]{1,0:T(8,128)(2,1)S(1)} %get-tuple-element.78.refs_0_, ...), custom_call_target="tpu_custom_call" | custom-call | tf_op jit(solution)/shard_map/rest_kernel/pallas_call | solution.py:99
  8.4 0.4 collective-permute-start
  8.8 2.9 %collective-permute-start.1 = (bf16[32,6400]{1,0:T(8,128)(2,1)S(1)}, bf16[32,6400]{1,0:T(8,128)(2,1)S(1)}, u32[]{:S(2)}, u32[]{:S(2)}) collective-permute-start(bf16[32,6400]{1,0:T(8,128)(2,1)S(1)} %get-tuple-element.83), channel_id=1, source_target_pairs={{0,24},{1,97},{2,26},{3,99},{4,28},{5,101},{6,30},{7,103},{8,0},{9... | collective-permute-start | bytes 1228808 | tf_op jit(solution)/shard_map/ppermute | solution.py:45
  11.7 1.1 %down_kernel.1 = (bf16[128,1600]{1,0:T(8,128)(2,1)S(1)}, bf16[128,1600]{1,0:T(8,128)(2,1)S(1)}, f32[8,128]{1,0:T(8,128)S(1)}) custom-call(bf16[256,640]{1,0:T(8,128)(2,1)S(1)} %copy-done.3, bf16[1600,640]{1,0:T(8,128)(2,1)S(1)} %bitcast.8, f32[8,128]{1,0:T(8,128)S(1)} %get-tuple-element.88.refs_2_), custom_call_target="tpu_custom_call" | custom-call | tf_op jit(solution)/shard_map/down_kernel/pallas_call | solution.py:99
  12.8 0.1 collective-permute-start.5
  12.9 0.2 collective-permute-done.3.refs_3_
  13.1 0.2 pass_kernel.1
  13.3 1.6 %collective-permute-start.4 = (bf16[32,6400]{1,0:T(8,128)(2,1)S(1)}, bf16[32,6400]{1,0:T(8,128)(2,1)S(1)}, u32[]{:S(2)}, u32[]{:S(2)}) collective-permute-start(bf16[32,6400]{1,0:T(8,128)(2,1)S(1)} %get-tuple-element.92), channel_id=1, source_target_pairs={{0,8},{1,33},{2,10},{3,35},{4,12},{5,37},{6,14},{7,39},{8,16},{9,4... | collective-permute-start | bytes 1228808 | tf_op jit(solution)/shard_map/ppermute | solution.py:45
  14.8 1.7 %collective-permute-start.8 = (bf16[32,6400]{1,0:T(8,128)(2,1)S(1)}, bf16[32,6400]{1,0:T(8,128)(2,1)S(1)}, u32[]{:S(2)}, u32[]{:S(2)}) collective-permute-start(bf16[32,6400]{1,0:T(8,128)(2,1)S(1)} %get-tuple-element.102), channel_id=1, source_target_pairs={{0,24},{1,97},{2,26},{3,99},{4,28},{5,101},{6,30},{7,103},{8,0},{9... | collective-permute-start | bytes 1228808 | tf_op jit(solution)/shard_map/ppermute | solution.py:45
  16.6 1.0 %collective-permute-done.refs_1_ = bf16[32,6400]{1,0:T(8,128)(2,1)S(1)} collective-permute-done((bf16[32,6400]{1,0:T(8,128)(2,1)S(1)}, bf16[32,6400]{1,0:T(8,128)(2,1)S(1)}, u32[]{:S(2)}, u32[]{:S(2)}) %collective-permute-start) | collective-permute-done | bytes 409632 | tf_op jit(solution)/shard_map/ppermute | solution.py:45
  17.6 0.0 collective-permute-done.1.refs_2_
  17.6 0.2 collect_kernel.1
  17.8 0.0 copy-start.1
  17.8 0.0 copy-start.2
  17.9 0.0 collective-permute-done.5.refs_1_
  17.9 0.1 down_split_kernel.1
  18.0 2.1 %collective-permute-start.7 = (bf16[64,1600]{1,0:T(8,128)(2,1)S(1)}, bf16[64,1600]{1,0:T(8,128)(2,1)S(1)}, u32[]{:S(2)}, u32[]{:S(2)}) collective-permute-start(bf16[64,1600]{1,0:T(8,128)(2,1)S(1)} %get-tuple-element.100), channel_id=1, source_target_pairs={{0,2},{2,0},{4,6},{6,4},{1,3},{3,1},{5,7},{7,5},{8,10},{10,8},{12,... | collective-permute-start | bytes 614408 | tf_op jit(solution)/shard_map/ppermute | solution.py:65
  20.0 2.4 %collective-permute-done.4.refs_1_ = bf16[32,6400]{1,0:T(8,128)(2,1)S(1)} collective-permute-done((bf16[32,6400]{1,0:T(8,128)(2,1)S(1)}, bf16[32,6400]{1,0:T(8,128)(2,1)S(1)}, u32[]{:S(2)}, u32[]{:S(2)}) %collective-permute-start.4) | collective-permute-done | bytes 409632 | tf_op jit(solution)/shard_map/ppermute | solution.py:45
  22.5 0.1 near_kernel.1
  22.6 1.6 %collective-permute-start.6 = (bf16[16,6400]{1,0:T(8,128)(2,1)S(1)}, bf16[16,6400]{1,0:T(8,128)(2,1)S(1)}, u32[]{:S(2)}, u32[]{:S(2)}) collective-permute-start(bf16[16,6400]{1,0:T(8,128)(2,1)S(1)} %get-tuple-element.98), channel_id=1, source_target_pairs={{0,32},{1,9},{2,34},{3,11},{4,36},{5,13},{6,38},{7,15},{8,40},{9,1... | collective-permute-start | bytes 614408 | tf_op jit(solution)/shard_map/ppermute | solution.py:45
  24.2 0.1 far_kernel.1
  24.3 1.7 %collective-permute-start.9 = (bf16[16,6400]{1,0:T(8,128)(2,1)S(1)}, bf16[16,6400]{1,0:T(8,128)(2,1)S(1)}, u32[]{:S(2)}, u32[]{:S(2)}) collective-permute-start(bf16[16,6400]{1,0:T(8,128)(2,1)S(1)} %get-tuple-element.107), channel_id=1, source_target_pairs={{0,96},{1,25},{2,98},{3,27},{4,100},{5,29},{6,102},{7,31},{8,104},... | collective-permute-start | bytes 614408 | tf_op jit(solution)/shard_map/ppermute | solution.py:45
  26.0 2.0 %collective-permute-start.10 = (bf16[16,6400]{1,0:T(8,128)(2,1)S(1)}, bf16[16,6400]{1,0:T(8,128)(2,1)S(1)}, u32[]{:S(2)}, u32[]{:S(2)}) collective-permute-start(bf16[16,6400]{1,0:T(8,128)(2,1)S(1)} %get-tuple-element.108), channel_id=1, source_target_pairs={{0,64},{1,17},{2,66},{3,19},{4,68},{5,21},{6,70},{7,23},{8,72},{9,... | collective-permute-start | bytes 614408 | tf_op jit(solution)/shard_map/ppermute | solution.py:45
  28.0 0.0 collective-permute-done.7.refs_1_
  28.0 0.1 down_halve_kernel.1
  28.1 4.1 %collective-permute-start.13 = (bf16[128,1600]{1,0:T(8,128)(2,1)S(1)}, bf16[128,1600]{1,0:T(8,128)(2,1)S(1)}, u32[]{:S(2)}, u32[]{:S(2)}) collective-permute-start(bf16[128,1600]{1,0:T(8,128)(2,1)S(1)} %get-tuple-element.116), channel_id=1, source_target_pairs={{0,6},{6,0},{2,4},{4,2},{1,7},{7,1},{3,5},{5,3},{8,14},{14,8},{10,... | collective-permute-start | bytes 1228808 | tf_op jit(solution)/shard_map/ppermute | solution.py:65
  32.3 0.0 collective-permute-done.9.refs_1_
  32.3 1.0 %collective-permute-done.10.refs_2_ = bf16[16,6400]{1,0:T(8,128)(2,1)S(1)} collective-permute-done((bf16[16,6400]{1,0:T(8,128)(2,1)S(1)}, bf16[16,6400]{1,0:T(8,128)(2,1)S(1)}, u32[]{:S(2)}, u32[]{:S(2)}) %collective-permute-start.10) | collective-permute-done | bytes 204832 | tf_op jit(solution)/shard_map/ppermute | solution.py:45
  33.3 0.7 %pair_sum_kernel.1 = (f32[4,3200]{1,0:T(4,128)S(1)}, bf16[4,3200]{1,0:T(4,128)(2,1)S(1)}, f32[16,6400]{1,0:T(8,128)S(1)}, f32[8,128]{1,0:T(8,128)S(1)}) custom-call(f32[16,6400]{1,0:T(8,128)S(1)} %get-tuple-element.106.refs_0_, bf16[16,6400]{1,0:T(8,128)(2,1)S(1)} %collective-permute-done.9.refs_1_, bf16[16,6400]{1,0:T(8,128)(2,1)S(1)} %collective-permute-done.10.refs_2_, ...), custom_call_target="tpu_custom_call" | custom-call | flops 8000000000 | tf_op jit(solution)/shard_map/pair_sum_kernel/pallas_call | solution.py:99
  34.0 1.4 %collective-permute-start.11 = (bf16[4,3200]{1,0:T(4,128)(2,1)S(1)}, bf16[4,3200]{1,0:T(4,128)(2,1)S(1)}, u32[]{:S(2)}, u32[]{:S(2)}) collective-permute-start(bf16[4,3200]{1,0:T(4,128)(2,1)S(1)} %get-tuple-element.111), channel_id=1, source_target_pairs={{0,32},{1,9},{2,34},{3,11},{4,36},{5,13},{6,38},{7,15},{8,40},{9,1... | collective-permute-start | bytes 76808 | tf_op jit(solution)/shard_map/ppermute | solution.py:60
  35.4 2.5 %collective-permute-done.11.refs_1_ = bf16[4,3200]{1,0:T(4,128)(2,1)S(1)} collective-permute-done((bf16[4,3200]{1,0:T(4,128)(2,1)S(1)}, bf16[4,3200]{1,0:T(4,128)(2,1)S(1)}, u32[]{:S(2)}, u32[]{:S(2)}) %collective-permute-start.11) | collective-permute-done | bytes 25632 | tf_op jit(solution)/shard_map/ppermute | solution.py:60
  38.0 2.0 %collective-permute-start.12 = (bf16[4,3200]{1,0:T(4,128)(2,1)S(1)}, bf16[4,3200]{1,0:T(4,128)(2,1)S(1)}, u32[]{:S(2)}, u32[]{:S(2)}) collective-permute-start(bf16[4,3200]{1,0:T(4,128)(2,1)S(1)} %get-tuple-element.114), channel_id=1, source_target_pairs={{0,96},{1,25},{2,98},{3,27},{4,100},{5,29},{6,102},{7,31},{8,104},... | collective-permute-start | bytes 76808 | tf_op jit(solution)/shard_map/ppermute | solution.py:60
  39.9 0.0 collective-permute-done.13.refs_1_
  39.9 0.6 %down_sum_kernel.1 = (f32[8,1600]{1,0:T(8,128)S(1)}, bf16[8,1600]{1,0:T(8,128)(2,1)S(1)}, f32[32,1600]{1,0:T(8,128)S(1)}, f32[8,128]{1,0:T(8,128)S(1)}) custom-call(f32[64,1600]{1,0:T(8,128)S(1)} %get-tuple-element.115.refs_0_, bf16[128,1600]{1,0:T(8,128)(2,1)S(1)} %collective-permute-done.13.refs_1_, f32[32,1600]{1,0:T(8,128)S(1)} %copy-done.1, ...), custom_call_target="tpu_custom_call" | custom-call | tf_op jit(solution)/shard_map/down_sum_kernel/pallas_call | solution.py:99
  40.6 2.0 %collective-permute-start.15 = (bf16[8,1600]{1,0:T(8,128)(2,1)S(1)}, bf16[8,1600]{1,0:T(8,128)(2,1)S(1)}, u32[]{:S(2)}, u32[]{:S(2)}) collective-permute-start(bf16[8,1600]{1,0:T(8,128)(2,1)S(1)} %get-tuple-element.124), channel_id=1, source_target_pairs={{0,2},{2,0},{4,6},{6,4},{1,3},{3,1},{5,7},{7,5},{8,10},{10,8},{12,... | collective-permute-start | bytes 76808 | tf_op jit(solution)/shard_map/ppermute | solution.py:65
  42.6 0.5 collective-permute-done.12.refs_1_
  43.1 1.2 %collective-permute-start.14 = (bf16[4,3200]{1,0:T(4,128)(2,1)S(1)}, bf16[4,3200]{1,0:T(4,128)(2,1)S(1)}, u32[]{:S(2)}, u32[]{:S(2)}) collective-permute-start(bf16[4,3200]{1,0:T(4,128)(2,1)S(1)} %get-tuple-element.120), channel_id=1, source_target_pairs={{0,8},{1,33},{2,10},{3,35},{4,12},{5,37},{6,14},{7,39},{8,0},{9,41... | collective-permute-start | bytes 76808 | tf_op jit(solution)/shard_map/ppermute | solution.py:60
  44.3 0.2 collective-permute-done.15.refs_1_
  44.5 0.1 collective-permute-start.17
  44.6 1.2 %moment_kernel.1 = (f32[16,3200]{1,0:T(8,128)}, f32[16,3200]{1,0:T(8,128)}, f32[16,3200]{1,0:T(8,128)}, f32[16,3200]{1,0:T(8,128)}, f32[32,1600]{1,0:T(8,128)}, ...) custom-call(f32[16,6400]{1,0:T(8,128)S(1)} %get-tuple-element.121.refs_0_, f32[32,1600]{1,0:T(8,128)S(1)} %get-tuple-element.122.refs_1_, ...), custom_call_target="tpu_custom_call" | custom-call | tf_op jit(solution)/shard_map/moment_kernel/pallas_call | solution.py:99
  45.8 1.2 %collective-permute-done.14.refs_1_ = bf16[4,3200]{1,0:T(4,128)(2,1)S(1)} collective-permute-done((bf16[4,3200]{1,0:T(4,128)(2,1)S(1)}, bf16[4,3200]{1,0:T(4,128)(2,1)S(1)}, u32[]{:S(2)}, u32[]{:S(2)}) %collective-permute-start.14) | collective-permute-done | bytes 25632 | tf_op jit(solution)/shard_map/ppermute | solution.py:60
  47.0 2.9 %collective-permute-start.16 = (bf16[4,3200]{1,0:T(4,128)(2,1)S(1)}, bf16[4,3200]{1,0:T(4,128)(2,1)S(1)}, u32[]{:S(2)}, u32[]{:S(2)}) collective-permute-start(bf16[4,3200]{1,0:T(4,128)(2,1)S(1)} %get-tuple-element.129), channel_id=1, source_target_pairs={{0,24},{1,97},{2,26},{3,99},{4,28},{5,101},{6,30},{7,103},{8,16},{... | collective-permute-start | bytes 76808 | tf_op jit(solution)/shard_map/ppermute | solution.py:60
  50.0 1.8 %down_update_kernel.1 = (bf16[1600,640]{1,0:T(8,128)(2,1)}, f32[8,128]{1,0:T(8,128)S(1)}) custom-call(bf16[1600,640]{1,0:T(8,128)(2,1)S(1)} %bitcast.9, f32[8,1600]{1,0:T(8,128)S(1)} %get-tuple-element.130.refs_1_, bf16[8,1600]{1,0:T(8,128)(2,1)S(1)} %collective-permute-done.17.refs_2_, f32[8,128]{1,0:T(8,128)S(1)} %get-tuple-element.132.refs_3_), custom_call_target="tpu_custom_call" | custom-call | tf_op jit(solution)/shard_map/down_update_kernel/pallas_call | solution.py:99
  51.8 0.4 collective-permute-done.16.refs_3_
  52.2 2.4 %update_kernel.1 = (bf16[320,3200]{1,0:T(8,128)(2,1)}, bf16[320,3200]{1,0:T(8,128)(2,1)}) custom-call(bf16[320,3200]{1,0:T(8,128)(2,1)S(1)} %get-tuple-element.76.refs_1_.refs_0_, bf16[320,3200]{1,0:T(8,128)(2,1)S(1)} %get-tuple-element.77.refs_3_.refs_1_, f32[4,3200]{1,0:T(4,128)S(1)} %get-tuple-element.128.refs_2_, ...), custom_call_target="tpu_custom_call" | custom-call | tf_op jit(solution)/shard_map/update_kernel/pallas_call | solution.py:99
  (23 shorter events, 0.1 us)
Async XLA Ops:
  3.5 9.4 %collective-permute-start.2 = (bf16[32,6400]{1,0:T(8,128)(2,1)S(1)}, bf16[32,6400]{1,0:T(8,128)(2,1)S(1)}, u32[]{:S(2)}, u32[]{:S(2)}) collective-permute-start(bf16[32,6400]{1,0:T(8,128)(2,1)S(1)} %get-tuple-element.85), channel_id=1, source_target_pairs={{0,8},{1,33},{2,10},{3,35},{4,12},{5,37},{6,14},{7,39},{8,16},{9,4... | collective-permute-start | bytes 1228808 | tf_op jit(solution)/shard_map/ppermute | solution.py:45
  5.1 8.0 %collective-permute-start.3 = (bf16[32,6400]{1,0:T(8,128)(2,1)S(1)}, bf16[32,6400]{1,0:T(8,128)(2,1)S(1)}, u32[]{:S(2)}, u32[]{:S(2)}) collective-permute-start(bf16[32,6400]{1,0:T(8,128)(2,1)S(1)} %get-tuple-element.87), channel_id=1, source_target_pairs={{0,24},{1,97},{2,26},{3,99},{4,28},{5,101},{6,30},{7,103},{8,0},{9... | collective-permute-start | bytes 1228808 | tf_op jit(solution)/shard_map/ppermute | solution.py:45
  6.8 4.9 %copy-start = (bf16[640,1600]{0,1:T(8,128)(2,1)S(1)}, bf16[640,1600]{0,1:T(8,128)(2,1)}, u32[]{:S(2)}) copy-start(bf16[640,1600]{0,1:T(8,128)(2,1)} %param.14) | copy-start | bytes 6144004
  6.8 4.9 %copy-start.3 = (bf16[256,640]{1,0:T(8,128)(2,1)S(1)}, bf16[256,640]{1,0:T(8,128)(2,1)}, u32[]{:S(2)}) copy-start(bf16[256,640]{1,0:T(8,128)(2,1)} %refs_0_.1) | copy-start | bytes 983044
  8.4 9.2 %collective-permute-start = (bf16[32,6400]{1,0:T(8,128)(2,1)S(1)}, bf16[32,6400]{1,0:T(8,128)(2,1)S(1)}, u32[]{:S(2)}, u32[]{:S(2)}) collective-permute-start(bf16[32,6400]{1,0:T(8,128)(2,1)S(1)} %get-tuple-element.82), channel_id=1, source_target_pairs={{0,8},{1,33},{2,10},{3,35},{4,12},{5,37},{6,14},{7,39},{8,16},{9,4... | collective-permute-start | bytes 1228808 | tf_op jit(solution)/shard_map/ppermute | solution.py:45
  8.8 8.8 %collective-permute-start.1 = (bf16[32,6400]{1,0:T(8,128)(2,1)S(1)}, bf16[32,6400]{1,0:T(8,128)(2,1)S(1)}, u32[]{:S(2)}, u32[]{:S(2)}) collective-permute-start(bf16[32,6400]{1,0:T(8,128)(2,1)S(1)} %get-tuple-element.83), channel_id=1, source_target_pairs={{0,24},{1,97},{2,26},{3,99},{4,28},{5,101},{6,30},{7,103},{8,0},{9... | collective-permute-start | bytes 1228808 | tf_op jit(solution)/shard_map/ppermute | solution.py:45
  12.8 5.1 %collective-permute-start.5 = (bf16[128,1600]{1,0:T(8,128)(2,1)S(1)}, bf16[128,1600]{1,0:T(8,128)(2,1)S(1)}, u32[]{:S(2)}, u32[]{:S(2)}) collective-permute-start(bf16[128,1600]{1,0:T(8,128)(2,1)S(1)} %get-tuple-element.94), channel_id=1, source_target_pairs={{0,1},{1,0},{2,3},{3,2},{4,5},{5,4},{6,7},{7,6},{8,9},{9,8},{10,11... | collective-permute-start | bytes 1228808 | tf_op jit(solution)/shard_map/ppermute | solution.py:69
  13.3 9.2 %collective-permute-start.4 = (bf16[32,6400]{1,0:T(8,128)(2,1)S(1)}, bf16[32,6400]{1,0:T(8,128)(2,1)S(1)}, u32[]{:S(2)}, u32[]{:S(2)}) collective-permute-start(bf16[32,6400]{1,0:T(8,128)(2,1)S(1)} %get-tuple-element.92), channel_id=1, source_target_pairs={{0,8},{1,33},{2,10},{3,35},{4,12},{5,37},{6,14},{7,39},{8,16},{9,4... | collective-permute-start | bytes 1228808 | tf_op jit(solution)/shard_map/ppermute | solution.py:45
  14.8 9.4 %collective-permute-start.8 = (bf16[32,6400]{1,0:T(8,128)(2,1)S(1)}, bf16[32,6400]{1,0:T(8,128)(2,1)S(1)}, u32[]{:S(2)}, u32[]{:S(2)}) collective-permute-start(bf16[32,6400]{1,0:T(8,128)(2,1)S(1)} %get-tuple-element.102), channel_id=1, source_target_pairs={{0,24},{1,97},{2,26},{3,99},{4,28},{5,101},{6,30},{7,103},{8,0},{9... | collective-permute-start | bytes 1228808 | tf_op jit(solution)/shard_map/ppermute | solution.py:45
  17.8 10.2 %copy-start.1 = (f32[32,1600]{1,0:T(8,128)S(1)}, f32[32,1600]{1,0:T(8,128)}, u32[]{:S(2)}) copy-start(f32[32,1600]{1,0:T(8,128)} %refs_6_.3) | copy-start | bytes 614404
  17.8 10.2 %copy-start.2 = (f32[32,1600]{1,0:T(8,128)S(1)}, f32[32,1600]{1,0:T(8,128)}, u32[]{:S(2)}) copy-start(f32[32,1600]{1,0:T(8,128)} %refs_7_.1) | copy-start | bytes 614404
  18.0 10.1 %collective-permute-start.7 = (bf16[64,1600]{1,0:T(8,128)(2,1)S(1)}, bf16[64,1600]{1,0:T(8,128)(2,1)S(1)}, u32[]{:S(2)}, u32[]{:S(2)}) collective-permute-start(bf16[64,1600]{1,0:T(8,128)(2,1)S(1)} %get-tuple-element.100), channel_id=1, source_target_pairs={{0,2},{2,0},{4,6},{6,4},{1,3},{3,1},{5,7},{7,5},{8,10},{10,8},{12,... | collective-permute-start | bytes 614408 | tf_op jit(solution)/shard_map/ppermute | solution.py:65
  22.5 10.8 %copy-start.4 = (f32[16,3200]{1,0:T(8,128)S(1)}, f32[16,3200]{1,0:T(8,128)}, u32[]{:S(2)}) copy-start(f32[16,3200]{1,0:T(8,128)} %refs_2_.5) | copy-start | bytes 614404
  22.5 10.8 %copy-start.5 = (f32[16,3200]{1,0:T(8,128)S(1)}, f32[16,3200]{1,0:T(8,128)}, u32[]{:S(2)}) copy-start(f32[16,3200]{1,0:T(8,128)} %refs_3_.7) | copy-start | bytes 614404
  22.5 10.8 %copy-start.6 = (f32[16,3200]{1,0:T(8,128)S(1)}, f32[16,3200]{1,0:T(8,128)}, u32[]{:S(2)}) copy-start(f32[16,3200]{1,0:T(8,128)} %refs_4_.3) | copy-start | bytes 614404
  22.5 10.8 %copy-start.7 = (f32[16,3200]{1,0:T(8,128)S(1)}, f32[16,3200]{1,0:T(8,128)}, u32[]{:S(2)}) copy-start(f32[16,3200]{1,0:T(8,128)} %refs_5_.3) | copy-start | bytes 614404
  22.6 9.7 %collective-permute-start.6 = (bf16[16,6400]{1,0:T(8,128)(2,1)S(1)}, bf16[16,6400]{1,0:T(8,128)(2,1)S(1)}, u32[]{:S(2)}, u32[]{:S(2)}) collective-permute-start(bf16[16,6400]{1,0:T(8,128)(2,1)S(1)} %get-tuple-element.98), channel_id=1, source_target_pairs={{0,32},{1,9},{2,34},{3,11},{4,36},{5,13},{6,38},{7,15},{8,40},{9,1... | collective-permute-start | bytes 614408 | tf_op jit(solution)/shard_map/ppermute | solution.py:45
  24.3 8.0 %collective-permute-start.9 = (bf16[16,6400]{1,0:T(8,128)(2,1)S(1)}, bf16[16,6400]{1,0:T(8,128)(2,1)S(1)}, u32[]{:S(2)}, u32[]{:S(2)}) collective-permute-start(bf16[16,6400]{1,0:T(8,128)(2,1)S(1)} %get-tuple-element.107), channel_id=1, source_target_pairs={{0,96},{1,25},{2,98},{3,27},{4,100},{5,29},{6,102},{7,31},{8,104},... | collective-permute-start | bytes 614408 | tf_op jit(solution)/shard_map/ppermute | solution.py:45
  26.0 7.3 %collective-permute-start.10 = (bf16[16,6400]{1,0:T(8,128)(2,1)S(1)}, bf16[16,6400]{1,0:T(8,128)(2,1)S(1)}, u32[]{:S(2)}, u32[]{:S(2)}) collective-permute-start(bf16[16,6400]{1,0:T(8,128)(2,1)S(1)} %get-tuple-element.108), channel_id=1, source_target_pairs={{0,64},{1,17},{2,66},{3,19},{4,68},{5,21},{6,70},{7,23},{8,72},{9,... | collective-permute-start | bytes 614408 | tf_op jit(solution)/shard_map/ppermute | solution.py:45
  28.1 11.8 %collective-permute-start.13 = (bf16[128,1600]{1,0:T(8,128)(2,1)S(1)}, bf16[128,1600]{1,0:T(8,128)(2,1)S(1)}, u32[]{:S(2)}, u32[]{:S(2)}) collective-permute-start(bf16[128,1600]{1,0:T(8,128)(2,1)S(1)} %get-tuple-element.116), channel_id=1, source_target_pairs={{0,6},{6,0},{2,4},{4,2},{1,7},{7,1},{3,5},{5,3},{8,14},{14,8},{10,... | collective-permute-start | bytes 1228808 | tf_op jit(solution)/shard_map/ppermute | solution.py:65
  34.0 3.9 %collective-permute-start.11 = (bf16[4,3200]{1,0:T(4,128)(2,1)S(1)}, bf16[4,3200]{1,0:T(4,128)(2,1)S(1)}, u32[]{:S(2)}, u32[]{:S(2)}) collective-permute-start(bf16[4,3200]{1,0:T(4,128)(2,1)S(1)} %get-tuple-element.111), channel_id=1, source_target_pairs={{0,32},{1,9},{2,34},{3,11},{4,36},{5,13},{6,38},{7,15},{8,40},{9,1... | collective-permute-start | bytes 76808 | tf_op jit(solution)/shard_map/ppermute | solution.py:60
  38.0 5.1 %collective-permute-start.12 = (bf16[4,3200]{1,0:T(4,128)(2,1)S(1)}, bf16[4,3200]{1,0:T(4,128)(2,1)S(1)}, u32[]{:S(2)}, u32[]{:S(2)}) collective-permute-start(bf16[4,3200]{1,0:T(4,128)(2,1)S(1)} %get-tuple-element.114), channel_id=1, source_target_pairs={{0,96},{1,25},{2,98},{3,27},{4,100},{5,29},{6,102},{7,31},{8,104},... | collective-permute-start | bytes 76808 | tf_op jit(solution)/shard_map/ppermute | solution.py:60
  40.6 3.9 %collective-permute-start.15 = (bf16[8,1600]{1,0:T(8,128)(2,1)S(1)}, bf16[8,1600]{1,0:T(8,128)(2,1)S(1)}, u32[]{:S(2)}, u32[]{:S(2)}) collective-permute-start(bf16[8,1600]{1,0:T(8,128)(2,1)S(1)} %get-tuple-element.124), channel_id=1, source_target_pairs={{0,2},{2,0},{4,6},{6,4},{1,3},{3,1},{5,7},{7,5},{8,10},{10,8},{12,... | collective-permute-start | bytes 76808 | tf_op jit(solution)/shard_map/ppermute | solution.py:65
  43.1 3.9 %collective-permute-start.14 = (bf16[4,3200]{1,0:T(4,128)(2,1)S(1)}, bf16[4,3200]{1,0:T(4,128)(2,1)S(1)}, u32[]{:S(2)}, u32[]{:S(2)}) collective-permute-start(bf16[4,3200]{1,0:T(4,128)(2,1)S(1)} %get-tuple-element.120), channel_id=1, source_target_pairs={{0,8},{1,33},{2,10},{3,35},{4,12},{5,37},{6,14},{7,39},{8,0},{9,41... | collective-permute-start | bytes 76808 | tf_op jit(solution)/shard_map/ppermute | solution.py:60
  44.5 5.5 %collective-permute-start.17 = (bf16[8,1600]{1,0:T(8,128)(2,1)S(1)}, bf16[8,1600]{1,0:T(8,128)(2,1)S(1)}, u32[]{:S(2)}, u32[]{:S(2)}) collective-permute-start(bf16[8,1600]{1,0:T(8,128)(2,1)S(1)} %get-tuple-element.131), channel_id=1, source_target_pairs={{0,1},{1,0},{2,3},{3,2},{4,5},{5,4},{6,7},{7,6},{8,9},{9,8},{10,11... | collective-permute-start | bytes 76808 | tf_op jit(solution)/shard_map/ppermute | solution.py:69
  47.0 5.1 %collective-permute-start.16 = (bf16[4,3200]{1,0:T(4,128)(2,1)S(1)}, bf16[4,3200]{1,0:T(4,128)(2,1)S(1)}, u32[]{:S(2)}, u32[]{:S(2)}) collective-permute-start(bf16[4,3200]{1,0:T(4,128)(2,1)S(1)} %get-tuple-element.129), channel_id=1, source_target_pairs={{0,24},{1,97},{2,26},{3,99},{4,28},{5,101},{6,30},{7,103},{8,16},{... | collective-permute-start | bytes 76808 | tf_op jit(solution)/shard_map/ppermute | solution.py:60

commit v7 on v6

--- a/solution.py
+++ b/solution.py
@@ -186,9 +186,8 @@
             keep[:, to] = part[128:]
 
 
-def pass_kernel(near, from_below, far, from_above, onward, backward):
-    onward[...] = wide(near[...], from_below[...]).astype(BF16)
-    backward[...] = wide(far[...], from_above[...]).astype(BF16)
+def pass_kernel(own, arrived, onward):
+    onward[...] = wide(own[...], arrived[...]).astype(BF16)
 
 
 def collect_kernel(keep, high_below, low_above, low, high):
@@ -346,8 +345,10 @@
     high_below, low_above = ring_send(forth, 1, 0), ring_send(back, 3, 0)
     own_down, other_down = run(down_kernel, (pltpu.VMEM((128, 1600), BF16),) * 2, proj_down, down)
     other_down = core_send(other_down)
-    forth, back = run(pass_kernel, (half, half), near, from_below, far, from_above)
-    low_below, high_above = ring_send(forth, 1, 0), ring_send(back, 3, 0)
+    (forth,) = run(pass_kernel, (half,), near, from_below)
+    low_below = ring_send(forth, 1, 0)
+    (back,) = run(pass_kernel, (half,), far, from_above)
+    high_above = ring_send(back, 3, 0)
     low, high = run(collect_kernel, (pltpu.VMEM((32, 6400), F32),) * 2, keep, high_below, low_above)
     own_down, other_down = run(
         down_split_kernel, (pltpu.VMEM((64, 1600), F32), pltpu.VMEM((64, 1600), BF16)), own_down, other_down

time: 54.7 us -> 54.6 us (level)
    pallas_call x19 -> x20, Pallas kernels: 13.1 us -> 13 us  [__call__(): pl.pallas_call(kernel, name=body.__name__, out_shape=[*outs, *token_out],...]
  transfers between devices with their start and end apart: 18 -> 18, of which waited for: 9 -> 8; matrix products, arithmetic and copies ran while one was open for 0% -> 0% of each run, Pallas kernels for 15% -> 15%
where the time goes in v7:
time: 54.6 us; the launch traced here: 54.3 us
  starting transfers between devices  31.3 us (57%)
  Pallas kernels  13 us (24%)
  waiting for transfers between devices  9.05 us (17%)
  between operations  0.81 us (1%)
    ppermute x9, starting transfers between devices, ring_send(): return lax.ppermute(value, AXES, ring_pairs(shift, stage))  15.4 us
    pallas_call x20, Pallas kernels, __call__(): pl.pallas_call(kernel, name=body.__name__, out_shape=[*outs, *token_out],...  13 us
    ppermute x3, starting transfers between devices, z_swap(): return lax.ppermute(value, 'z', pairs)  8.27 us
    ppermute x4, starting transfers between devices, ring_swap(): return lax.ppermute(value, AXES, pairs)  7.45 us
    ppermute x9, waiting for transfers between devices, ring_send(): return lax.ppermute(value, AXES, ring_pairs(shift, stage))  4.26 us
    ppermute x4, waiting for transfers between devices, ring_swap(): return lax.ppermute(value, AXES, pairs)  4.19 us
  transfers between devices with their start and end apart: 18, of which 8 were waited for; matrix products, arithmetic and copies ran while one was open for 0% of the time, Pallas kernels for 15%

profile of v7, /device:TPU:0, one launch (start us, length us, event | category | flops | bytes accessed | tf_op | source)
XLA Modules:
  0.0 54.3 jit_solution(11899071206274583219)
XLA Ops:
  0.6 2.8 %first_kernel.1 = (bf16[32,6400]{1,0:T(8,128)(2,1)S(1)}, bf16[32,6400]{1,0:T(8,128)(2,1)S(1)}, bf16[192,320]{1,0:T(8,128)(2,1)S(1)}, bf16[192,320]{1,0:T(8,128)(...) custom-call(bf16[320,256]{1,0:T(8,128)(2,1)} %bitcast.12, ...), custom_call_target="tpu_custom_call" | custom-call | tf_op jit(solution)/shard_map/first_kernel/pallas_call | solution.py:99
  3.5 1.6 %collective-permute-start.3 = (bf16[32,6400]{1,0:T(8,128)(2,1)S(1)}, bf16[32,6400]{1,0:T(8,128)(2,1)S(1)}, u32[]{:S(2)}, u32[]{:S(2)}) collective-permute-start(bf16[32,6400]{1,0:T(8,128)(2,1)S(1)} %get-tuple-element.88), channel_id=1, source_target_pairs={{0,8},{1,33},{2,10},{3,35},{4,12},{5,37},{6,14},{7,39},{8,16},{9,4... | collective-permute-start | bytes 1228808 | tf_op jit(solution)/shard_map/ppermute | solution.py:45
  5.1 1.7 %collective-permute-start.2 = (bf16[32,6400]{1,0:T(8,128)(2,1)S(1)}, bf16[32,6400]{1,0:T(8,128)(2,1)S(1)}, u32[]{:S(2)}, u32[]{:S(2)}) collective-permute-start(bf16[32,6400]{1,0:T(8,128)(2,1)S(1)} %get-tuple-element.86), channel_id=1, source_target_pairs={{0,24},{1,97},{2,26},{3,99},{4,28},{5,101},{6,30},{7,103},{8,0},{9... | collective-permute-start | bytes 1228808 | tf_op jit(solution)/shard_map/ppermute | solution.py:45
  6.8 1.6 %rest_kernel.1 = (bf16[32,6400]{1,0:T(8,128)(2,1)S(1)}, bf16[32,6400]{1,0:T(8,128)(2,1)S(1)}, bf16[32,6400]{1,0:T(8,128)(2,1)S(1)}, bf16[32,6400]{1,0:T(8,128)(2...) custom-call(bf16[192,320]{1,0:T(8,128)(2,1)S(1)} %get-tuple-element.79.refs_0_, ...), custom_call_target="tpu_custom_call" | custom-call | tf_op jit(solution)/shard_map/rest_kernel/pallas_call | solution.py:99
  8.4 0.4 collective-permute-start
  8.8 2.9 %collective-permute-start.1 = (bf16[32,6400]{1,0:T(8,128)(2,1)S(1)}, bf16[32,6400]{1,0:T(8,128)(2,1)S(1)}, u32[]{:S(2)}, u32[]{:S(2)}) collective-permute-start(bf16[32,6400]{1,0:T(8,128)(2,1)S(1)} %get-tuple-element.84), channel_id=1, source_target_pairs={{0,24},{1,97},{2,26},{3,99},{4,28},{5,101},{6,30},{7,103},{8,0},{9... | collective-permute-start | bytes 1228808 | tf_op jit(solution)/shard_map/ppermute | solution.py:45
  11.7 1.1 %down_kernel.1 = (bf16[128,1600]{1,0:T(8,128)(2,1)S(1)}, bf16[128,1600]{1,0:T(8,128)(2,1)S(1)}, f32[8,128]{1,0:T(8,128)S(1)}) custom-call(bf16[256,640]{1,0:T(8,128)(2,1)S(1)} %copy-done.3, bf16[1600,640]{1,0:T(8,128)(2,1)S(1)} %bitcast.8, f32[8,128]{1,0:T(8,128)S(1)} %get-tuple-element.89.refs_2_), custom_call_target="tpu_custom_call" | custom-call | tf_op jit(solution)/shard_map/down_kernel/pallas_call | solution.py:99
  12.8 0.1 collective-permute-start.5
  12.9 0.0 collective-permute-done.3.refs_1_
  12.9 0.1 pass_kernel.2
  13.0 0.5 collective-permute-start.4
  13.5 0.0 collective-permute-done.2.refs_1_
  13.5 0.1 pass_kernel.3
  13.6 2.9 %collective-permute-start.8 = (bf16[32,6400]{1,0:T(8,128)(2,1)S(1)}, bf16[32,6400]{1,0:T(8,128)(2,1)S(1)}, u32[]{:S(2)}, u32[]{:S(2)}) collective-permute-start(bf16[32,6400]{1,0:T(8,128)(2,1)S(1)} %get-tuple-element.104), channel_id=1, source_target_pairs={{0,24},{1,97},{2,26},{3,99},{4,28},{5,101},{6,30},{7,103},{8,0},{9... | collective-permute-start | bytes 1228808 | tf_op jit(solution)/shard_map/ppermute | solution.py:45
  16.5 1.1 %collective-permute-done.refs_1_ = bf16[32,6400]{1,0:T(8,128)(2,1)S(1)} collective-permute-done((bf16[32,6400]{1,0:T(8,128)(2,1)S(1)}, bf16[32,6400]{1,0:T(8,128)(2,1)S(1)}, u32[]{:S(2)}, u32[]{:S(2)}) %collective-permute-start) | collective-permute-done | bytes 409632 | tf_op jit(solution)/shard_map/ppermute | solution.py:45
  17.6 0.0 collective-permute-done.1.refs_2_
  17.6 0.2 collect_kernel.1
  17.8 0.0 copy-start.1
  17.8 0.0 copy-start.2
  17.8 0.1 down_split_kernel.1
  18.0 2.1 %collective-permute-start.7 = (bf16[64,1600]{1,0:T(8,128)(2,1)S(1)}, bf16[64,1600]{1,0:T(8,128)(2,1)S(1)}, u32[]{:S(2)}, u32[]{:S(2)}) collective-permute-start(bf16[64,1600]{1,0:T(8,128)(2,1)S(1)} %get-tuple-element.102), channel_id=1, source_target_pairs={{0,2},{2,0},{4,6},{6,4},{1,3},{3,1},{5,7},{7,5},{8,10},{10,8},{12,... | collective-permute-start | bytes 614408 | tf_op jit(solution)/shard_map/ppermute | solution.py:65
  20.0 2.2 %collective-permute-done.4.refs_1_ = bf16[32,6400]{1,0:T(8,128)(2,1)S(1)} collective-permute-done((bf16[32,6400]{1,0:T(8,128)(2,1)S(1)}, bf16[32,6400]{1,0:T(8,128)(2,1)S(1)}, u32[]{:S(2)}, u32[]{:S(2)}) %collective-permute-start.4) | collective-permute-done | bytes 409632 | tf_op jit(solution)/shard_map/ppermute | solution.py:45
  22.2 0.1 near_kernel.1
  22.3 1.7 %collective-permute-start.6 = (bf16[16,6400]{1,0:T(8,128)(2,1)S(1)}, bf16[16,6400]{1,0:T(8,128)(2,1)S(1)}, u32[]{:S(2)}, u32[]{:S(2)}) collective-permute-start(bf16[16,6400]{1,0:T(8,128)(2,1)S(1)} %get-tuple-element.100), channel_id=1, source_target_pairs={{0,32},{1,9},{2,34},{3,11},{4,36},{5,13},{6,38},{7,15},{8,40},{9,1... | collective-permute-start | bytes 614408 | tf_op jit(solution)/shard_map/ppermute | solution.py:45
  24.1 0.1 far_kernel.1
  24.1 1.6 %collective-permute-start.9 = (bf16[16,6400]{1,0:T(8,128)(2,1)S(1)}, bf16[16,6400]{1,0:T(8,128)(2,1)S(1)}, u32[]{:S(2)}, u32[]{:S(2)}) collective-permute-start(bf16[16,6400]{1,0:T(8,128)(2,1)S(1)} %get-tuple-element.109), channel_id=1, source_target_pairs={{0,96},{1,25},{2,98},{3,27},{4,100},{5,29},{6,102},{7,31},{8,104},... | collective-permute-start | bytes 614408 | tf_op jit(solution)/shard_map/ppermute | solution.py:45
  25.8 2.1 %collective-permute-start.10 = (bf16[16,6400]{1,0:T(8,128)(2,1)S(1)}, bf16[16,6400]{1,0:T(8,128)(2,1)S(1)}, u32[]{:S(2)}, u32[]{:S(2)}) collective-permute-start(bf16[16,6400]{1,0:T(8,128)(2,1)S(1)} %get-tuple-element.110), channel_id=1, source_target_pairs={{0,64},{1,17},{2,66},{3,19},{4,68},{5,21},{6,70},{7,23},{8,72},{9,... | collective-permute-start | bytes 614408 | tf_op jit(solution)/shard_map/ppermute | solution.py:45
  27.8 0.0 collective-permute-done.7.refs_1_
  27.9 0.1 down_halve_kernel.1
  28.0 4.1 %collective-permute-start.13 = (bf16[128,1600]{1,0:T(8,128)(2,1)S(1)}, bf16[128,1600]{1,0:T(8,128)(2,1)S(1)}, u32[]{:S(2)}, u32[]{:S(2)}) collective-permute-start(bf16[128,1600]{1,0:T(8,128)(2,1)S(1)} %get-tuple-element.118), channel_id=1, source_target_pairs={{0,6},{6,0},{2,4},{4,2},{1,7},{7,1},{3,5},{5,3},{8,14},{14,8},{10,... | collective-permute-start | bytes 1228808 | tf_op jit(solution)/shard_map/ppermute | solution.py:65
  32.1 0.9 %collective-permute-done.10.refs_2_ = bf16[16,6400]{1,0:T(8,128)(2,1)S(1)} collective-permute-done((bf16[16,6400]{1,0:T(8,128)(2,1)S(1)}, bf16[16,6400]{1,0:T(8,128)(2,1)S(1)}, u32[]{:S(2)}, u32[]{:S(2)}) %collective-permute-start.10) | collective-permute-done | bytes 204832 | tf_op jit(solution)/shard_map/ppermute | solution.py:45
  33.1 0.7 %pair_sum_kernel.1 = (f32[4,3200]{1,0:T(4,128)S(1)}, bf16[4,3200]{1,0:T(4,128)(2,1)S(1)}, f32[16,6400]{1,0:T(8,128)S(1)}, f32[8,128]{1,0:T(8,128)S(1)}) custom-call(f32[16,6400]{1,0:T(8,128)S(1)} %get-tuple-element.108.refs_0_, bf16[16,6400]{1,0:T(8,128)(2,1)S(1)} %collective-permute-done.9.refs_1_, bf16[16,6400]{1,0:T(8,128)(2,1)S(1)} %collective-permute-done.10.refs_2_, ...), custom_call_target="tpu_custom_call" | custom-call | flops 8000000000 | tf_op jit(solution)/shard_map/pair_sum_kernel/pallas_call | solution.py:99
  33.8 1.5 %collective-permute-start.11 = (bf16[4,3200]{1,0:T(4,128)(2,1)S(1)}, bf16[4,3200]{1,0:T(4,128)(2,1)S(1)}, u32[]{:S(2)}, u32[]{:S(2)}) collective-permute-start(bf16[4,3200]{1,0:T(4,128)(2,1)S(1)} %get-tuple-element.113), channel_id=1, source_target_pairs={{0,32},{1,9},{2,34},{3,11},{4,36},{5,13},{6,38},{7,15},{8,40},{9,1... | collective-permute-start | bytes 76808 | tf_op jit(solution)/shard_map/ppermute | solution.py:60
  35.2 2.4 %collective-permute-done.11.refs_1_ = bf16[4,3200]{1,0:T(4,128)(2,1)S(1)} collective-permute-done((bf16[4,3200]{1,0:T(4,128)(2,1)S(1)}, bf16[4,3200]{1,0:T(4,128)(2,1)S(1)}, u32[]{:S(2)}, u32[]{:S(2)}) %collective-permute-start.11) | collective-permute-done | bytes 25632 | tf_op jit(solution)/shard_map/ppermute | solution.py:60
  37.7 2.0 %collective-permute-start.12 = (bf16[4,3200]{1,0:T(4,128)(2,1)S(1)}, bf16[4,3200]{1,0:T(4,128)(2,1)S(1)}, u32[]{:S(2)}, u32[]{:S(2)}) collective-permute-start(bf16[4,3200]{1,0:T(4,128)(2,1)S(1)} %get-tuple-element.116), channel_id=1, source_target_pairs={{0,96},{1,25},{2,98},{3,27},{4,100},{5,29},{6,102},{7,31},{8,104},... | collective-permute-start | bytes 76808 | tf_op jit(solution)/shard_map/ppermute | solution.py:60
  39.7 0.6 %down_sum_kernel.1 = (f32[8,1600]{1,0:T(8,128)S(1)}, bf16[8,1600]{1,0:T(8,128)(2,1)S(1)}, f32[32,1600]{1,0:T(8,128)S(1)}, f32[8,128]{1,0:T(8,128)S(1)}) custom-call(f32[64,1600]{1,0:T(8,128)S(1)} %get-tuple-element.117.refs_0_, bf16[128,1600]{1,0:T(8,128)(2,1)S(1)} %collective-permute-done.13.refs_1_, f32[32,1600]{1,0:T(8,128)S(1)} %copy-done.1, ...), custom_call_target="tpu_custom_call" | custom-call | tf_op jit(solution)/shard_map/down_sum_kernel/pallas_call | solution.py:99
  40.3 2.1 %collective-permute-start.15 = (bf16[8,1600]{1,0:T(8,128)(2,1)S(1)}, bf16[8,1600]{1,0:T(8,128)(2,1)S(1)}, u32[]{:S(2)}, u32[]{:S(2)}) collective-permute-start(bf16[8,1600]{1,0:T(8,128)(2,1)S(1)} %get-tuple-element.126), channel_id=1, source_target_pairs={{0,2},{2,0},{4,6},{6,4},{1,3},{3,1},{5,7},{7,5},{8,10},{10,8},{12,... | collective-permute-start | bytes 76808 | tf_op jit(solution)/shard_map/ppermute | solution.py:65
  42.4 0.4 collective-permute-done.12.refs_1_
  42.8 0.8 %collective-permute-start.14 = (bf16[4,3200]{1,0:T(4,128)(2,1)S(1)}, bf16[4,3200]{1,0:T(4,128)(2,1)S(1)}, u32[]{:S(2)}, u32[]{:S(2)}) collective-permute-start(bf16[4,3200]{1,0:T(4,128)(2,1)S(1)} %get-tuple-element.122), channel_id=1, source_target_pairs={{0,8},{1,33},{2,10},{3,35},{4,12},{5,37},{6,14},{7,39},{8,0},{9,41... | collective-permute-start | bytes 76808 | tf_op jit(solution)/shard_map/ppermute | solution.py:60
  43.6 0.6 %collective-permute-done.15.refs_1_ = bf16[8,1600]{1,0:T(8,128)(2,1)S(1)} collective-permute-done((bf16[8,1600]{1,0:T(8,128)(2,1)S(1)}, bf16[8,1600]{1,0:T(8,128)(2,1)S(1)}, u32[]{:S(2)}, u32[]{:S(2)}) %collective-permute-start.15) | collective-permute-done | bytes 25632 | tf_op jit(solution)/shard_map/ppermute | solution.py:65
  44.2 0.1 collective-permute-start.17
  44.3 1.2 %moment_kernel.1 = (f32[16,3200]{1,0:T(8,128)}, f32[16,3200]{1,0:T(8,128)}, f32[16,3200]{1,0:T(8,128)}, f32[16,3200]{1,0:T(8,128)}, f32[32,1600]{1,0:T(8,128)}, ...) custom-call(f32[16,6400]{1,0:T(8,128)S(1)} %get-tuple-element.123.refs_0_, f32[32,1600]{1,0:T(8,128)S(1)} %get-tuple-element.124.refs_1_, ...), custom_call_target="tpu_custom_call" | custom-call | tf_op jit(solution)/shard_map/moment_kernel/pallas_call | solution.py:99
  45.6 1.2 %collective-permute-done.14.refs_1_ = bf16[4,3200]{1,0:T(4,128)(2,1)S(1)} collective-permute-done((bf16[4,3200]{1,0:T(4,128)(2,1)S(1)}, bf16[4,3200]{1,0:T(4,128)(2,1)S(1)}, u32[]{:S(2)}, u32[]{:S(2)}) %collective-permute-start.14) | collective-permute-done | bytes 25632 | tf_op jit(solution)/shard_map/ppermute | solution.py:60
  46.8 3.2 %collective-permute-start.16 = (bf16[4,3200]{1,0:T(4,128)(2,1)S(1)}, bf16[4,3200]{1,0:T(4,128)(2,1)S(1)}, u32[]{:S(2)}, u32[]{:S(2)}) collective-permute-start(bf16[4,3200]{1,0:T(4,128)(2,1)S(1)} %get-tuple-element.131), channel_id=1, source_target_pairs={{0,24},{1,97},{2,26},{3,99},{4,28},{5,101},{6,30},{7,103},{8,16},{... | collective-permute-start | bytes 76808 | tf_op jit(solution)/shard_map/ppermute | solution.py:60
  50.0 0.0 collective-permute-done.17.refs_2_
  50.0 1.8 %down_update_kernel.1 = (bf16[1600,640]{1,0:T(8,128)(2,1)}, f32[8,128]{1,0:T(8,128)S(1)}) custom-call(bf16[1600,640]{1,0:T(8,128)(2,1)S(1)} %bitcast.9, f32[8,1600]{1,0:T(8,128)S(1)} %get-tuple-element.132.refs_1_, bf16[8,1600]{1,0:T(8,128)(2,1)S(1)} %collective-permute-done.17.refs_2_, f32[8,128]{1,0:T(8,128)S(1)} %get-tuple-element.134.refs_3_), custom_call_target="tpu_custom_call" | custom-call | tf_op jit(solution)/shard_map/down_update_kernel/pallas_call | solution.py:99
  51.8 0.1 collective-permute-done.16.refs_3_
  51.9 2.4 %update_kernel.1 = (bf16[320,3200]{1,0:T(8,128)(2,1)}, bf16[320,3200]{1,0:T(8,128)(2,1)}) custom-call(bf16[320,3200]{1,0:T(8,128)(2,1)S(1)} %get-tuple-element.77.refs_1_.refs_0_, bf16[320,3200]{1,0:T(8,128)(2,1)S(1)} %get-tuple-element.78.refs_3_.refs_1_, f32[4,3200]{1,0:T(4,128)S(1)} %get-tuple-element.130.refs_2_, ...), custom_call_target="tpu_custom_call" | custom-call | tf_op jit(solution)/shard_map/update_kernel/pallas_call | solution.py:99
  (24 shorter events, 0.1 us)
Async XLA Ops:
  3.5 9.4 %collective-permute-start.3 = (bf16[32,6400]{1,0:T(8,128)(2,1)S(1)}, bf16[32,6400]{1,0:T(8,128)(2,1)S(1)}, u32[]{:S(2)}, u32[]{:S(2)}) collective-permute-start(bf16[32,6400]{1,0:T(8,128)(2,1)S(1)} %get-tuple-element.88), channel_id=1, source_target_pairs={{0,8},{1,33},{2,10},{3,35},{4,12},{5,37},{6,14},{7,39},{8,16},{9,4... | collective-permute-start | bytes 1228808 | tf_op jit(solution)/shard_map/ppermute | solution.py:45
  5.1 8.4 %collective-permute-start.2 = (bf16[32,6400]{1,0:T(8,128)(2,1)S(1)}, bf16[32,6400]{1,0:T(8,128)(2,1)S(1)}, u32[]{:S(2)}, u32[]{:S(2)}) collective-permute-start(bf16[32,6400]{1,0:T(8,128)(2,1)S(1)} %get-tuple-element.86), channel_id=1, source_target_pairs={{0,24},{1,97},{2,26},{3,99},{4,28},{5,101},{6,30},{7,103},{8,0},{9... | collective-permute-start | bytes 1228808 | tf_op jit(solution)/shard_map/ppermute | solution.py:45
  6.8 4.9 %copy-start = (bf16[640,1600]{0,1:T(8,128)(2,1)S(1)}, bf16[640,1600]{0,1:T(8,128)(2,1)}, u32[]{:S(2)}) copy-start(bf16[640,1600]{0,1:T(8,128)(2,1)} %param.14) | copy-start | bytes 6144004
  6.8 4.9 %copy-start.3 = (bf16[256,640]{1,0:T(8,128)(2,1)S(1)}, bf16[256,640]{1,0:T(8,128)(2,1)}, u32[]{:S(2)}) copy-start(bf16[256,640]{1,0:T(8,128)(2,1)} %refs_0_.1) | copy-start | bytes 983044
  8.4 9.2 %collective-permute-start = (bf16[32,6400]{1,0:T(8,128)(2,1)S(1)}, bf16[32,6400]{1,0:T(8,128)(2,1)S(1)}, u32[]{:S(2)}, u32[]{:S(2)}) collective-permute-start(bf16[32,6400]{1,0:T(8,128)(2,1)S(1)} %get-tuple-element.83), channel_id=1, source_target_pairs={{0,8},{1,33},{2,10},{3,35},{4,12},{5,37},{6,14},{7,39},{8,16},{9,4... | collective-permute-start | bytes 1228808 | tf_op jit(solution)/shard_map/ppermute | solution.py:45
  8.8 8.8 %collective-permute-start.1 = (bf16[32,6400]{1,0:T(8,128)(2,1)S(1)}, bf16[32,6400]{1,0:T(8,128)(2,1)S(1)}, u32[]{:S(2)}, u32[]{:S(2)}) collective-permute-start(bf16[32,6400]{1,0:T(8,128)(2,1)S(1)} %get-tuple-element.84), channel_id=1, source_target_pairs={{0,24},{1,97},{2,26},{3,99},{4,28},{5,101},{6,30},{7,103},{8,0},{9... | collective-permute-start | bytes 1228808 | tf_op jit(solution)/shard_map/ppermute | solution.py:45
  12.8 5.0 %collective-permute-start.5 = (bf16[128,1600]{1,0:T(8,128)(2,1)S(1)}, bf16[128,1600]{1,0:T(8,128)(2,1)S(1)}, u32[]{:S(2)}, u32[]{:S(2)}) collective-permute-start(bf16[128,1600]{1,0:T(8,128)(2,1)S(1)} %get-tuple-element.96), channel_id=1, source_target_pairs={{0,1},{1,0},{2,3},{3,2},{4,5},{5,4},{6,7},{7,6},{8,9},{9,8},{10,11... | collective-permute-start | bytes 1228808 | tf_op jit(solution)/shard_map/ppermute | solution.py:69
  13.0 9.2 %collective-permute-start.4 = (bf16[32,6400]{1,0:T(8,128)(2,1)S(1)}, bf16[32,6400]{1,0:T(8,128)(2,1)S(1)}, u32[]{:S(2)}, u32[]{:S(2)}) collective-permute-start(bf16[32,6400]{1,0:T(8,128)(2,1)S(1)} %get-tuple-element.94), channel_id=1, source_target_pairs={{0,8},{1,33},{2,10},{3,35},{4,12},{5,37},{6,14},{7,39},{8,16},{9,4... | collective-permute-start | bytes 1228808 | tf_op jit(solution)/shard_map/ppermute | solution.py:45
  13.6 10.5 %collective-permute-start.8 = (bf16[32,6400]{1,0:T(8,128)(2,1)S(1)}, bf16[32,6400]{1,0:T(8,128)(2,1)S(1)}, u32[]{:S(2)}, u32[]{:S(2)}) collective-permute-start(bf16[32,6400]{1,0:T(8,128)(2,1)S(1)} %get-tuple-element.104), channel_id=1, source_target_pairs={{0,24},{1,97},{2,26},{3,99},{4,28},{5,101},{6,30},{7,103},{8,0},{9... | collective-permute-start | bytes 1228808 | tf_op jit(solution)/shard_map/ppermute | solution.py:45
  17.8 10.0 %copy-start.1 = (f32[32,1600]{1,0:T(8,128)S(1)}, f32[32,1600]{1,0:T(8,128)}, u32[]{:S(2)}) copy-start(f32[32,1600]{1,0:T(8,128)} %refs_6_.3) | copy-start | bytes 614404
  17.8 10.0 %copy-start.2 = (f32[32,1600]{1,0:T(8,128)S(1)}, f32[32,1600]{1,0:T(8,128)}, u32[]{:S(2)}) copy-start(f32[32,1600]{1,0:T(8,128)} %refs_7_.1) | copy-start | bytes 614404
  18.0 9.9 %collective-permute-start.7 = (bf16[64,1600]{1,0:T(8,128)(2,1)S(1)}, bf16[64,1600]{1,0:T(8,128)(2,1)S(1)}, u32[]{:S(2)}, u32[]{:S(2)}) collective-permute-start(bf16[64,1600]{1,0:T(8,128)(2,1)S(1)} %get-tuple-element.102), channel_id=1, source_target_pairs={{0,2},{2,0},{4,6},{6,4},{1,3},{3,1},{5,7},{7,5},{8,10},{10,8},{12,... | collective-permute-start | bytes 614408 | tf_op jit(solution)/shard_map/ppermute | solution.py:65
  22.2 10.8 %copy-start.4 = (f32[16,3200]{1,0:T(8,128)S(1)}, f32[16,3200]{1,0:T(8,128)}, u32[]{:S(2)}) copy-start(f32[16,3200]{1,0:T(8,128)} %refs_2_.5) | copy-start | bytes 614404
  22.2 10.8 %copy-start.5 = (f32[16,3200]{1,0:T(8,128)S(1)}, f32[16,3200]{1,0:T(8,128)}, u32[]{:S(2)}) copy-start(f32[16,3200]{1,0:T(8,128)} %refs_3_.7) | copy-start | bytes 614404
  22.2 10.8 %copy-start.6 = (f32[16,3200]{1,0:T(8,128)S(1)}, f32[16,3200]{1,0:T(8,128)}, u32[]{:S(2)}) copy-start(f32[16,3200]{1,0:T(8,128)} %refs_4_.3) | copy-start | bytes 614404
  22.2 10.8 %copy-start.7 = (f32[16,3200]{1,0:T(8,128)S(1)}, f32[16,3200]{1,0:T(8,128)}, u32[]{:S(2)}) copy-start(f32[16,3200]{1,0:T(8,128)} %refs_5_.3) | copy-start | bytes 614404
  22.3 9.8 %collective-permute-start.6 = (bf16[16,6400]{1,0:T(8,128)(2,1)S(1)}, bf16[16,6400]{1,0:T(8,128)(2,1)S(1)}, u32[]{:S(2)}, u32[]{:S(2)}) collective-permute-start(bf16[16,6400]{1,0:T(8,128)(2,1)S(1)} %get-tuple-element.100), channel_id=1, source_target_pairs={{0,32},{1,9},{2,34},{3,11},{4,36},{5,13},{6,38},{7,15},{8,40},{9,1... | collective-permute-start | bytes 614408 | tf_op jit(solution)/shard_map/ppermute | solution.py:45
  24.1 8.0 %collective-permute-start.9 = (bf16[16,6400]{1,0:T(8,128)(2,1)S(1)}, bf16[16,6400]{1,0:T(8,128)(2,1)S(1)}, u32[]{:S(2)}, u32[]{:S(2)}) collective-permute-start(bf16[16,6400]{1,0:T(8,128)(2,1)S(1)} %get-tuple-element.109), channel_id=1, source_target_pairs={{0,96},{1,25},{2,98},{3,27},{4,100},{5,29},{6,102},{7,31},{8,104},... | collective-permute-start | bytes 614408 | tf_op jit(solution)/shard_map/ppermute | solution.py:45
  25.8 7.3 %collective-permute-start.10 = (bf16[16,6400]{1,0:T(8,128)(2,1)S(1)}, bf16[16,6400]{1,0:T(8,128)(2,1)S(1)}, u32[]{:S(2)}, u32[]{:S(2)}) collective-permute-start(bf16[16,6400]{1,0:T(8,128)(2,1)S(1)} %get-tuple-element.110), channel_id=1, source_target_pairs={{0,64},{1,17},{2,66},{3,19},{4,68},{5,21},{6,70},{7,23},{8,72},{9,... | collective-permute-start | bytes 614408 | tf_op jit(solution)/shard_map/ppermute | solution.py:45
  28.0 11.7 %collective-permute-start.13 = (bf16[128,1600]{1,0:T(8,128)(2,1)S(1)}, bf16[128,1600]{1,0:T(8,128)(2,1)S(1)}, u32[]{:S(2)}, u32[]{:S(2)}) collective-permute-start(bf16[128,1600]{1,0:T(8,128)(2,1)S(1)} %get-tuple-element.118), channel_id=1, source_target_pairs={{0,6},{6,0},{2,4},{4,2},{1,7},{7,1},{3,5},{5,3},{8,14},{14,8},{10,... | collective-permute-start | bytes 1228808 | tf_op jit(solution)/shard_map/ppermute | solution.py:65
  33.8 3.9 %collective-permute-start.11 = (bf16[4,3200]{1,0:T(4,128)(2,1)S(1)}, bf16[4,3200]{1,0:T(4,128)(2,1)S(1)}, u32[]{:S(2)}, u32[]{:S(2)}) collective-permute-start(bf16[4,3200]{1,0:T(4,128)(2,1)S(1)} %get-tuple-element.113), channel_id=1, source_target_pairs={{0,32},{1,9},{2,34},{3,11},{4,36},{5,13},{6,38},{7,15},{8,40},{9,1... | collective-permute-start | bytes 76808 | tf_op jit(solution)/shard_map/ppermute | solution.py:60
  37.7 5.1 %collective-permute-start.12 = (bf16[4,3200]{1,0:T(4,128)(2,1)S(1)}, bf16[4,3200]{1,0:T(4,128)(2,1)S(1)}, u32[]{:S(2)}, u32[]{:S(2)}) collective-permute-start(bf16[4,3200]{1,0:T(4,128)(2,1)S(1)} %get-tuple-element.116), channel_id=1, source_target_pairs={{0,96},{1,25},{2,98},{3,27},{4,100},{5,29},{6,102},{7,31},{8,104},... | collective-permute-start | bytes 76808 | tf_op jit(solution)/shard_map/ppermute | solution.py:60
  40.3 3.9 %collective-permute-start.15 = (bf16[8,1600]{1,0:T(8,128)(2,1)S(1)}, bf16[8,1600]{1,0:T(8,128)(2,1)S(1)}, u32[]{:S(2)}, u32[]{:S(2)}) collective-permute-start(bf16[8,1600]{1,0:T(8,128)(2,1)S(1)} %get-tuple-element.126), channel_id=1, source_target_pairs={{0,2},{2,0},{4,6},{6,4},{1,3},{3,1},{5,7},{7,5},{8,10},{10,8},{12,... | collective-permute-start | bytes 76808 | tf_op jit(solution)/shard_map/ppermute | solution.py:65
  42.8 3.9 %collective-permute-start.14 = (bf16[4,3200]{1,0:T(4,128)(2,1)S(1)}, bf16[4,3200]{1,0:T(4,128)(2,1)S(1)}, u32[]{:S(2)}, u32[]{:S(2)}) collective-permute-start(bf16[4,3200]{1,0:T(4,128)(2,1)S(1)} %get-tuple-element.122), channel_id=1, source_target_pairs={{0,8},{1,33},{2,10},{3,35},{4,12},{5,37},{6,14},{7,39},{8,0},{9,41... | collective-permute-start | bytes 76808 | tf_op jit(solution)/shard_map/ppermute | solution.py:60
  44.2 5.7 %collective-permute-start.17 = (bf16[8,1600]{1,0:T(8,128)(2,1)S(1)}, bf16[8,1600]{1,0:T(8,128)(2,1)S(1)}, u32[]{:S(2)}, u32[]{:S(2)}) collective-permute-start(bf16[8,1600]{1,0:T(8,128)(2,1)S(1)} %get-tuple-element.133), channel_id=1, source_target_pairs={{0,1},{1,0},{2,3},{3,2},{4,5},{5,4},{6,7},{7,6},{8,9},{9,8},{10,11... | collective-permute-start | bytes 76808 | tf_op jit(solution)/shard_map/ppermute | solution.py:69
  46.8 5.1 %collective-permute-start.16 = (bf16[4,3200]{1,0:T(4,128)(2,1)S(1)}, bf16[4,3200]{1,0:T(4,128)(2,1)S(1)}, u32[]{:S(2)}, u32[]{:S(2)}) collective-permute-start(bf16[4,3200]{1,0:T(4,128)(2,1)S(1)} %get-tuple-element.131), channel_id=1, source_target_pairs={{0,24},{1,97},{2,26},{3,99},{4,28},{5,101},{6,30},{7,103},{8,16},{... | collective-permute-start | bytes 76808 | tf_op jit(solution)/shard_map/ppermute | solution.py:60

commit v8 on v7

--- a/solution.py
+++ b/solution.py
@@ -222,11 +222,24 @@
     return jnp.sum(corrected * corrected, 0, keepdims=True), jnp.sum(projected * projected, 0, keepdims=True)
 
 
-def pair_sum_kernel(own, a, b, first_gate, second_gate, first_up, second_up, sums, sent, total):
+def ready_kernel(own, arrived, first_gate, second_gate, first_up, second_up, total, first, second):
+    total[...] = wide(own[...], arrived[...])
+    for at, old_first, old_second in ((0, first_gate, second_gate), (3200, first_up, second_up)):
+        first[:, at : at + 3200] = old_first[...] * (beta_first / (1.0 - beta_first**STEP))
+        second[:, at : at + 3200] = old_second[...] * (beta_second / (1.0 - beta_second**STEP))
+
+
+def pair_sum_kernel(own, a, b, first, second, sums, sent, total):
     projected = wide(own[...], a[...], b[...])
     total[...] = projected
-    sums[0:1], sums[1:2] = channel_sums(projected[:, :3200], first_gate, second_gate)
-    sums[2:3], sums[3:4] = channel_sums(projected[:, 3200:], first_up, second_up)
+    squared = projected * projected
+    corrected = (first[...] + projected * ((1.0 - beta_first) / (1.0 - beta_first**STEP))) / (
+        jnp.sqrt(second[...] + squared * ((1.0 - beta_second) / (1.0 - beta_second**STEP))) + adam_epsilon
+    )
+    corrected_sq = jnp.sum(corrected * corrected, 0, keepdims=True)
+    projected_sq = jnp.sum(squared, 0, keepdims=True)
+    sums[0:1], sums[1:2] = corrected_sq[:, :3200], projected_sq[:, :3200]
+    sums[2:3], sums[3:4] = corrected_sq[:, 3200:], projected_sq[:, 3200:]
     sent[...] = sums[...].astype(BF16)
 
 
@@ -367,9 +380,9 @@
     other_down = z_swap(other_down, True)
 
     states = (first_gate, second_gate, first_up, second_up)
-    (own,) = run(add_kernel, (pltpu.VMEM((16, 6400), F32),), own, above)
+    own, old_first, old_second = run(ready_kernel, (pltpu.VMEM((16, 6400), F32),) * 3, own, above, *states)
     sums, sent, total = run(
-        pair_sum_kernel, (pair_row, sent_pair, pltpu.VMEM((16, 6400), F32)), own, below, opposite, *states,
+        pair_sum_kernel, (pair_row, sent_pair, pltpu.VMEM((16, 6400), F32)), own, below, opposite, old_first, old_second,
         cost=8 * 10**9,
     )
     other = ring_swap(sent, False, 1)

time: 54.6 us -> 54.4 us (level)
  transfers between devices with their start and end apart: 18 -> 18, of which waited for: 8 -> 8; matrix products, arithmetic and copies ran while one was open for 0% -> 0% of each run, Pallas kernels for 15% -> 14%
where the time goes in v8:
time: 54.4 us; the launch traced here: 54.1 us
  starting transfers between devices  31.3 us (58%)
  Pallas kernels  13 us (24%)
  waiting for transfers between devices  8.93 us (16%)
  between operations  0.84 us (2%)
    ppermute x9, starting transfers between devices, ring_send(): return lax.ppermute(value, AXES, ring_pairs(shift, stage))  15.4 us
    pallas_call x20, Pallas kernels, __call__(): pl.pallas_call(kernel, name=body.__name__, out_shape=[*outs, *token_out],...  13 us
    ppermute x3, starting transfers between devices, z_swap(): return lax.ppermute(value, 'z', pairs)  8.27 us
    ppermute x4, starting transfers between devices, ring_swap(): return lax.ppermute(value, AXES, pairs)  7.42 us
    ppermute x4, waiting for transfers between devices, ring_swap(): return lax.ppermute(value, AXES, pairs)  4.22 us
    ppermute x9, waiting for transfers between devices, ring_send(): return lax.ppermute(value, AXES, ring_pairs(shift, stage))  4.09 us
  transfers between devices with their start and end apart: 18, of which 8 were waited for; matrix products, arithmetic and copies ran while one was open for 0% of the time, Pallas kernels for 14%

profile of v8, /device:TPU:0, one launch (start us, length us, event | category | flops | bytes accessed | tf_op | source)
XLA Modules:
  0.0 54.1 jit_solution(10909299701638700675)
XLA Ops:
  0.6 2.8 %first_kernel.1 = (bf16[32,6400]{1,0:T(8,128)(2,1)S(1)}, bf16[32,6400]{1,0:T(8,128)(2,1)S(1)}, bf16[192,320]{1,0:T(8,128)(2,1)S(1)}, bf16[192,320]{1,0:T(8,128)(...) custom-call(bf16[320,256]{1,0:T(8,128)(2,1)} %bitcast.12, ...), custom_call_target="tpu_custom_call" | custom-call | tf_op jit(solution)/shard_map/first_kernel/pallas_call | solution.py:99
  3.5 1.6 %collective-permute-start.3 = (bf16[32,6400]{1,0:T(8,128)(2,1)S(1)}, bf16[32,6400]{1,0:T(8,128)(2,1)S(1)}, u32[]{:S(2)}, u32[]{:S(2)}) collective-permute-start(bf16[32,6400]{1,0:T(8,128)(2,1)S(1)} %get-tuple-element.90), channel_id=1, source_target_pairs={{0,8},{1,33},{2,10},{3,35},{4,12},{5,37},{6,14},{7,39},{8,16},{9,4... | collective-permute-start | bytes 1228808 | tf_op jit(solution)/shard_map/ppermute | solution.py:45
  5.1 1.7 %collective-permute-start.2 = (bf16[32,6400]{1,0:T(8,128)(2,1)S(1)}, bf16[32,6400]{1,0:T(8,128)(2,1)S(1)}, u32[]{:S(2)}, u32[]{:S(2)}) collective-permute-start(bf16[32,6400]{1,0:T(8,128)(2,1)S(1)} %get-tuple-element.88), channel_id=1, source_target_pairs={{0,24},{1,97},{2,26},{3,99},{4,28},{5,101},{6,30},{7,103},{8,0},{9... | collective-permute-start | bytes 1228808 | tf_op jit(solution)/shard_map/ppermute | solution.py:45
  6.8 1.6 %rest_kernel.1 = (bf16[32,6400]{1,0:T(8,128)(2,1)S(1)}, bf16[32,6400]{1,0:T(8,128)(2,1)S(1)}, bf16[32,6400]{1,0:T(8,128)(2,1)S(1)}, bf16[32,6400]{1,0:T(8,128)(2...) custom-call(bf16[192,320]{1,0:T(8,128)(2,1)S(1)} %get-tuple-element.81.refs_0_, ...), custom_call_target="tpu_custom_call" | custom-call | tf_op jit(solution)/shard_map/rest_kernel/pallas_call | solution.py:99
  8.4 0.4 collective-permute-start
  8.8 2.9 %collective-permute-start.1 = (bf16[32,6400]{1,0:T(8,128)(2,1)S(1)}, bf16[32,6400]{1,0:T(8,128)(2,1)S(1)}, u32[]{:S(2)}, u32[]{:S(2)}) collective-permute-start(bf16[32,6400]{1,0:T(8,128)(2,1)S(1)} %get-tuple-element.86), channel_id=1, source_target_pairs={{0,24},{1,97},{2,26},{3,99},{4,28},{5,101},{6,30},{7,103},{8,0},{9... | collective-permute-start | bytes 1228808 | tf_op jit(solution)/shard_map/ppermute | solution.py:45
  11.7 1.1 %down_kernel.1 = (bf16[128,1600]{1,0:T(8,128)(2,1)S(1)}, bf16[128,1600]{1,0:T(8,128)(2,1)S(1)}, f32[8,128]{1,0:T(8,128)S(1)}) custom-call(bf16[256,640]{1,0:T(8,128)(2,1)S(1)} %copy-done.7, bf16[1600,640]{1,0:T(8,128)(2,1)S(1)} %bitcast.8, f32[8,128]{1,0:T(8,128)S(1)} %get-tuple-element.91.refs_2_), custom_call_target="tpu_custom_call" | custom-call | tf_op jit(solution)/shard_map/down_kernel/pallas_call | solution.py:99
  12.8 0.1 collective-permute-start.5
  12.9 0.1 pass_kernel.2
  13.0 0.5 collective-permute-start.4
  13.5 0.1 pass_kernel.3
  13.6 2.9 %collective-permute-start.8 = (bf16[32,6400]{1,0:T(8,128)(2,1)S(1)}, bf16[32,6400]{1,0:T(8,128)(2,1)S(1)}, u32[]{:S(2)}, u32[]{:S(2)}) collective-permute-start(bf16[32,6400]{1,0:T(8,128)(2,1)S(1)} %get-tuple-element.106), channel_id=1, source_target_pairs={{0,24},{1,97},{2,26},{3,99},{4,28},{5,101},{6,30},{7,103},{8,0},{9... | collective-permute-start | bytes 1228808 | tf_op jit(solution)/shard_map/ppermute | solution.py:45
  16.5 1.1 %collective-permute-done.refs_1_ = bf16[32,6400]{1,0:T(8,128)(2,1)S(1)} collective-permute-done((bf16[32,6400]{1,0:T(8,128)(2,1)S(1)}, bf16[32,6400]{1,0:T(8,128)(2,1)S(1)}, u32[]{:S(2)}, u32[]{:S(2)}) %collective-permute-start) | collective-permute-done | bytes 409632 | tf_op jit(solution)/shard_map/ppermute | solution.py:45
  17.6 0.2 collect_kernel.1
  17.8 0.0 copy-start.1
  17.8 0.0 copy-start.2
  17.9 0.0 copy-start.3
  17.9 0.0 copy-start.4
  17.9 0.0 copy-start.5
  17.9 0.0 copy-start.6
  17.9 0.1 down_split_kernel.1
  18.0 2.1 %collective-permute-start.7 = (bf16[64,1600]{1,0:T(8,128)(2,1)S(1)}, bf16[64,1600]{1,0:T(8,128)(2,1)S(1)}, u32[]{:S(2)}, u32[]{:S(2)}) collective-permute-start(bf16[64,1600]{1,0:T(8,128)(2,1)S(1)} %get-tuple-element.104), channel_id=1, source_target_pairs={{0,2},{2,0},{4,6},{6,4},{1,3},{3,1},{5,7},{7,5},{8,10},{10,8},{12,... | collective-permute-start | bytes 614408 | tf_op jit(solution)/shard_map/ppermute | solution.py:65
  20.1 2.1 %collective-permute-done.4.refs_1_ = bf16[32,6400]{1,0:T(8,128)(2,1)S(1)} collective-permute-done((bf16[32,6400]{1,0:T(8,128)(2,1)S(1)}, bf16[32,6400]{1,0:T(8,128)(2,1)S(1)}, u32[]{:S(2)}, u32[]{:S(2)}) %collective-permute-start.4) | collective-permute-done | bytes 409632 | tf_op jit(solution)/shard_map/ppermute | solution.py:45
  22.2 0.1 near_kernel.1
  22.3 1.7 %collective-permute-start.6 = (bf16[16,6400]{1,0:T(8,128)(2,1)S(1)}, bf16[16,6400]{1,0:T(8,128)(2,1)S(1)}, u32[]{:S(2)}, u32[]{:S(2)}) collective-permute-start(bf16[16,6400]{1,0:T(8,128)(2,1)S(1)} %get-tuple-element.102), channel_id=1, source_target_pairs={{0,32},{1,9},{2,34},{3,11},{4,36},{5,13},{6,38},{7,15},{8,40},{9,1... | collective-permute-start | bytes 614408 | tf_op jit(solution)/shard_map/ppermute | solution.py:45
  24.1 0.1 far_kernel.1
  24.1 1.6 %collective-permute-start.9 = (bf16[16,6400]{1,0:T(8,128)(2,1)S(1)}, bf16[16,6400]{1,0:T(8,128)(2,1)S(1)}, u32[]{:S(2)}, u32[]{:S(2)}) collective-permute-start(bf16[16,6400]{1,0:T(8,128)(2,1)S(1)} %get-tuple-element.111), channel_id=1, source_target_pairs={{0,96},{1,25},{2,98},{3,27},{4,100},{5,29},{6,102},{7,31},{8,104},... | collective-permute-start | bytes 614408 | tf_op jit(solution)/shard_map/ppermute | solution.py:45
  25.8 2.1 %collective-permute-start.10 = (bf16[16,6400]{1,0:T(8,128)(2,1)S(1)}, bf16[16,6400]{1,0:T(8,128)(2,1)S(1)}, u32[]{:S(2)}, u32[]{:S(2)}) collective-permute-start(bf16[16,6400]{1,0:T(8,128)(2,1)S(1)} %get-tuple-element.112), channel_id=1, source_target_pairs={{0,64},{1,17},{2,66},{3,19},{4,68},{5,21},{6,70},{7,23},{8,72},{9,... | collective-permute-start | bytes 614408 | tf_op jit(solution)/shard_map/ppermute | solution.py:45
  27.9 0.1 down_halve_kernel.1
  28.0 4.1 %collective-permute-start.13 = (bf16[128,1600]{1,0:T(8,128)(2,1)S(1)}, bf16[128,1600]{1,0:T(8,128)(2,1)S(1)}, u32[]{:S(2)}, u32[]{:S(2)}) collective-permute-start(bf16[128,1600]{1,0:T(8,128)(2,1)S(1)} %get-tuple-element.122), channel_id=1, source_target_pairs={{0,6},{6,0},{2,4},{4,2},{1,7},{7,1},{3,5},{5,3},{8,14},{14,8},{10,... | collective-permute-start | bytes 1228808 | tf_op jit(solution)/shard_map/ppermute | solution.py:65
  32.1 0.1 ready_kernel.1
  32.2 0.8 %collective-permute-done.10.refs_2_ = bf16[16,6400]{1,0:T(8,128)(2,1)S(1)} collective-permute-done((bf16[16,6400]{1,0:T(8,128)(2,1)S(1)}, bf16[16,6400]{1,0:T(8,128)(2,1)S(1)}, u32[]{:S(2)}, u32[]{:S(2)}) %collective-permute-start.10) | collective-permute-done | bytes 204832 | tf_op jit(solution)/shard_map/ppermute | solution.py:45
  33.1 0.5 pair_sum_kernel.1
  33.6 1.5 %collective-permute-start.11 = (bf16[4,3200]{1,0:T(4,128)(2,1)S(1)}, bf16[4,3200]{1,0:T(4,128)(2,1)S(1)}, u32[]{:S(2)}, u32[]{:S(2)}) collective-permute-start(bf16[4,3200]{1,0:T(4,128)(2,1)S(1)} %get-tuple-element.117), channel_id=1, source_target_pairs={{0,32},{1,9},{2,34},{3,11},{4,36},{5,13},{6,38},{7,15},{8,40},{9,1... | collective-permute-start | bytes 76808 | tf_op jit(solution)/shard_map/ppermute | solution.py:60
  35.0 2.4 %collective-permute-done.11.refs_1_ = bf16[4,3200]{1,0:T(4,128)(2,1)S(1)} collective-permute-done((bf16[4,3200]{1,0:T(4,128)(2,1)S(1)}, bf16[4,3200]{1,0:T(4,128)(2,1)S(1)}, u32[]{:S(2)}, u32[]{:S(2)}) %collective-permute-start.11) | collective-permute-done | bytes 25632 | tf_op jit(solution)/shard_map/ppermute | solution.py:60
  37.5 2.0 %collective-permute-start.12 = (bf16[4,3200]{1,0:T(4,128)(2,1)S(1)}, bf16[4,3200]{1,0:T(4,128)(2,1)S(1)}, u32[]{:S(2)}, u32[]{:S(2)}) collective-permute-start(bf16[4,3200]{1,0:T(4,128)(2,1)S(1)} %get-tuple-element.120), channel_id=1, source_target_pairs={{0,96},{1,25},{2,98},{3,27},{4,100},{5,29},{6,102},{7,31},{8,104},... | collective-permute-start | bytes 76808 | tf_op jit(solution)/shard_map/ppermute | solution.py:60
  39.5 0.6 %down_sum_kernel.1 = (f32[8,1600]{1,0:T(8,128)S(1)}, bf16[8,1600]{1,0:T(8,128)(2,1)S(1)}, f32[32,1600]{1,0:T(8,128)S(1)}, f32[8,128]{1,0:T(8,128)S(1)}) custom-call(f32[64,1600]{1,0:T(8,128)S(1)} %get-tuple-element.121.refs_0_, bf16[128,1600]{1,0:T(8,128)(2,1)S(1)} %collective-permute-done.13.refs_1_, f32[32,1600]{1,0:T(8,128)S(1)} %copy-done.1, ...), custom_call_target="tpu_custom_call" | custom-call | tf_op jit(solution)/shard_map/down_sum_kernel/pallas_call | solution.py:99
  40.1 2.1 %collective-permute-start.15 = (bf16[8,1600]{1,0:T(8,128)(2,1)S(1)}, bf16[8,1600]{1,0:T(8,128)(2,1)S(1)}, u32[]{:S(2)}, u32[]{:S(2)}) collective-permute-start(bf16[8,1600]{1,0:T(8,128)(2,1)S(1)} %get-tuple-element.130), channel_id=1, source_target_pairs={{0,2},{2,0},{4,6},{6,4},{1,3},{3,1},{5,7},{7,5},{8,10},{10,8},{12,... | collective-permute-start | bytes 76808 | tf_op jit(solution)/shard_map/ppermute | solution.py:65
  42.2 0.5 collective-permute-done.12.refs_1_
  42.6 0.8 %collective-permute-start.14 = (bf16[4,3200]{1,0:T(4,128)(2,1)S(1)}, bf16[4,3200]{1,0:T(4,128)(2,1)S(1)}, u32[]{:S(2)}, u32[]{:S(2)}) collective-permute-start(bf16[4,3200]{1,0:T(4,128)(2,1)S(1)} %get-tuple-element.126), channel_id=1, source_target_pairs={{0,8},{1,33},{2,10},{3,35},{4,12},{5,37},{6,14},{7,39},{8,0},{9,41... | collective-permute-start | bytes 76808 | tf_op jit(solution)/shard_map/ppermute | solution.py:60
  43.4 0.6 %collective-permute-done.15.refs_1_ = bf16[8,1600]{1,0:T(8,128)(2,1)S(1)} collective-permute-done((bf16[8,1600]{1,0:T(8,128)(2,1)S(1)}, bf16[8,1600]{1,0:T(8,128)(2,1)S(1)}, u32[]{:S(2)}, u32[]{:S(2)}) %collective-permute-start.15) | collective-permute-done | bytes 25632 | tf_op jit(solution)/shard_map/ppermute | solution.py:65
  44.0 0.1 collective-permute-start.17
  44.1 1.2 %moment_kernel.1 = (f32[16,3200]{1,0:T(8,128)}, f32[16,3200]{1,0:T(8,128)}, f32[16,3200]{1,0:T(8,128)}, f32[16,3200]{1,0:T(8,128)}, f32[32,1600]{1,0:T(8,128)}, ...) custom-call(f32[16,6400]{1,0:T(8,128)S(1)} %get-tuple-element.127.refs_0_, f32[32,1600]{1,0:T(8,128)S(1)} %get-tuple-element.128.refs_1_, ...), custom_call_target="tpu_custom_call" | custom-call | tf_op jit(solution)/shard_map/moment_kernel/pallas_call | solution.py:99
  45.3 1.2 %collective-permute-done.14.refs_1_ = bf16[4,3200]{1,0:T(4,128)(2,1)S(1)} collective-permute-done((bf16[4,3200]{1,0:T(4,128)(2,1)S(1)}, bf16[4,3200]{1,0:T(4,128)(2,1)S(1)}, u32[]{:S(2)}, u32[]{:S(2)}) %collective-permute-start.14) | collective-permute-done | bytes 25632 | tf_op jit(solution)/shard_map/ppermute | solution.py:60
  46.6 3.2 %collective-permute-start.16 = (bf16[4,3200]{1,0:T(4,128)(2,1)S(1)}, bf16[4,3200]{1,0:T(4,128)(2,1)S(1)}, u32[]{:S(2)}, u32[]{:S(2)}) collective-permute-start(bf16[4,3200]{1,0:T(4,128)(2,1)S(1)} %get-tuple-element.135), channel_id=1, source_target_pairs={{0,24},{1,97},{2,26},{3,99},{4,28},{5,101},{6,30},{7,103},{8,16},{... | collective-permute-start | bytes 76808 | tf_op jit(solution)/shard_map/ppermute | solution.py:60
  49.8 1.8 %down_update_kernel.1 = (bf16[1600,640]{1,0:T(8,128)(2,1)}, f32[8,128]{1,0:T(8,128)S(1)}) custom-call(bf16[1600,640]{1,0:T(8,128)(2,1)S(1)} %bitcast.9, f32[8,1600]{1,0:T(8,128)S(1)} %get-tuple-element.136.refs_1_, bf16[8,1600]{1,0:T(8,128)(2,1)S(1)} %collective-permute-done.17.refs_2_, f32[8,128]{1,0:T(8,128)S(1)} %get-tuple-element.138.refs_3_), custom_call_target="tpu_custom_call" | custom-call | tf_op jit(solution)/shard_map/down_update_kernel/pallas_call | solution.py:99
  51.6 0.1 collective-permute-done.16.refs_3_
  51.7 2.4 %update_kernel.1 = (bf16[320,3200]{1,0:T(8,128)(2,1)}, bf16[320,3200]{1,0:T(8,128)(2,1)}) custom-call(bf16[320,3200]{1,0:T(8,128)(2,1)S(1)} %get-tuple-element.79.refs_1_.refs_0_, bf16[320,3200]{1,0:T(8,128)(2,1)S(1)} %get-tuple-element.80.refs_3_.refs_1_, f32[4,3200]{1,0:T(4,128)S(1)} %get-tuple-element.134.refs_2_, ...), custom_call_target="tpu_custom_call" | custom-call | tf_op jit(solution)/shard_map/update_kernel/pallas_call | solution.py:99
  (24 shorter events, 0.1 us)
Async XLA Ops:
  3.5 9.4 %collective-permute-start.3 = (bf16[32,6400]{1,0:T(8,128)(2,1)S(1)}, bf16[32,6400]{1,0:T(8,128)(2,1)S(1)}, u32[]{:S(2)}, u32[]{:S(2)}) collective-permute-start(bf16[32,6400]{1,0:T(8,128)(2,1)S(1)} %get-tuple-element.90), channel_id=1, source_target_pairs={{0,8},{1,33},{2,10},{3,35},{4,12},{5,37},{6,14},{7,39},{8,16},{9,4... | collective-permute-start | bytes 1228808 | tf_op jit(solution)/shard_map/ppermute | solution.py:45
  5.1 8.4 %collective-permute-start.2 = (bf16[32,6400]{1,0:T(8,128)(2,1)S(1)}, bf16[32,6400]{1,0:T(8,128)(2,1)S(1)}, u32[]{:S(2)}, u32[]{:S(2)}) collective-permute-start(bf16[32,6400]{1,0:T(8,128)(2,1)S(1)} %get-tuple-element.88), channel_id=1, source_target_pairs={{0,24},{1,97},{2,26},{3,99},{4,28},{5,101},{6,30},{7,103},{8,0},{9... | collective-permute-start | bytes 1228808 | tf_op jit(solution)/shard_map/ppermute | solution.py:45
  6.8 4.9 %copy-start = (bf16[640,1600]{0,1:T(8,128)(2,1)S(1)}, bf16[640,1600]{0,1:T(8,128)(2,1)}, u32[]{:S(2)}) copy-start(bf16[640,1600]{0,1:T(8,128)(2,1)} %param.14) | copy-start | bytes 6144004
  6.8 4.9 %copy-start.7 = (bf16[256,640]{1,0:T(8,128)(2,1)S(1)}, bf16[256,640]{1,0:T(8,128)(2,1)}, u32[]{:S(2)}) copy-start(bf16[256,640]{1,0:T(8,128)(2,1)} %refs_0_.1) | copy-start | bytes 983044
  8.4 9.2 %collective-permute-start = (bf16[32,6400]{1,0:T(8,128)(2,1)S(1)}, bf16[32,6400]{1,0:T(8,128)(2,1)S(1)}, u32[]{:S(2)}, u32[]{:S(2)}) collective-permute-start(bf16[32,6400]{1,0:T(8,128)(2,1)S(1)} %get-tuple-element.85), channel_id=1, source_target_pairs={{0,8},{1,33},{2,10},{3,35},{4,12},{5,37},{6,14},{7,39},{8,16},{9,4... | collective-permute-start | bytes 1228808 | tf_op jit(solution)/shard_map/ppermute | solution.py:45
  8.8 8.8 %collective-permute-start.1 = (bf16[32,6400]{1,0:T(8,128)(2,1)S(1)}, bf16[32,6400]{1,0:T(8,128)(2,1)S(1)}, u32[]{:S(2)}, u32[]{:S(2)}) collective-permute-start(bf16[32,6400]{1,0:T(8,128)(2,1)S(1)} %get-tuple-element.86), channel_id=1, source_target_pairs={{0,24},{1,97},{2,26},{3,99},{4,28},{5,101},{6,30},{7,103},{8,0},{9... | collective-permute-start | bytes 1228808 | tf_op jit(solution)/shard_map/ppermute | solution.py:45
  12.8 5.1 %collective-permute-start.5 = (bf16[128,1600]{1,0:T(8,128)(2,1)S(1)}, bf16[128,1600]{1,0:T(8,128)(2,1)S(1)}, u32[]{:S(2)}, u32[]{:S(2)}) collective-permute-start(bf16[128,1600]{1,0:T(8,128)(2,1)S(1)} %get-tuple-element.98), channel_id=1, source_target_pairs={{0,1},{1,0},{2,3},{3,2},{4,5},{5,4},{6,7},{7,6},{8,9},{9,8},{10,11... | collective-permute-start | bytes 1228808 | tf_op jit(solution)/shard_map/ppermute | solution.py:69
  13.0 9.2 %collective-permute-start.4 = (bf16[32,6400]{1,0:T(8,128)(2,1)S(1)}, bf16[32,6400]{1,0:T(8,128)(2,1)S(1)}, u32[]{:S(2)}, u32[]{:S(2)}) collective-permute-start(bf16[32,6400]{1,0:T(8,128)(2,1)S(1)} %get-tuple-element.96), channel_id=1, source_target_pairs={{0,8},{1,33},{2,10},{3,35},{4,12},{5,37},{6,14},{7,39},{8,16},{9,4... | collective-permute-start | bytes 1228808 | tf_op jit(solution)/shard_map/ppermute | solution.py:45
  13.6 10.5 %collective-permute-start.8 = (bf16[32,6400]{1,0:T(8,128)(2,1)S(1)}, bf16[32,6400]{1,0:T(8,128)(2,1)S(1)}, u32[]{:S(2)}, u32[]{:S(2)}) collective-permute-start(bf16[32,6400]{1,0:T(8,128)(2,1)S(1)} %get-tuple-element.106), channel_id=1, source_target_pairs={{0,24},{1,97},{2,26},{3,99},{4,28},{5,101},{6,30},{7,103},{8,0},{9... | collective-permute-start | bytes 1228808 | tf_op jit(solution)/shard_map/ppermute | solution.py:45
  17.8 10.0 %copy-start.1 = (f32[32,1600]{1,0:T(8,128)S(1)}, f32[32,1600]{1,0:T(8,128)}, u32[]{:S(2)}) copy-start(f32[32,1600]{1,0:T(8,128)} %refs_6_.1) | copy-start | bytes 614404
  17.8 10.0 %copy-start.2 = (f32[32,1600]{1,0:T(8,128)S(1)}, f32[32,1600]{1,0:T(8,128)}, u32[]{:S(2)}) copy-start(f32[32,1600]{1,0:T(8,128)} %refs_7_.1) | copy-start | bytes 614404
  17.9 14.2 %copy-start.3 = (f32[16,3200]{1,0:T(8,128)S(1)}, f32[16,3200]{1,0:T(8,128)}, u32[]{:S(2)}) copy-start(f32[16,3200]{1,0:T(8,128)} %refs_2_.7) | copy-start | bytes 614404
  17.9 14.2 %copy-start.4 = (f32[16,3200]{1,0:T(8,128)S(1)}, f32[16,3200]{1,0:T(8,128)}, u32[]{:S(2)}) copy-start(f32[16,3200]{1,0:T(8,128)} %refs_3_.7) | copy-start | bytes 614404
  17.9 14.2 %copy-start.5 = (f32[16,3200]{1,0:T(8,128)S(1)}, f32[16,3200]{1,0:T(8,128)}, u32[]{:S(2)}) copy-start(f32[16,3200]{1,0:T(8,128)} %refs_4_.3) | copy-start | bytes 614404
  17.9 14.2 %copy-start.6 = (f32[16,3200]{1,0:T(8,128)S(1)}, f32[16,3200]{1,0:T(8,128)}, u32[]{:S(2)}) copy-start(f32[16,3200]{1,0:T(8,128)} %refs_5_.3) | copy-start | bytes 614404
  18.0 9.8 %collective-permute-start.7 = (bf16[64,1600]{1,0:T(8,128)(2,1)S(1)}, bf16[64,1600]{1,0:T(8,128)(2,1)S(1)}, u32[]{:S(2)}, u32[]{:S(2)}) collective-permute-start(bf16[64,1600]{1,0:T(8,128)(2,1)S(1)} %get-tuple-element.104), channel_id=1, source_target_pairs={{0,2},{2,0},{4,6},{6,4},{1,3},{3,1},{5,7},{7,5},{8,10},{10,8},{12,... | collective-permute-start | bytes 614408 | tf_op jit(solution)/shard_map/ppermute | solution.py:65
  22.3 9.8 %collective-permute-start.6 = (bf16[16,6400]{1,0:T(8,128)(2,1)S(1)}, bf16[16,6400]{1,0:T(8,128)(2,1)S(1)}, u32[]{:S(2)}, u32[]{:S(2)}) collective-permute-start(bf16[16,6400]{1,0:T(8,128)(2,1)S(1)} %get-tuple-element.102), channel_id=1, source_target_pairs={{0,32},{1,9},{2,34},{3,11},{4,36},{5,13},{6,38},{7,15},{8,40},{9,1... | collective-permute-start | bytes 614408 | tf_op jit(solution)/shard_map/ppermute | solution.py:45
  24.1 8.1 %collective-permute-start.9 = (bf16[16,6400]{1,0:T(8,128)(2,1)S(1)}, bf16[16,6400]{1,0:T(8,128)(2,1)S(1)}, u32[]{:S(2)}, u32[]{:S(2)}) collective-permute-start(bf16[16,6400]{1,0:T(8,128)(2,1)S(1)} %get-tuple-element.111), channel_id=1, source_target_pairs={{0,96},{1,25},{2,98},{3,27},{4,100},{5,29},{6,102},{7,31},{8,104},... | collective-permute-start | bytes 614408 | tf_op jit(solution)/shard_map/ppermute | solution.py:45
  25.8 7.3 %collective-permute-start.10 = (bf16[16,6400]{1,0:T(8,128)(2,1)S(1)}, bf16[16,6400]{1,0:T(8,128)(2,1)S(1)}, u32[]{:S(2)}, u32[]{:S(2)}) collective-permute-start(bf16[16,6400]{1,0:T(8,128)(2,1)S(1)} %get-tuple-element.112), channel_id=1, source_target_pairs={{0,64},{1,17},{2,66},{3,19},{4,68},{5,21},{6,70},{7,23},{8,72},{9,... | collective-permute-start | bytes 614408 | tf_op jit(solution)/shard_map/ppermute | solution.py:45
  28.0 11.5 %collective-permute-start.13 = (bf16[128,1600]{1,0:T(8,128)(2,1)S(1)}, bf16[128,1600]{1,0:T(8,128)(2,1)S(1)}, u32[]{:S(2)}, u32[]{:S(2)}) collective-permute-start(bf16[128,1600]{1,0:T(8,128)(2,1)S(1)} %get-tuple-element.122), channel_id=1, source_target_pairs={{0,6},{6,0},{2,4},{4,2},{1,7},{7,1},{3,5},{5,3},{8,14},{14,8},{10,... | collective-permute-start | bytes 1228808 | tf_op jit(solution)/shard_map/ppermute | solution.py:65
  33.6 3.9 %collective-permute-start.11 = (bf16[4,3200]{1,0:T(4,128)(2,1)S(1)}, bf16[4,3200]{1,0:T(4,128)(2,1)S(1)}, u32[]{:S(2)}, u32[]{:S(2)}) collective-permute-start(bf16[4,3200]{1,0:T(4,128)(2,1)S(1)} %get-tuple-element.117), channel_id=1, source_target_pairs={{0,32},{1,9},{2,34},{3,11},{4,36},{5,13},{6,38},{7,15},{8,40},{9,1... | collective-permute-start | bytes 76808 | tf_op jit(solution)/shard_map/ppermute | solution.py:60
  37.5 5.1 %collective-permute-start.12 = (bf16[4,3200]{1,0:T(4,128)(2,1)S(1)}, bf16[4,3200]{1,0:T(4,128)(2,1)S(1)}, u32[]{:S(2)}, u32[]{:S(2)}) collective-permute-start(bf16[4,3200]{1,0:T(4,128)(2,1)S(1)} %get-tuple-element.120), channel_id=1, source_target_pairs={{0,96},{1,25},{2,98},{3,27},{4,100},{5,29},{6,102},{7,31},{8,104},... | collective-permute-start | bytes 76808 | tf_op jit(solution)/shard_map/ppermute | solution.py:60
  40.1 3.9 %collective-permute-start.15 = (bf16[8,1600]{1,0:T(8,128)(2,1)S(1)}, bf16[8,1600]{1,0:T(8,128)(2,1)S(1)}, u32[]{:S(2)}, u32[]{:S(2)}) collective-permute-start(bf16[8,1600]{1,0:T(8,128)(2,1)S(1)} %get-tuple-element.130), channel_id=1, source_target_pairs={{0,2},{2,0},{4,6},{6,4},{1,3},{3,1},{5,7},{7,5},{8,10},{10,8},{12,... | collective-permute-start | bytes 76808 | tf_op jit(solution)/shard_map/ppermute | solution.py:65
  42.6 3.9 %collective-permute-start.14 = (bf16[4,3200]{1,0:T(4,128)(2,1)S(1)}, bf16[4,3200]{1,0:T(4,128)(2,1)S(1)}, u32[]{:S(2)}, u32[]{:S(2)}) collective-permute-start(bf16[4,3200]{1,0:T(4,128)(2,1)S(1)} %get-tuple-element.126), channel_id=1, source_target_pairs={{0,8},{1,33},{2,10},{3,35},{4,12},{5,37},{6,14},{7,39},{8,0},{9,41... | collective-permute-start | bytes 76808 | tf_op jit(solution)/shard_map/ppermute | solution.py:60
  44.0 5.7 %collective-permute-start.17 = (bf16[8,1600]{1,0:T(8,128)(2,1)S(1)}, bf16[8,1600]{1,0:T(8,128)(2,1)S(1)}, u32[]{:S(2)}, u32[]{:S(2)}) collective-permute-start(bf16[8,1600]{1,0:T(8,128)(2,1)S(1)} %get-tuple-element.137), channel_id=1, source_target_pairs={{0,1},{1,0},{2,3},{3,2},{4,5},{5,4},{6,7},{7,6},{8,9},{9,8},{10,11... | collective-permute-start | bytes 76808 | tf_op jit(solution)/shard_map/ppermute | solution.py:69
  46.6 5.1 %collective-permute-start.16 = (bf16[4,3200]{1,0:T(4,128)(2,1)S(1)}, bf16[4,3200]{1,0:T(4,128)(2,1)S(1)}, u32[]{:S(2)}, u32[]{:S(2)}) collective-permute-start(bf16[4,3200]{1,0:T(4,128)(2,1)S(1)} %get-tuple-element.135), channel_id=1, source_target_pairs={{0,24},{1,97},{2,26},{3,99},{4,28},{5,101},{6,30},{7,103},{8,16},{... | collective-permute-start | bytes 76808 | tf_op jit(solution)/shard_map/ppermute | solution.py:60
